TPU v7x, 32 devices: a whole 2x2x4 slice. The times are simulated.
32 devices in a mesh: dp: 8 (over z, core), seq: 4 (over y, x).
Axes of the slice: x: 2, y: 2, z: 4, core: 2. Of those that a mesh axis runs over, the one named last changes fastest.
Arguments:
- hidden_in: bfloat16 [8, 512, 2048], P('dp', 'seq'), may hold values from -6 to 6
- boundary: int32 [8, 4], P('dp'), may hold values from 1 to 511, as said below
- norm_gain: float32 [2048], replicated, may hold values from 0.5 to 1.5
- proj_weight: bfloat16 [2048, 12288], P(('dp', 'seq')), may hold values from -0.125 to 0.125
- rate_weight: bfloat16 [2048, 32], P(('dp', 'seq')), may hold values from -0.125 to 0.125
- conv_weight: float32 [4, 8192], replicated, may hold values from -3 to 3
- log_rate: float32 [16], replicated, may hold values from -8 to 0
- rate_bias: float32 [16], replicated, may hold values from -4 to 4
- head_gain: float32 [256], replicated, may hold values from 0.5 to 1.5
- out_weight: bfloat16 [2048, 4096], P(('dp', 'seq')), may hold values from -0.09375 to 0.09375
- ffn_norm_gain: float32 [2048], replicated, may hold values from 0.5 to 1.5
- gate_up_weight: bfloat16 [2048, 11008], P(('dp', 'seq')), may hold values from -0.125 to 0.125
- down_weight: bfloat16 [2048, 5504], P(('dp', 'seq')), may hold values from -0.078125 to 0.078125
- grad_out: bfloat16 [8, 512, 2048], P('dp', 'seq'), may hold values from -6 to 6
Outputs:
- result: bfloat16 [8, 512, 2048], P('dp', 'seq')
- grad_in: bfloat16 [8, 512, 2048], P('dp', 'seq')
- final_state: float32 [8, 16, 256, 128], P('dp')
- grad_norm_gain: float32 [2048], replicated
- grad_proj_weight: float32 [2048, 12288], P(('dp', 'seq'))
- grad_rate_weight: float32 [2048, 32], P(('dp', 'seq'))
- grad_conv_weight: float32 [4, 8192], replicated
- grad_log_rate: float32 [16], replicated
- grad_rate_bias: float32 [16], replicated
- grad_head_gain: float32 [256], replicated
- grad_out_weight: float32 [2048, 4096], P(('dp', 'seq'))
- grad_ffn_norm_gain: float32 [2048], replicated
- grad_gate_up_weight: float32 [2048, 11008], P(('dp', 'seq'))
- grad_down_weight: float32 [2048, 5504], P(('dp', 'seq'))
Inputs may be any that keep to these rules, and one draw needn't show every extreme that they name: `boundary`: in each row the first entry lies among the first 128 positions and the others among the last 128 positions.
All inputs are finite; a program needn't handle non-finite values.
Results may differ from a plain program's by a relative error of at most 0.019.
The roundings to bfloat16 on the way count: a program that leaves them out, or rounds other values in their place, can miss the bound.
Values may be sent and summed in bfloat16 or wider, within the bound.
No kernel may reach another device: no remote copies, remote signals or barrier semaphores. Data moves between devices by JAX's collectives and lax.ppermute only.
A program may use at most 608 MiB of HBM per device.

v0:
```python
import jax
import jax.numpy as jnp
from jax import lax
from jax.sharding import PartitionSpec as P

HEADS = 16
KEY = 128
VALUE = 256
FF = 5504
CONV = 4
GROUP = 64
HK = 2048
HV = 4096


EPS = 1e-06
HIGH = lax.Precision.HIGHEST


def passed_along(block, axis, distance):
    devices = range(lax.axis_size(axis))
    route = [(i - distance, i) for i in devices if i - distance in devices]
    return lax.ppermute(block, axis, route)


def prefix(x, axis, combine, identity):
    size, index = (lax.axis_size(axis), lax.axis_index(axis))
    everything = jax.tree.map(
        lambda part, kind: lax.all_gather(part.astype(kind), axis), x, (jnp.bfloat16, jnp.bfloat16)
    )
    start = jax.tree.map(
        lambda part, zero: jnp.broadcast_to(jnp.asarray(zero, part.dtype), part.shape), x, identity
    )

    def prefix_step(k, before):
        reached = k < index
        new = combine(
            before, jax.tree.map(lambda part, own: part[k].astype(own.dtype), everything, x)
        )
        return jax.tree.map(lambda a, b: jnp.where(reached, a, b), new, before)

    return lax.fori_loop(0, size, prefix_step, start)


def entering(x, axis, combine, identity):
    size, index = (lax.axis_size(axis), lax.axis_index(axis))
    everything = jax.tree.map(
        lambda part, kind: lax.all_gather(part.astype(kind), axis),
        x,
        jax.tree.map(lambda a: jnp.bfloat16 if a.dtype == jnp.float32 else a.dtype, x),
    )
    start = jax.tree.map(
        lambda part, zero: jnp.broadcast_to(jnp.asarray(zero, part.dtype), part.shape), x, identity
    )

    def entering_step(k, before):
        at = size - 1 - k
        reached = at > index
        new = combine(
            before, jax.tree.map(lambda part, own: part[at].astype(own.dtype), everything, x)
        )
        return jax.tree.map(lambda a, b: jnp.where(reached, a, b), new, before)

    return lax.fori_loop(0, size, entering_step, start)


def batched(left, right):
    return jnp.einsum("hij,hjk->hik", left, right, precision=HIGH)


def group_pass(state, block):
    query, key_rows, value_rows, decay_log, beta, start = block
    size = query.shape[0]
    cumulative = jnp.cumsum(decay_log, axis=0)
    segment = jnp.cumsum(start)
    alive = (segment == 0.0).astype(jnp.float32)
    index = jnp.arange(size)
    joined = jnp.logical_and(index[:, None] >= index[None, :], segment[:, None] == segment[None, :])
    strict = (index[:, None] > index[None, :]).astype(jnp.float32)
    joined_f = joined.astype(jnp.float32)
    gap = cumulative.T[:, :, None] - cumulative.T[:, None, :]
    pair = jnp.exp(jnp.where(joined[None], gap, 0.0)) * joined_f[None]
    head_decay = jnp.exp(cumulative) * alive[:, None]
    keys_keys = jnp.einsum("ihk,jhk->hij", key_rows, key_rows, precision=HIGH)
    negated = -(beta.T[:, :, None] * pair * keys_keys * strict[None])
    identity = jnp.broadcast_to(jnp.eye(size, dtype=jnp.float32), negated.shape)
    key_state = jnp.einsum("ihk,hvk->hiv", key_rows, state, precision=HIGH)
    targets = beta.T[:, :, None] * (
        jnp.transpose(value_rows, (1, 0, 2)) - head_decay.T[:, :, None] * key_state
    )
    inverse = identity + negated
    power = negated
    for level in range(size.bit_length() - 2):
        power = batched(power, power)
        inverse = batched(inverse, identity + power)
    updates = batched(inverse, targets)
    query_keys = jnp.einsum("ihk,jhk->hij", query, key_rows, precision=HIGH) * pair
    query_state = jnp.einsum("ihk,hvk->hiv", query, state, precision=HIGH)
    output = head_decay.T[:, :, None] * query_state + batched(query_keys, updates)
    last_row = pair[:, size - 1, :]
    carried = jnp.einsum("hj,hjv,jhk->hvk", last_row, updates, key_rows, precision=HIGH)
    new_state = head_decay[size - 1][:, None, None] * state + carried
    return (new_state, jnp.transpose(output, (1, 0, 2)))


def seq_pass(state, query, key_rows, value_rows, decay_log, beta, start, block):
    length = query.shape[0]
    count = length // block
    pieces = tuple(
        (
            arr.reshape((count, block) + arr.shape[1:])
            for arr in (query, key_rows, value_rows, decay_log, beta, start)
        )
    )
    final, outputs = lax.scan(jax.checkpoint(group_pass), state, pieces)
    return (final, outputs.reshape((length,) + outputs.shape[2:]))


def rounded(value):
    return lax.optimization_barrier(value.astype(jnp.bfloat16)).astype(jnp.float32)


def contract_rows(left, right):
    return lax.dot_general(
        left, right, (((1,), (1,)), ((), ())), preferred_element_type=jnp.float32
    )


def contract_tokens(left, right):
    return lax.dot_general(
        left, right, (((0,), (0,)), ((), ())), preferred_element_type=jnp.float32
    )


def silu_slope(value):
    logistic = jax.nn.sigmoid(value)
    return logistic * (1.0 + value * (1.0 - logistic))


def norm_back(normed, factor, grad):
    return factor * (grad - normed * jnp.mean(grad * normed, axis=-1, keepdims=True))


def unit_back(normed, factor, grad):
    return factor * (grad - normed * jnp.sum(grad * normed, axis=-1, keepdims=True))


def combine_maps(earlier, later):
    first = jnp.einsum("hij,hjk->hik", earlier[0], later[0], precision=HIGH)
    second = jnp.einsum("hvj,hjk->hvk", earlier[1], later[0], precision=HIGH) + later[1]
    return (first, second)


def combine_back(earlier, later):
    first = jnp.einsum("hij,hjk->hik", earlier[0], later[0], precision=HIGH)
    second = jnp.einsum("hvj,hjk->hvk", earlier[1], later[0], precision=HIGH) + later[1]
    return (first, second, earlier[2] + later[2])


def on_device(
    hidden_in,
    boundary,
    norm_gain,
    proj_weight,
    rate_weight,
    conv_weight,
    log_rate,
    rate_bias,
    head_gain,
    out_weight,
    ffn_norm_gain,
    gate_up_weight,
    down_weight,
    grad_out,
):
    tokens = hidden_in.shape[1]
    chan = 2 * HK + HV
    row = hidden_in[0].astype(jnp.float32)
    place = lax.axis_index("seq")
    offsets = place * tokens - (CONV - 2) + jnp.arange(tokens + CONV - 2)
    bounds = boundary[0]
    start_ext = jnp.logical_or(
        jnp.any(offsets[:, None] == bounds[None, :], axis=1), offsets == 0
    ).astype(jnp.float32)
    start = start_ext[CONV - 2 :]
    scale = lax.rsqrt(jnp.mean(row * row, axis=1, keepdims=True) + EPS)
    normed = row * scale
    first_in = (normed * norm_gain).astype(jnp.bfloat16)
    mix_whole = (
        lax.all_gather(proj_weight, ("dp", "seq"), axis=0, tiled=True),
        lax.all_gather(rate_weight, ("dp", "seq"), axis=0, tiled=True),
    )
    projected = jnp.dot(first_in, mix_whole[0], preferred_element_type=jnp.float32)
    rates = jnp.dot(first_in, mix_whole[1], preferred_element_type=jnp.float32)
    conv_in = projected[:, :chan].astype(jnp.bfloat16)
    out_gate = projected[:, chan:]
    rim = passed_along(conv_in[tokens - (CONV - 1) :], "seq", 1)
    padded = jnp.concatenate([rim, conv_in], axis=0).astype(jnp.float32)
    conv_out = conv_weight[CONV - 1] * padded[CONV - 1 :]
    keep = jnp.ones((tokens,), jnp.float32)
    keeps = [keep]
    for lag in range(1, CONV):
        keep = keep * (1.0 - start_ext[CONV - 1 - lag : CONV - 1 - lag + tokens])
        keeps.append(keep)
        conv_out = (
            conv_out
            + conv_weight[CONV - 1 - lag]
            * padded[CONV - 1 - lag : CONV - 1 - lag + tokens]
            * keep[:, None]
        )
    act = jax.nn.silu(conv_out)
    query_raw = act[:, :HK].reshape(tokens, HEADS, KEY)
    key_raw = act[:, HK : 2 * HK].reshape(tokens, HEADS, KEY)
    query_factor = lax.rsqrt(jnp.sum(query_raw * query_raw, axis=2, keepdims=True) + EPS)
    key_factor = lax.rsqrt(jnp.sum(key_raw * key_raw, axis=2, keepdims=True) + EPS)
    query_unit = query_raw * query_factor
    key_unit = key_raw * key_factor
    query = rounded(query_unit * KEY ** (-0.5))
    keys = rounded(key_unit)
    values = rounded(act[:, 2 * HK :].reshape(tokens, HEADS, VALUE))
    rate_input = rates[:, :HEADS] + rate_bias
    decay_log = -jnp.exp(log_rate) * jax.nn.softplus(rate_input)
    beta = jax.nn.sigmoid(rates[:, HEADS:])
    state_zero = jnp.zeros((HEADS, VALUE, KEY), jnp.float32)
    ident = jnp.broadcast_to(jnp.eye(KEY, dtype=jnp.float32), (HEADS, KEY, KEY))
    augmented = jnp.concatenate([state_zero, ident], axis=1)
    values_aug = jnp.concatenate([values, jnp.zeros((tokens, HEADS, KEY), jnp.float32)], axis=2)
    final_aug, out_aug = seq_pass(augmented, query, keys, values_aug, decay_log, beta, start, GROUP)
    transfer = final_aug[:, VALUE:, :]
    offset = final_aug[:, :VALUE, :]
    scanned = prefix((transfer, offset), "seq", combine_maps, (ident, state_zero))
    incoming = scanned[1]
    mixed = seq_pass(incoming, query, keys, values, decay_log, beta, start, GROUP)[1]
    own_final = jnp.einsum("hvj,hjk->hvk", incoming, transfer, precision=HIGH) + offset
    head_factor = lax.rsqrt(jnp.mean(mixed * mixed, axis=2, keepdims=True) + EPS)
    head_unit = mixed * head_factor
    gate_view = out_gate.reshape(tokens, HEADS, VALUE)
    gate_act = jax.nn.silu(gate_view)
    branch = (head_unit * head_gain * gate_act).reshape(tokens, HV).astype(jnp.bfloat16)
    hidden = row + contract_rows(
        branch, lax.all_gather(out_weight, ("dp", "seq"), axis=0, tiled=True)
    )
    scale_two = lax.rsqrt(jnp.mean(hidden * hidden, axis=1, keepdims=True) + EPS)
    normed_two = hidden * scale_two
    second_in = (normed_two * ffn_norm_gain).astype(jnp.bfloat16)
    ffn_whole = lax.all_gather(gate_up_weight, ("dp", "seq"), axis=0, tiled=True)
    both = jnp.dot(second_in, ffn_whole, preferred_element_type=jnp.float32)
    gate_part = both[:, :FF]
    up_part = both[:, FF:]
    gate_silu = jax.nn.silu(gate_part)
    inner = (gate_silu * up_part).astype(jnp.bfloat16)
    result = hidden + contract_rows(
        inner, lax.all_gather(down_weight, ("dp", "seq"), axis=0, tiled=True)
    )
    cotangent = grad_out[0].astype(jnp.float32)
    cot_low = grad_out[0]
    down_whole = lax.all_gather(down_weight, ("dp", "seq"), axis=0, tiled=True)
    d_inner = jnp.dot(cot_low, down_whole, preferred_element_type=jnp.float32)
    d_both = jnp.concatenate(
        [d_inner * up_part * silu_slope(gate_part), d_inner * gate_silu], axis=1
    ).astype(jnp.bfloat16)
    d_second = contract_rows(
        d_both, lax.all_gather(gate_up_weight, ("dp", "seq"), axis=0, tiled=True)
    )
    grad_gain_two = jnp.sum(d_second * normed_two, axis=0)
    d_hidden = cotangent + norm_back(normed_two, scale_two, d_second * ffn_norm_gain)
    d_mix = d_hidden.astype(jnp.bfloat16)
    out_whole = lax.all_gather(out_weight, ("dp", "seq"), axis=0, tiled=True)
    d_branch = jnp.dot(d_mix, out_whole, preferred_element_type=jnp.float32).reshape(
        tokens, HEADS, VALUE
    )
    d_scaled = d_branch * gate_act
    grad_head_gain = jnp.sum(d_scaled * head_unit, axis=(0, 1))
    d_gate_view = d_branch * head_unit * head_gain * silu_slope(gate_view)
    d_mixed = norm_back(head_unit, head_factor, d_scaled * head_gain)

    def recur(query_in, keys_in, values_in, decay_in, beta_in, state_in):
        return seq_pass(state_in, query_in, keys_in, values_in, decay_in, beta_in, start, GROUP)

    recomputed, pullback = jax.vjp(recur, query, keys, values, decay_log, beta, incoming)
    local_grads = pullback((state_zero, d_mixed))
    to_last = (place == lax.axis_size("seq") - 1).astype(jnp.float32)
    swapped = jnp.swapaxes(transfer, 1, 2)
    back_scan = entering(
        (swapped, local_grads[5], own_final * to_last),
        "seq",
        combine_back,
        (ident, state_zero, state_zero),
    )
    final_state = back_scan[2] + own_final * to_last
    outer_grads = pullback((back_scan[1], jnp.zeros_like(d_mixed)))
    d_query = rounded(local_grads[0] + outer_grads[0])
    d_keys = rounded(local_grads[1] + outer_grads[1])
    d_values = rounded(local_grads[2] + outer_grads[2])
    d_decay = local_grads[3] + outer_grads[3]
    d_beta = local_grads[4] + outer_grads[4]
    d_query_raw = unit_back(query_unit, query_factor, d_query * KEY ** (-0.5))
    d_key_raw = unit_back(key_unit, key_factor, d_keys)
    d_act = jnp.concatenate(
        [
            d_query_raw.reshape(tokens, HK),
            d_key_raw.reshape(tokens, HK),
            d_values.reshape(tokens, HV),
        ],
        axis=1,
    )
    d_conv = d_act * silu_slope(conv_out)
    d_padded = jnp.pad(conv_weight[CONV - 1] * d_conv, ((CONV - 1, 0), (0, 0)))
    tap_grads = [None] * CONV
    tap_grads[CONV - 1] = jnp.sum(d_conv * padded[CONV - 1 :], axis=0)
    for lag in range(1, CONV):
        masked = d_conv * keeps[lag][:, None]
        tap_grads[CONV - 1 - lag] = jnp.sum(
            masked * padded[CONV - 1 - lag : CONV - 1 - lag + tokens], axis=0
        )
        d_padded = d_padded + jnp.pad(
            conv_weight[CONV - 1 - lag] * masked, ((CONV - 1 - lag, lag), (0, 0))
        )
    grad_conv = jnp.stack(tap_grads, axis=0)
    rim_grad = passed_along(d_padded[: CONV - 1].astype(jnp.bfloat16), "seq", -1).astype(
        jnp.float32
    )
    d_conv_in = d_padded[CONV - 1 :] + jnp.pad(rim_grad, ((tokens - (CONV - 1), 0), (0, 0)))
    d_rate_input = d_decay * -jnp.exp(log_rate) * jax.nn.sigmoid(rate_input)
    grad_log_rate = jnp.sum(d_decay * decay_log, axis=0)
    grad_rate_bias = jnp.sum(d_rate_input, axis=0)
    d_rates = jnp.concatenate([d_rate_input, d_beta * beta * (1.0 - beta)], axis=1).astype(
        jnp.bfloat16
    )
    d_projected = jnp.concatenate([d_conv_in, d_gate_view.reshape(tokens, HV)], axis=1).astype(
        jnp.bfloat16
    )
    pieces = lax.all_gather((proj_weight, rate_weight), ("dp", "seq"), axis=0, tiled=True)
    d_first = contract_rows(d_projected, pieces[0]) + contract_rows(d_rates, pieces[1])
    grad_gain_one = jnp.sum(d_first * normed, axis=0)
    d_row = d_hidden + norm_back(normed, scale, d_first * norm_gain)
    summed = lax.psum_scatter(
        jnp.concatenate(
            [
                contract_tokens(first_in, d_projected),
                contract_tokens(first_in, d_rates),
                contract_tokens(d_mix, branch),
                contract_tokens(second_in, d_both),
                contract_tokens(cot_low, inner),
            ],
            axis=1,
        ),
        ("dp", "seq"),
        scatter_dimension=0,
        tiled=True,
    )
    edge_one = 2 * HK + 2 * HV
    edge_two = edge_one + 2 * HEADS
    edge_three = edge_two + HV
    edge_four = edge_three + 2 * FF
    smalls = lax.psum(
        (grad_gain_one, grad_conv, grad_log_rate, grad_rate_bias, grad_head_gain, grad_gain_two),
        ("dp", "seq"),
    )
    return (
        result.astype(jnp.bfloat16)[None],
        d_row.astype(jnp.bfloat16)[None],
        final_state[None],
        smalls[0],
        summed[:, :edge_one],
        summed[:, edge_one:edge_two],
        smalls[1],
        smalls[2],
        smalls[3],
        smalls[4],
        summed[:, edge_two:edge_three],
        smalls[5],
        summed[:, edge_three:edge_four],
        summed[:, edge_four:],
    )


def solution(mesh):
    in_specs = (
        P("dp", "seq", None),
        P("dp", None),
        P(),
        P(("dp", "seq"), None),
        P(("dp", "seq"), None),
        P(),
        P(),
        P(),
        P(),
        P(("dp", "seq"), None),
        P(),
        P(("dp", "seq"), None),
        P(("dp", "seq"), None),
        P("dp", "seq", None),
    )
    out_specs = (
        P("dp", "seq", None),
        P("dp", "seq", None),
        P("dp", None, None, None),
        P(),
        P(("dp", "seq"), None),
        P(("dp", "seq"), None),
        P(),
        P(),
        P(),
        P(),
        P(("dp", "seq"), None),
        P(),
        P(("dp", "seq"), None),
        P(("dp", "seq"), None),
    )
    return jax.shard_map(
        on_device, mesh=mesh, in_specs=in_specs, out_specs=out_specs, check_vma=False
    )
```

profile of v0, /device:TPU:0, one launch (start us, length us, event | category | flops | bytes accessed | tf_op | source)
XLA Modules:
  0.0 4994.7 jit_solution(8451867688264168210)
XLA Ops:
  8.0 73.6 %all-gather.5 = bf16[32,64,32]{1,2,0:T(8,128)(2,1)S(1)} all-gather(bf16[1,64,32]{1,2,0:T(8,128)(2,1)} %bitcast.1424), channel_id=1, replica_groups=mesh['dp'=8,'seq'=4] {'dp','seq'}, dimensions={0}, use_global_device_ids=true | all-gather | bytes 135168 | tf_op jit(solution)/shard_map/all_gather | solution.py:191
  83.7 206.7 %all-gather.16.cloned.1.call-done = bf16[2048,12288]{1,0:T(8,128)(2,1)} async-done(((bf16[64,12288]{1,0:T(8,128)(2,1)}), bf16[2048,12288]{1,0:T(8,128)(2,1)}) %all-gather.16.cloned.1.call-update) | async-done | bytes 50331664 | tf_op jit(solution)/shard_map/all_gather | solution.py:190
  290.4 20.4 fusion.445
  329.4 50.8 %while.118 = (s32[]{:T(128)}, f32[16,384,128]{2,1,0:T(8,128)}, f32[2,64,16]{2,1,0:T(8,128)S(1)}, f32[2,64]{1,0:T(2,128)S(1)}, f32[2,64,16]{1,2,0:T(8,128)S(1)}, ...) while((s32[]{:T(128)}, f32[16,384,128]{2,1,0:T(8,128)}, ...), condition=%wide.region_6.7_spmd, body=%wide.region_3.6_spmd.sunk | while | flops 2117963904 | bytes 67436408 | solution.py:115
  394.4 21.7 all-gather.24.cloned.1.call-done
  416.1 55.2 %all-gather.26.cloned.1.call-done = bf16[64,256,128]{2,1,0:T(8,128)(2,1)} async-done(((bf16[16,256,128]{2,1,0:T(8,128)(2,1)}), bf16[64,256,128]{2,1,0:T(8,128)(2,1)}) %all-gather.26.cloned.1.call-update) | async-done | bytes 4194320 | tf_op jit(solution)/shard_map/all_gather | solution.py:29
  471.2 42.2 while.122
  516.6 52.7 %while.119 = (s32[]{:T(128)}, f32[16,256,128]{2,1,0:T(8,128)}, f32[2,64,16,256]{3,1,2,0:T(8,128)}, f32[2,64,16]{2,1,0:T(8,128)S(1)}, f32[2,64]{1,0:T(2,128)S(1)}...) while((s32[]{:T(128)}, f32[16,256,128]{2,1,0:T(8,128)}, ...), condition=%wide.region_13.14_spmd, body=%wide.region_10.13_spmd.sunk | while | flops 2319160320 | bytes 79845600 | solution.py:115
  601.7 238.4 %all-gather.20.cloned.1.call-done = bf16[2048,11008]{1,0:T(8,128)(2,1)} async-done(((bf16[64,11008]{1,0:T(8,128)(2,1)}), bf16[2048,11008]{1,0:T(8,128)(2,1)}) %all-gather.20.cloned.1.call-update) | async-done | bytes 45088784 | tf_op jit(solution)/shard_map/all_gather | solution.py:246
  840.1 20.8 fusion.434
  860.9 122.2 %all-gather.22.cloned.1.call-done = bf16[2048,5504]{1,0:T(8,128)(2,1)} async-done(((bf16[64,5504]{1,0:T(8,128)(2,1)}), bf16[2048,5504]{1,0:T(8,128)(2,1)}) %all-gather.22.cloned.1.call-update) | async-done | bytes 22544400 | tf_op jit(solution)/shard_map/all_gather | solution.py:253
  983.1 15.8 multiply_convert_fusion.1
  998.8 22.1 multiply_reduce_fusion.15
  1021.0 38.6 while.121
  1090.5 231.9 %while.123 = (s32[]{:T(128)}, f32[16,256,128]{2,1,0:T(8,128)}, f32[2,64,16,128]{3,2,1,0:T(8,128)}, f32[2,64,16,128]{3,2,1,0:T(8,128)}, f32[2,64,16,256]{3,2,1,0:...) while((s32[]{:T(128)}, f32[16,256,128]{2,1,0:T(8,128)}, ...), condition=%wide.region_33.34_spmd.clone, body=%wide.region_22.33_spmd.clone.sunk | while | flops 6358470656 | bytes 254915984 | solution.py:115
  1332.2 13.2 fusion.415
  1345.5 19.8 convolution_bitcast_fusion.10
  1365.3 33.8 fusion.381
  1399.2 31.6 all-gather.32.cloned.1.call-done
  1430.8 61.9 %while.124 = (s32[]{:T(128)}, f32[16,256,128]{1,2,0:T(8,128)}, f32[16,256,128]{1,2,0:T(8,128)}, s32[]{:T(128)}, bf16[4,16,128,128]{3,2,1,0:T(8,128)(2,1)}, /*ind...) while((s32[]{:T(128)}, f32[16,256,128]{1,2,0:T(8,128)}, ...), condition=%wide.region_35.36_spmd.clone, body=%wide.region_34.35_spmd.clone.sunk | while | flops 810024960 | bytes 25692348 | solution.py:64
  1499.4 228.5 %while.120 = (s32[]{:T(128)}, f32[16,256,128]{2,1,0:T(8,128)}, f32[2,64,16,128]{3,2,1,0:T(8,128)}, f32[2,64,16,128]{3,2,1,0:T(8,128)}, f32[2,64,16,256]{3,2,1,0:...) while((s32[]{:T(128)}, f32[16,256,128]{2,1,0:T(8,128)}, ...), condition=%wide.region_47.48_spmd, body=%wide.region_36.47_spmd.sunk | while | flops 6357946368 | bytes 245480880 | solution.py:115
  1732.6 19.7 fusion.392
  1753.6 19.8 fusion.389
  1797.3 36.5 convolution_dynamic-update-slice_fusion
  1840.2 173.0 %dynamic-update-slice.2 = f32[2048,32928]{1,0:T(8,128)} dynamic-update-slice(f32[2048,32928]{1,0:T(8,128)} %dynamic-update-slice.1, f32[2048,4096]{1,0:T(8,128)} %fusion.415, s32[]{} %constant.349, s32[]{} %constant.351) | dynamic-update-slice | bytes 67108864
  2013.2 352.6 %dynamic-update-slice.3 = f32[2048,32928]{1,0:T(8,128)} dynamic-update-slice(f32[2048,32928]{1,0:T(8,128)} %dynamic-update-slice.2, f32[2048,11008]{1,0:T(8,128)} %fusion.381, s32[]{} %constant.349, s32[]{} %constant.352) | dynamic-update-slice | bytes 180355072
  2365.8 187.5 %dynamic-update-slice.4 = f32[2048,32928]{1,0:T(8,128)} dynamic-update-slice(f32[2048,32928]{1,0:T(8,128)} %dynamic-update-slice.3, f32[2048,5504]{1,0:T(8,128)} %convolution_bitcast_fusion.10, s32[]{} %constant.349, s32[]{} %constant.353) | dynamic-update-slice | bytes 90177536 | tf_op jit(solution)/shard_map/concatenate | solution.py:338
  2554.5 14.1 fusion.371
  2577.3 29.0 fusion.400
  2608.8 40.6 all-reduce.11
  2649.5 2208.5 %reduce-scatter.2.cloned.1.call-done = f32[64,32928]{1,0:T(8,128)} async-done(((f32[2048,32928]{1,0:T(8,128)}), f32[64,32928]{1,0:T(8,128)}) %reduce-scatter.2.cloned.1.call-update) | async-done | bytes 8429584 | tf_op jit(solution)/shard_map/reduce_scatter | solution.py:337
  4872.7 113.5 %all-reduce.14.cloned.1.call-done = f32[4,8192]{1,0:T(4,128)} async-done(((f32[4,8192]{1,0:T(4,128)}), f32[4,8192]{1,0:T(4,128)}) %all-reduce.14.cloned.1.call-update) | async-done | bytes 131088 | tf_op jit(solution)/shard_map/psum | solution.py:356
  (1362 shorter events, 854.1 us)
Async XLA Ops:
  7.2 74.9 %copy-start.97 = (bf16[1,128,2048]{2,1,0:T(8,128)(2,1)S(1)}, bf16[1,128,2048]{2,1,0:T(8,128)(2,1)}, u32[]{:S(2)}) copy-start(bf16[1,128,2048]{2,1,0:T(8,128)(2,1)} %param.28) | copy-start | bytes 1572868
  7.2 75.1 %copy-start.202 = (f32[16]{0:T(128)S(1)}, f32[16]{0:T(128)}, u32[]{:S(2)}) copy-start(f32[16]{0:T(128)} %param.34) | copy-start | bytes 196
  7.2 75.2 %copy-start.142 = (f32[2048]{0:T(1024)S(1)}, f32[2048]{0:T(1024)}, u32[]{:S(2)}) copy-start(f32[2048]{0:T(1024)} %param.30) | copy-start | bytes 24580
  7.2 76.2 %copy-start.195 = (f32[16]{0:T(128)S(1)}, f32[16]{0:T(128)}, u32[]{:S(2)}) copy-start(f32[16]{0:T(128)} %param.35) | copy-start | bytes 196
  7.2 76.3 %copy-start.167 = (f32[4,8192]{1,0:T(4,128)S(1)}, f32[4,8192]{1,0:T(4,128)}, u32[]{:S(2)}) copy-start(f32[4,8192]{1,0:T(4,128)} %param.33) | copy-start | bytes 393220
  7.2 283.2 %all-gather.16.cloned.1.call-start = ((), (), s32[]{:S(2)}) async-start(), calls=%async_computation.1 | async-start | bytes 51904512 | tf_op jit(solution)/shard_map/all_gather | solution.py:190
  8.0 408.1 %all-gather.24.cloned.1.call-start = ((), (), s32[]{:S(2)}) async-start(), calls=%async_computation.7 | async-start | bytes 2621440 | tf_op jit(solution)/shard_map/all_gather | solution.py:29
  82.0 228.9 %copy-start.149 = (bf16[2048,32]{0,1:T(8,128)(2,1)}, bf16[2048,32]{0,1:T(8,128)(2,1)S(1)}, u32[]{:S(2)}) copy-start(bf16[2048,32]{0,1:T(8,128)(2,1)S(1)} %reshape.994) | copy-start | bytes 393220
  82.3 228.6 %copy-start.168 = (f32[128]{0:T(128)}, f32[128]{0:T(128)S(1)}, u32[]{:S(2)}) copy-start(f32[128]{0:T(128)S(1)} %add_rsqrt_fusion.4) | copy-start | bytes 1540
  82.4 237.8 %copy-start.189 = (f32[128]{0:T(128)}, f32[128]{0:T(128)S(1)}, u32[]{:S(2)}) copy-start(f32[128]{0:T(128)S(1)} %get-tuple-element.1884) | copy-start | bytes 1540
  82.4 237.8 %copy-start.191 = (f32[128]{0:T(128)}, f32[128]{0:T(128)S(1)}, u32[]{:S(2)}) copy-start(f32[128]{0:T(128)S(1)} %get-tuple-element.1885) | copy-start | bytes 1540
  82.4 237.8 %copy-start.193 = (f32[128]{0:T(128)}, f32[128]{0:T(128)S(1)}, u32[]{:S(2)}) copy-start(f32[128]{0:T(128)S(1)} %get-tuple-element.1944) | copy-start | bytes 1540
  83.6 232.4 %copy-start.173 = (f32[128,16]{0,1:T(8,128)}, f32[128,16]{0,1:T(8,128)S(1)}, u32[]{:S(2)}) copy-start(f32[128,16]{0,1:T(8,128)S(1)} %get-tuple-element.1942) | copy-start | bytes 24580
  83.7 236.6 %copy-start.151 = (f32[1,8192]{1,0:T(1,128)}, f32[1,8192]{1,0:T(1,128)S(1)}, u32[]{:S(2)}) copy-start(f32[1,8192]{1,0:T(1,128)S(1)} %get-tuple-element.1936) | copy-start | bytes 98308
  83.7 236.6 %copy-start.153 = (f32[1,8192]{1,0:T(1,128)}, f32[1,8192]{1,0:T(1,128)S(1)}, u32[]{:S(2)}) copy-start(f32[1,8192]{1,0:T(1,128)S(1)} %get-tuple-element.1937) | copy-start | bytes 98308
  83.7 236.6 %copy-start.155 = (f32[1,8192]{1,0:T(1,128)}, f32[1,8192]{1,0:T(1,128)S(1)}, u32[]{:S(2)}) copy-start(f32[1,8192]{1,0:T(1,128)S(1)} %get-tuple-element.1938) | copy-start | bytes 98308
  83.7 236.6 %copy-start.157 = (f32[1,8192]{1,0:T(1,128)}, f32[1,8192]{1,0:T(1,128)S(1)}, u32[]{:S(2)}) copy-start(f32[1,8192]{1,0:T(1,128)S(1)} %get-tuple-element.1939) | copy-start | bytes 98308
  312.6 7.0 collective-permute-start
  382.3 88.9 %all-gather.26.cloned.1.call-start = ((), (), s32[]{:S(2)}) async-start(), calls=%async_computation.8 | async-start | bytes 5242880 | tf_op jit(solution)/shard_map/all_gather | solution.py:29
  385.2 203.7 %all-gather.18.cloned.1.call-start = ((), (), s32[]{:S(2)}) async-start(), calls=%async_computation.2 | async-start | bytes 17301504 | tf_op jit(solution)/shard_map/all_gather | solution.py:241
  385.8 454.3 %all-gather.20.cloned.1.call-start = ((), (), s32[]{:S(2)}) async-start(), calls=%async_computation.3 | async-start | bytes 46497792 | tf_op jit(solution)/shard_map/all_gather | solution.py:246
  386.3 596.7 %all-gather.22.cloned.1.call-start = ((), (), s32[]{:S(2)}) async-start(), calls=%async_computation.4 | async-start | bytes 23248896 | tf_op jit(solution)/shard_map/all_gather | solution.py:253
  386.9 1012.2 %all-gather.28.cloned.1.call-start = ((), (), s32[]{:S(2)}) async-start(), calls=%async_computation.9 | async-start | bytes 2621440 | tf_op jit(solution)/shard_map/all_gather | solution.py:48
  394.3 1004.8 %all-gather.30.cloned.1.call-start = ((), (), s32[]{:S(2)}) async-start(), calls=%async_computation.10 | async-start | bytes 5242880 | tf_op jit(solution)/shard_map/all_gather | solution.py:48
  588.9 251.2 %copy-start.145 = (f32[2048]{0:T(1024)S(1)}, f32[2048]{0:T(1024)}, u32[]{:S(2)}) copy-start(f32[2048]{0:T(1024)} %param.38) | copy-start | bytes 24580
  601.7 457.9 %copy-start.171 = (f32[128]{0:T(128)}, f32[128]{0:T(128)S(1)}, u32[]{:S(2)}) copy-start(f32[128]{0:T(128)S(1)} %add_rsqrt_fusion.3) | copy-start | bytes 1540
  1325.4 105.3 %all-gather.32.cloned.1.call-start = ((), (), s32[]{:S(2)}) async-start(), calls=%async_computation.11 | async-start | bytes 5242880 | tf_op jit(solution)/shard_map/all_gather | solution.py:48
  1345.4 3512.5 %reduce-scatter.2.cloned.1.call-start = ((), (), s32[]{:S(2)}) async-start(), calls=%async_computation.5 | async-start | bytes 278986752 | tf_op jit(solution)/shard_map/reduce_scatter | solution.py:337
  1499.4 228.5 %copy-start.162 = (f32[2,64,16]{2,1,0:T(8,128)S(1)}, f32[2,64,16]{2,1,0:T(8,128)}, u32[]{:S(2)}) copy-start(f32[2,64,16]{2,1,0:T(8,128)} %copy-done.161) | copy-start | bytes 24580
  1499.4 228.6 %copy-start.179 = (f32[2,64,16]{1,2,0:T(8,128)S(1)}, f32[2,64,16]{1,2,0:T(8,128)}, u32[]{:S(2)}) copy-start(f32[2,64,16]{1,2,0:T(8,128)} %copy-done.178) | copy-start | bytes 24580
  1790.7 6.2 collective-permute-start.1
  2553.3 2432.9 %all-reduce.14.cloned.1.call-start = ((), (), s32[]{:S(2)}) async-start(), calls=%async_computation.6 | async-start | bytes 262144 | tf_op jit(solution)/shard_map/psum | solution.py:356
  (296 other events, 1195.9 us)
Sparse Core Ops, SparseCore 0:
  11.0 279.4 all-gather.15
  382.5 33.5 all-gather.23
  418.5 52.6 all-gather.25
  474.0 114.8 all-gather.17
  591.6 248.4 all-gather.19
  842.8 140.2 all-gather.21
  985.5 33.4 all-gather.27
  1325.5 50.5 all-gather.29
  1378.0 52.6 all-gather.31
  2553.4 2304.4 reduce-scatter.1
  4864.0 122.0 all-reduce.13
where the time goes:
time: 5020 us; the launch traced here: 4990 us
  waiting for transfers between devices  3010 us (60%)
  local copies, waits for them, and re-layouts  943 us (19%)
  matrix products  743 us (15%)
  other arithmetic  129 us (3%)
  blocking collectives  114 us (2%)
    reduce_scatter x1, waiting for transfers between devices, on_device(): lax.psum_scatter(jnp.concatenate([contract_tokens(first_in, d_projected),...  2210 us
    unnamed x214, local copies, waits for them, and re-layouts  555 us
    dot_general x208, matrix products, batched(): return jnp.einsum('hij,hjk->hik', left, right, precision=HIGH)  249 us
    all_gather x1, waiting for transfers between devices, on_device(): lax.all_gather(gate_up_weight, ('dp', 'seq'), axis=0, tiled=True)  238 us
    all_gather x1, waiting for transfers between devices, on_device(): lax.all_gather(proj_weight, ('dp', 'seq'), axis=0, tiled=True)  207 us
    concatenate x1, local copies, waits for them, and re-layouts, on_device(): jnp.concatenate([contract_tokens(first_in, d_projected), contract_tokens(...  187 us
    all_gather x1, waiting for transfers between devices, on_device(): lax.all_gather(down_weight, ('dp', 'seq'), axis=0, tiled=True)  122 us
    psum x1, waiting for transfers between devices, on_device(): lax.psum((grad_gain_one, grad_conv, grad_log_rate, grad_rate_bias, grad_h...  113 us
  transfers between devices with their start and end apart: 13, of which 10 were waited for; matrix products, arithmetic and copies ran while one was open for 12% of the time, Pallas kernels for 0%

commit v1 on v0

v1 whole, which is shorter than its diff:
```python
import jax
import jax.numpy as jnp
from jax import lax
from jax.sharding import Mesh
from jax.sharding import PartitionSpec as P

HEADS = 16
KEY = 128
VALUE = 256
FF = 5504
CONV = 4
GROUP = 64
HK = 2048
HV = 4096


EPS = 1e-06
HIGH = lax.Precision.HIGHEST
PLANE = ("core", "seq")


def batched(left, right):
    return jnp.einsum("hij,hjk->hik", left, right, precision=HIGH)


def group_pass(state, block):
    query, key_rows, value_rows, decay_log, beta, start = block
    size = query.shape[0]
    cumulative = jnp.cumsum(decay_log, axis=0)
    segment = jnp.cumsum(start)
    alive = (segment == 0.0).astype(jnp.float32)
    index = jnp.arange(size)
    joined = jnp.logical_and(index[:, None] >= index[None, :], segment[:, None] == segment[None, :])
    strict = (index[:, None] > index[None, :]).astype(jnp.float32)
    joined_f = joined.astype(jnp.float32)
    gap = cumulative.T[:, :, None] - cumulative.T[:, None, :]
    pair = jnp.exp(jnp.where(joined[None], gap, 0.0)) * joined_f[None]
    head_decay = jnp.exp(cumulative) * alive[:, None]
    keys_keys = jnp.einsum("ihk,jhk->hij", key_rows, key_rows, precision=HIGH)
    negated = -(beta.T[:, :, None] * pair * keys_keys * strict[None])
    identity = jnp.broadcast_to(jnp.eye(size, dtype=jnp.float32), negated.shape)
    key_state = jnp.einsum("ihk,hvk->hiv", key_rows, state, precision=HIGH)
    targets = beta.T[:, :, None] * (
        jnp.transpose(value_rows, (1, 0, 2)) - head_decay.T[:, :, None] * key_state
    )
    inverse = identity + negated
    power = negated
    for level in range(size.bit_length() - 2):
        power = batched(power, power)
        inverse = batched(inverse, identity + power)
    updates = batched(inverse, targets)
    query_keys = jnp.einsum("ihk,jhk->hij", query, key_rows, precision=HIGH) * pair
    query_state = jnp.einsum("ihk,hvk->hiv", query, state, precision=HIGH)
    output = head_decay.T[:, :, None] * query_state + batched(query_keys, updates)
    last_row = pair[:, size - 1, :]
    carried = jnp.einsum("hj,hjv,jhk->hvk", last_row, updates, key_rows, precision=HIGH)
    new_state = head_decay[size - 1][:, None, None] * state + carried
    return (new_state, jnp.transpose(output, (1, 0, 2)))


def seq_pass(state, query, key_rows, value_rows, decay_log, beta, start, block):
    length = query.shape[0]
    count = length // block
    pieces = tuple(
        (
            arr.reshape((count, block) + arr.shape[1:])
            for arr in (query, key_rows, value_rows, decay_log, beta, start)
        )
    )
    final, outputs = lax.scan(jax.checkpoint(group_pass), state, pieces)
    return (final, outputs.reshape((length,) + outputs.shape[2:]))


def rounded(value):
    return lax.optimization_barrier(value.astype(jnp.bfloat16)).astype(jnp.float32)


def contract_rows(left, right):
    return lax.dot_general(
        left, right, (((1,), (1,)), ((), ())), preferred_element_type=jnp.float32
    )


def contract_tokens(left, right):
    return lax.dot_general(
        left, right, (((0,), (0,)), ((), ())), preferred_element_type=jnp.float32
    )


def silu_slope(value):
    logistic = jax.nn.sigmoid(value)
    return logistic * (1.0 + value * (1.0 - logistic))


def norm_back(normed, factor, grad):
    return factor * (grad - normed * jnp.mean(grad * normed, axis=-1, keepdims=True))


def unit_back(normed, factor, grad):
    return factor * (grad - normed * jnp.sum(grad * normed, axis=-1, keepdims=True))


def swap_core(x):
    return lax.ppermute(x, "core", [(0, 1), (1, 0)])


def from_peer(x, distance):
    size = lax.axis_size("seq")
    return lax.ppermute(x, "seq", [(i, i ^ distance) for i in range(size)])


def plane_gather(x):
    size, me, core = lax.axis_size("seq"), lax.axis_index("seq"), lax.axis_index("core")
    tokens = x.shape[0]
    row = jnp.zeros((size * tokens, x.shape[1]), x.dtype)
    row = lax.dynamic_update_slice(row, x, (me * tokens, 0))
    for k in range(1, size):
        row = lax.dynamic_update_slice(row, from_peer(x, k), ((me ^ k) * tokens, 0))
    other = swap_core(row)
    first = jnp.where(core == 0, row, other)
    second = jnp.where(core == 0, other, row)
    return jnp.concatenate([first, second], axis=0)


def plane_sum(x):
    size, me, core = lax.axis_size("seq"), lax.axis_index("seq"), lax.axis_index("core")
    half = x.shape[0] // 2
    tokens = half // size
    sent = lax.dynamic_slice_in_dim(x, (1 - core) * half, half, 0).astype(jnp.bfloat16)
    mine = lax.dynamic_slice_in_dim(x, core * half, half, 0)
    row = mine + swap_core(sent).astype(jnp.float32)
    total = lax.dynamic_slice_in_dim(row, me * tokens, tokens, 0)
    for k in range(1, size):
        block = lax.dynamic_slice_in_dim(row, (me ^ k) * tokens, tokens, 0)
        total = total + from_peer(block.astype(jnp.bfloat16), k).astype(jnp.float32)
    return total


def weight_columns(parts, split):
    rows = parts[0].shape[0]
    blocks = [jnp.swapaxes(p.reshape(rows, split, -1), 0, 1) for p in parts]
    blocks = jnp.concatenate(blocks, axis=2) if len(blocks) > 1 else blocks[0]
    blocks = lax.all_to_all(blocks, PLANE, 0, 0)
    return lax.all_gather(blocks.reshape(split * rows, -1), "z", axis=0, tiled=True)


def weight_rows(partial, split):
    mine = lax.psum_scatter(
        partial.astype(jnp.bfloat16), "z", scatter_dimension=0, tiled=True
    )
    blocks = lax.all_to_all(mine.reshape(split, -1, mine.shape[1]), PLANE, 0, 0)
    return jnp.swapaxes(blocks, 0, 1).astype(jnp.float32)


def on_device(
    hidden_in,
    boundary,
    norm_gain,
    proj_weight,
    rate_weight,
    conv_weight,
    log_rate,
    rate_bias,
    head_gain,
    out_weight,
    ffn_norm_gain,
    gate_up_weight,
    down_weight,
    grad_out,
):
    own = hidden_in.shape[1]
    seq = lax.axis_size("seq")
    split = 2 * seq
    length = own * seq
    tokens = 2 * length
    heads = HEADS // split
    hk, hv, ff = heads * KEY, heads * VALUE, FF // split
    chan = 2 * hk + hv
    here = lax.axis_index("core") * seq + lax.axis_index("seq")

    mix_in = weight_columns(
        [proj_weight[:, :HK], proj_weight[:, HK : 2 * HK], proj_weight[:, 2 * HK : 2 * HK + HV]],
        split,
    )
    rate_all = lax.all_gather(rate_weight, ("z", "core", "seq"), axis=0, tiled=True)
    gate_out = weight_columns([proj_weight[:, 2 * HK + HV :], out_weight], split)
    gate_in, out_cols = gate_out[:, :hv], gate_out[:, hv:]
    ffn_in = weight_columns([gate_up_weight[:, :FF], gate_up_weight[:, FF:]], split)
    down_cols = weight_columns([down_weight], split)

    x = hidden_in[0].astype(jnp.float32)
    scale = lax.rsqrt(jnp.mean(x * x, axis=1, keepdims=True) + EPS)
    normed = x * scale
    first_in = plane_gather((normed * norm_gain).astype(jnp.bfloat16))
    cot = plane_gather(grad_out[0])

    bounds = boundary
    other = swap_core(bounds)
    core = lax.axis_index("core")
    bounds = jnp.where(
        core == 0, jnp.concatenate([bounds, other], 0), jnp.concatenate([other, bounds], 0)
    )
    positions = jnp.arange(length)
    start = jnp.logical_or(
        jnp.any(positions[None, :, None] == bounds[:, None, :], axis=2), positions == 0
    ).astype(jnp.float32)

    projected = jnp.dot(first_in, mix_in, preferred_element_type=jnp.float32)
    rates = jnp.dot(first_in, rate_all, preferred_element_type=jnp.float32)
    conv_in = projected.astype(jnp.bfloat16).astype(jnp.float32).reshape(2, length, chan)

    def own_columns(whole, width):
        return lax.dynamic_slice_in_dim(whole, here * width, width, whole.ndim - 1)

    taps = jnp.concatenate(
        [
            own_columns(conv_weight[:, :HK], hk),
            own_columns(conv_weight[:, HK : 2 * HK], hk),
            own_columns(conv_weight[:, 2 * HK :], hv),
        ],
        axis=1,
    )
    conv_out = taps[CONV - 1] * conv_in
    keep = jnp.ones((2, length), jnp.float32)
    keeps = [keep]
    for lag in range(1, CONV):
        before = jnp.pad(start, ((0, 0), (lag - 1, 0)))[:, :length]
        keep = keep * (1.0 - before)
        keeps.append(keep)
        moved = jnp.pad(conv_in, ((0, 0), (lag, 0), (0, 0)))[:, :length]
        conv_out = conv_out + taps[CONV - 1 - lag] * moved * keep[:, :, None]
    act = jax.nn.silu(conv_out)
    query_raw = act[:, :, :hk].reshape(2, length, heads, KEY)
    key_raw = act[:, :, hk : 2 * hk].reshape(2, length, heads, KEY)
    query_factor = lax.rsqrt(jnp.sum(query_raw * query_raw, axis=3, keepdims=True) + EPS)
    key_factor = lax.rsqrt(jnp.sum(key_raw * key_raw, axis=3, keepdims=True) + EPS)
    query_unit = query_raw * query_factor
    key_unit = key_raw * key_factor
    query = rounded(query_unit * KEY ** (-0.5))
    keys = rounded(key_unit)
    values = rounded(act[:, :, 2 * hk :].reshape(2, length, heads, VALUE))
    own_rate, own_bias = own_columns(log_rate, heads), own_columns(rate_bias, heads)
    rate_input = own_columns(rates[:, :HEADS], heads).reshape(2, length, heads) + own_bias
    decay_log = -jnp.exp(own_rate) * jax.nn.softplus(rate_input)
    beta = jax.nn.sigmoid(own_columns(rates[:, HEADS:], heads)).reshape(2, length, heads)
    state_zero = jnp.zeros((2, heads, VALUE, KEY), jnp.float32)

    def recur(query_in, keys_in, values_in, decay_in, beta_in):
        def one(state, q, k, v, d, b, s):
            return seq_pass(state, q, k, v, d, b, s, GROUP)

        return jax.vmap(one)(state_zero, query_in, keys_in, values_in, decay_in, beta_in, start)

    (final, mixed), pullback = jax.vjp(recur, query, keys, values, decay_log, beta)

    gate_view = jnp.dot(first_in, gate_in, preferred_element_type=jnp.float32).reshape(
        2, length, heads, VALUE
    )
    head_factor = lax.rsqrt(jnp.mean(mixed * mixed, axis=3, keepdims=True) + EPS)
    head_unit = mixed * head_factor
    gate_act = jax.nn.silu(gate_view)
    branch = (head_unit * head_gain * gate_act).reshape(tokens, hv).astype(jnp.bfloat16)
    hidden = x + plane_sum(contract_rows(branch, out_cols))
    scale_two = lax.rsqrt(jnp.mean(hidden * hidden, axis=1, keepdims=True) + EPS)
    normed_two = hidden * scale_two
    second_in = plane_gather((normed_two * ffn_norm_gain).astype(jnp.bfloat16))
    both = jnp.dot(second_in, ffn_in, preferred_element_type=jnp.float32)
    gate_part = both[:, :ff]
    up_part = both[:, ff:]
    gate_silu = jax.nn.silu(gate_part)
    inner = (gate_silu * up_part).astype(jnp.bfloat16)
    result = hidden + plane_sum(contract_rows(inner, down_cols))

    d_inner = jnp.dot(cot, down_cols, preferred_element_type=jnp.float32)
    d_both = jnp.concatenate(
        [d_inner * up_part * silu_slope(gate_part), d_inner * gate_silu], axis=1
    ).astype(jnp.bfloat16)
    d_second = plane_sum(contract_rows(d_both, ffn_in))
    grad_ffn_in = weight_rows(contract_tokens(second_in, d_both), split)
    grad_down = weight_rows(contract_tokens(cot, inner), split)
    grad_gain_two = jnp.sum(d_second * normed_two, axis=0)
    d_hidden = grad_out[0].astype(jnp.float32) + norm_back(
        normed_two, scale_two, d_second * ffn_norm_gain
    )
    d_mix = plane_gather(d_hidden.astype(jnp.bfloat16))
    d_branch = jnp.dot(d_mix, out_cols, preferred_element_type=jnp.float32).reshape(
        2, length, heads, VALUE
    )
    d_scaled = d_branch * gate_act
    grad_head_gain = jnp.sum(d_scaled * head_unit, axis=(0, 1, 2))
    d_gate = (
        (d_branch * head_unit * head_gain * silu_slope(gate_view))
        .reshape(tokens, hv)
        .astype(jnp.bfloat16)
    )
    d_mixed = norm_back(head_unit, head_factor, d_scaled * head_gain)
    grad_gate_out = weight_rows(
        jnp.concatenate([contract_tokens(first_in, d_gate), contract_tokens(d_mix, branch)], 1),
        split,
    )
    d_query, d_keys, d_values, d_decay, d_beta = pullback((state_zero, d_mixed))
    d_query, d_keys, d_values = rounded(d_query), rounded(d_keys), rounded(d_values)
    d_query_raw = unit_back(query_unit, query_factor, d_query * KEY ** (-0.5))
    d_key_raw = unit_back(key_unit, key_factor, d_keys)
    d_act = jnp.concatenate(
        [
            d_query_raw.reshape(2, length, hk),
            d_key_raw.reshape(2, length, hk),
            d_values.reshape(2, length, hv),
        ],
        axis=2,
    )
    d_conv = d_act * silu_slope(conv_out)
    d_conv_in = taps[CONV - 1] * d_conv
    tap_grads = [None] * CONV
    tap_grads[CONV - 1] = jnp.sum(d_conv * conv_in, axis=(0, 1))
    for lag in range(1, CONV):
        masked = d_conv * keeps[lag][:, :, None]
        moved = jnp.pad(conv_in, ((0, 0), (lag, 0), (0, 0)))[:, :length]
        tap_grads[CONV - 1 - lag] = jnp.sum(masked * moved, axis=(0, 1))
        d_conv_in = d_conv_in + taps[CONV - 1 - lag] * jnp.pad(
            masked, ((0, 0), (0, lag), (0, 0))
        )[:, lag:]
    grad_taps = jnp.stack(tap_grads, axis=0)
    d_rate_input = d_decay * -jnp.exp(own_rate) * jax.nn.sigmoid(rate_input)
    grad_log_rate = jnp.sum(d_decay * decay_log, axis=(0, 1))
    grad_rate_bias = jnp.sum(d_rate_input, axis=(0, 1))
    d_rates = jnp.concatenate(
        [d_rate_input, d_beta * beta * (1.0 - beta)], axis=2
    ).astype(jnp.bfloat16).reshape(tokens, 2 * heads)
    rate_cols = jnp.concatenate(
        [own_columns(rate_all[:, :HEADS], heads), own_columns(rate_all[:, HEADS:], heads)], axis=1
    )
    d_conv_low = d_conv_in.reshape(tokens, chan).astype(jnp.bfloat16)
    d_first = plane_sum(
        contract_rows(d_conv_low, mix_in)
        + contract_rows(d_gate, gate_in)
        + contract_rows(d_rates, rate_cols)
    )
    grad_mix_in = weight_rows(contract_tokens(first_in, d_conv_low), split)
    grad_gain_one = jnp.sum(d_first * normed, axis=0)
    d_row = d_hidden + norm_back(normed, scale, d_first * norm_gain)

    grad_rate = contract_tokens(first_in, d_rates)
    sides = jnp.concatenate(
        [grad_taps.reshape(-1), grad_log_rate, grad_rate_bias, grad_rate.reshape(-1)]
    )
    sums = jnp.concatenate([grad_gain_one, grad_gain_two, grad_head_gain])
    n_sides = sides.shape[0]
    small = lax.psum(jnp.concatenate([sides, sums]), "z")
    small = lax.all_gather(small, PLANE, axis=0)
    sums = jnp.sum(small[:, n_sides:], axis=0)
    width = norm_gain.shape[0]

    def side(at, count):
        return small[:, at : at + count]

    grad_conv = side(0, CONV * chan).reshape(split, CONV, chan)
    grad_conv = jnp.swapaxes(grad_conv, 0, 1)
    grad_conv = jnp.concatenate(
        [
            grad_conv[:, :, :hk].reshape(CONV, HK),
            grad_conv[:, :, hk : 2 * hk].reshape(CONV, HK),
            grad_conv[:, :, 2 * hk :].reshape(CONV, HV),
        ],
        axis=1,
    )
    at = CONV * chan
    grad_log_rate = side(at, heads).reshape(HEADS)
    grad_rate_bias = side(at + heads, heads).reshape(HEADS)
    rows = proj_weight.shape[0]
    first_row = (lax.axis_index("z") * split + here) * rows
    grad_rate = lax.dynamic_slice_in_dim(
        side(at + 2 * heads, width * 2 * heads).reshape(split, width, 2 * heads), first_row, rows, 1
    )
    grad_rate = jnp.concatenate(
        [
            jnp.swapaxes(grad_rate[:, :, :heads], 0, 1).reshape(rows, HEADS),
            jnp.swapaxes(grad_rate[:, :, heads:], 0, 1).reshape(rows, HEADS),
        ],
        axis=1,
    )
    grad_proj = jnp.concatenate(
        [
            grad_mix_in[:, :, :hk].reshape(rows, HK),
            grad_mix_in[:, :, hk : 2 * hk].reshape(rows, HK),
            grad_mix_in[:, :, 2 * hk :].reshape(rows, HV),
            grad_gate_out[:, :, :hv].reshape(rows, HV),
        ],
        axis=1,
    )
    grad_gate_up = jnp.concatenate(
        [grad_ffn_in[:, :, :ff].reshape(rows, FF), grad_ffn_in[:, :, ff:].reshape(rows, FF)], axis=1
    )
    finals = lax.all_gather(final, PLANE, axis=0)
    final_state = lax.dynamic_index_in_dim(finals, core, 1, keepdims=False)
    final_state = final_state.reshape(HEADS, VALUE, KEY)
    return (
        result.astype(jnp.bfloat16)[None],
        d_row.astype(jnp.bfloat16)[None],
        final_state[None],
        sums[:width],
        grad_proj,
        grad_rate,
        grad_conv,
        grad_log_rate,
        grad_rate_bias,
        sums[2 * width :],
        grad_gate_out[:, :, hv:].reshape(rows, HV),
        sums[width : 2 * width],
        grad_gate_up,
        grad_down.reshape(rows, FF),
    )


def solution(mesh):
    dp, seq = mesh.shape["dp"], mesh.shape["seq"]
    planes = Mesh(mesh.devices.reshape(dp // 2, 2, seq), ("z", "core", "seq"))
    row = ("z", "core")
    every = ("z", "core", "seq")
    in_specs = (
        P(row, "seq", None),
        P(row, None),
        P(),
        P(every, None),
        P(every, None),
        P(),
        P(),
        P(),
        P(),
        P(every, None),
        P(),
        P(every, None),
        P(every, None),
        P(row, "seq", None),
    )
    out_specs = (
        P(row, "seq", None),
        P(row, "seq", None),
        P(row, None, None, None),
        P(),
        P(every, None),
        P(every, None),
        P(),
        P(),
        P(),
        P(),
        P(every, None),
        P(),
        P(every, None),
        P(every, None),
    )
    return jax.shard_map(
        on_device, mesh=planes, in_specs=in_specs, out_specs=out_specs, check_vma=False
    )
```

time: 5020 us -> 1370 us (0.27)
  waiting for transfers between devices: 3010 us -> 340 us
  local copies, waits for them, and re-layouts: 943 us -> 249 us
  matrix products: 743 us -> 392 us
  starting transfers between devices: 5.07 us -> 65.6 us
    reduce_scatter x1 -> x4, waiting for transfers between devices: 2210 us -> 141 us  [weight_rows(): lax.psum_scatter(partial.astype(jnp.bfloat16), 'z', scatter_dimension=0,...]
    all_gather x9 -> x5, waiting for transfers between devices: 683 us -> 45.8 us  [the longest x4 45.8 us: weight_columns(): lax.all_gather(blocks.reshape(split * rows, -1), 'z', axis=0, tiled=True)]
    unnamed x214 -> x220, local copies, waits for them, and re-layouts: 555 us -> 38.5 us
    concatenate x3, local copies, waits for them, and re-layouts: 191 us -> 1.25 us  [the longest x2 1.16 us: weight_columns(): blocks = jnp.concatenate(blocks, axis=2) if len(blocks) > 1 else blocks[0]]
    ppermute x2 -> x33, waiting for transfers between devices: 2.71 us -> 125 us  [the longest x24 114 us: from_peer(): return lax.ppermute(x, 'seq', [(i, i ^ distance) for i in range(size)])]
    psum x1, waiting for transfers between devices: 113 us -> 0.01 us  [on_device(): small = lax.psum(jnp.concatenate([sides, sums]), 'z')]
    dot_general x208 -> x376, matrix products: 249 us -> 147 us  [batched(): return jnp.einsum('hij,hjk->hik', left, right, precision=HIGH)]
    dot_general x5 -> x6, matrix products: 105 us -> 32.7 us  [contract_tokens(): lax.dot_general(left, right, (((0,), (0,)), ((), ())), preferred_element_...]
  transfers between devices with their start and end apart: 13 -> 49, of which waited for: 10 -> 22; matrix products, arithmetic and copies ran while one was open for 12% -> 54% of each run, Pallas kernels for 0% -> 0%
where the time goes in v1:
time: 1370 us; the launch traced here: 1360 us
  matrix products  392 us (29%)
  waiting for transfers between devices  340 us (25%)
  local copies, waits for them, and re-layouts  249 us (18%)
  blocking collectives  152 us (11%)
  other arithmetic  137 us (10%)
  starting transfers between devices  65.6 us (5%)
  between operations  16.1 us (1%)
    dot_general x376, matrix products, batched(): return jnp.einsum('hij,hjk->hik', left, right, precision=HIGH)  147 us
    reduce_scatter x4, waiting for transfers between devices, weight_rows(): lax.psum_scatter(partial.astype(jnp.bfloat16), 'z', scatter_dimension=0,...  141 us
    ppermute x24, waiting for transfers between devices, from_peer(): return lax.ppermute(x, 'seq', [(i, i ^ distance) for i in range(size)])  114 us
    all_gather x1, blocking collectives, on_device(): lax.all_gather(rate_weight, ('z', 'core', 'seq'), axis=0, tiled=True)  89.4 us
    squeeze x72, local copies, waits for them, and re-layouts, seq_pass(): final, outputs = lax.scan(jax.checkpoint(group_pass), state, pieces)  67.9 us
    all_gather x4, waiting for transfers between devices, weight_columns(): lax.all_gather(blocks.reshape(split * rows, -1), 'z', axis=0, tiled=True)  45.8 us
    ppermute x24, starting transfers between devices, from_peer(): return lax.ppermute(x, 'seq', [(i, i ^ distance) for i in range(size)])  39.2 us
    unnamed x220, local copies, waits for them, and re-layouts  38.5 us
  transfers between devices with their start and end apart: 49, of which 22 were waited for; matrix products, arithmetic and copies ran while one was open for 54% of the time, Pallas kernels for 0%

profile of v1, /device:TPU:0, one launch (start us, length us, event | category | flops | bytes accessed | tf_op | source)
XLA Modules:
  0.0 1359.2 jit_solution(6899522690276182190)
XLA Ops:
  10.6 20.1 %all_to_all.40 = bf16[8,64,1024]{2,1,0:T(8,128)(2,1)} all-to-all(bf16[8,64,1024]{2,1,0:T(8,128)(2,1)S(1)} %copy.760), channel_id=1, replica_groups=mesh['z'=4,'core'=2,'seq'=4] {'core','seq'}, dimensions={0} | all-to-all | bytes 2097152 | tf_op jit(solution)/shard_map/all_to_all | solution.py:143
  31.9 18.1 %all_to_all.41 = bf16[8,64,1024]{2,1,0:T(8,128)(2,1)} all-to-all(bf16[8,64,1024]{2,1,0:T(8,128)(2,1)S(1)} %copy.776), channel_id=1, replica_groups=mesh['z'=4,'core'=2,'seq'=4] {'core','seq'}, dimensions={0} | all-to-all | bytes 2097152 | tf_op jit(solution)/shard_map/all_to_all | solution.py:143
  66.9 89.4 %all-gather.1 = bf16[32,64,32]{1,2,0:T(8,128)(2,1)S(1)} all-gather(bf16[1,64,32]{1,2,0:T(8,128)(2,1)S(1)} %bitcast.888), channel_id=1, replica_groups=mesh['z'=4,'core'=2,'seq'=4] {'z','core','seq'}, dimensions={0}, use_global_device_ids=true | all-gather | bytes 135168 | tf_op jit(solution)/shard_map/all_gather | solution.py:185
  173.1 9.3 convolution_convert_fusion.5
  187.0 9.8 fusion.176
  213.6 117.4 %while.43 = (s32[]{:T(128)}, f32[2,2,256,128]{3,2,1,0:T(8,128)S(1)}, f32[8,2,64,2,256]{4,2,3,1,0:T(8,128)S(1)}, f32[8,2,2,256,128]{4,3,2,1,0:T(8,128)}, f32[8,2,...) while((s32[]{:T(128)}, ...), condition=%wide.region_7.8_spmd.clone.clone, body=%wide.region_4.7_spmd.clone.clone.sunk | while | flops 580358528 | bytes 8765138 | solution.py:70
  337.8 8.8 multiply_convert_fusion.4
  383.4 8.2 collective-permute-done.7
  406.5 14.0 %collective-permute-start.11 = (bf16[128,2048]{1,0:T(8,128)(2,1)S(1)}, bf16[128,2048]{1,0:T(8,128)(2,1)S(1)}, u32[]{:S(2)}, u32[]{:S(2)}) collective-permute-start(bf16[128,2048]{1,0:T(8,128)(2,1)S(1)} %get-tuple-element.852), channel_id=1, source_target_pairs={{0,3},{1,2},{2,1},{3,0},{4,7},{5,6},{6,5},{7,4},{8,11},{9,10},{10,... | collective-permute-start | bytes 1572872 | tf_op jit(solution)/shard_map/ppermute | solution.py:109
  421.4 12.2 collective-permute-done.9
  434.4 9.5 collective-permute-done.10
  455.0 12.9 fusion.180
  467.9 45.8 %all-gather.15.cloned.1.call-done = bf16[2048,688]{1,0:T(8,128)(2,1)} async-done(((bf16[512,688]{1,0:T(8,128)(2,1)}), bf16[2048,688]{1,0:T(8,128)(2,1)}) %all-gather.15.cloned.1.call-update) | async-done | bytes 2818064 | tf_op jit(solution)/shard_map/all_gather | solution.py:144
  513.7 9.2 multiply_convert_fusion.1
  547.8 11.3 collective-permute-done.22
  559.1 11.2 collective-permute-done.23
  578.9 11.4 collective-permute-done.25
  591.1 9.3 collective-permute-done.26
  642.5 305.7 %while.42 = (s32[]{:T(128)}, f32[2,2,256,128]{3,2,1,0:T(8,128)S(1)}, bf16[8,2,64,2,128]{4,2,0,3,1:T(8,128)(2,1)}, bf16[8,2,64,2,128]{4,2,0,3,1:T(8,128)(2,1)}, b...) while((s32[]{:T(128)}, ...), condition=%wide.region_23.24_spmd.clone, body=%wide.region_12.23_spmd.clone.sunk | while | flops 1589153920 | bytes 29800552 | solution.py:70
  959.5 10.1 multiply_reduce_fusion.7
  969.7 8.9 fusion.173
  1008.2 9.1 collective-permute-done.30
  1017.3 10.8 collective-permute-done.31
  1032.1 10.3 convolution_convert_fusion
  1042.5 9.4 convolution_convert_fusion.1
  1105.4 10.8 collective-permute-done.16
  1120.1 24.5 %all-gather.2 = f32[8,1,16644]{2,1,0:T(1,128)S(1)} all-gather(f32[1,1,16644]{2,1,0:T(1,128)} %bitcast.869), channel_id=1, replica_groups=mesh['z'=4,'core'=2,'seq'=4] {'core','seq'}, dimensions={0}, use_global_device_ids=true | all-gather | bytes 599184 | tf_op jit(solution)/shard_map/all_gather | solution.py:351
  1150.7 16.0 %reduce-scatter.9.cloned.1.call-done = bf16[512,1376]{0,1:T(8,128)(2,1)} async-done(((bf16[2048,1376]{0,1:T(8,128)(2,1)}), bf16[512,1376]{0,1:T(8,128)(2,1)}) %reduce-scatter.9.cloned.1.call-update) | async-done | bytes 1409040 | tf_op jit(solution)/shard_map/reduce_scatter | solution.py:148
  1174.8 17.2 %all-to-all-done.6 = bf16[8,64,1376]{2,1,0:T(8,128)(2,1)S(1)} async-done(((bf16[8,64,1376]{2,1,0:T(8,128)(2,1)}), bf16[8,64,1376]{2,1,0:T(8,128)(2,1)S(1)}, u32[]{:S(2)}, u32[]{:S(2)}) %all-to-all-start.6) | async-done | bytes 1409056 | tf_op jit(solution)/shard_map/all_to_all | solution.py:151
  1192.0 54.4 %reduce-scatter.5.cloned.1.call-done = bf16[512,1024]{1,0:T(8,128)(2,1)} async-done(((bf16[2048,1024]{1,0:T(8,128)(2,1)}), bf16[512,1024]{1,0:T(8,128)(2,1)}) %reduce-scatter.5.cloned.1.call-update) | async-done | bytes 1048592 | tf_op jit(solution)/shard_map/reduce_scatter | solution.py:148
  1255.5 70.3 %reduce-scatter.7.cloned.1.call-done = bf16[512,1024]{0,1:T(8,128)(2,1)} async-done(((bf16[2048,1024]{0,1:T(8,128)(2,1)}), bf16[512,1024]{0,1:T(8,128)(2,1)}) %reduce-scatter.7.cloned.1.call-update) | async-done | bytes 1048592 | tf_op jit(solution)/shard_map/reduce_scatter | solution.py:148
  1335.8 11.4 all-to-all-done.5
  (1576 shorter events, 762.9 us)
Async XLA Ops:
  7.2 165.9 %all-gather.9.cloned.1.call-start = ((), (), s32[]{:S(2)}) async-start(), calls=%async_computation.12 | async-start | bytes 5242880 | tf_op jit(solution)/shard_map/all_gather | solution.py:144
  30.7 307.1 %all-gather.11.cloned.1.call-start = ((), (), s32[]{:S(2)}) async-start(), calls=%async_computation.13 | async-start | bytes 5242880 | tf_op jit(solution)/shard_map/all_gather | solution.py:144
  52.8 105.1 %collective-permute-start = (bf16[128,2048]{1,0:T(8,128)(2,1)}, bf16[128,2048]{1,0:T(8,128)(2,1)}, u32[]{:S(2)}, u32[]{:S(2)}) collective-permute-start(bf16[128,2048]{1,0:T(8,128)(2,1)} %get-tuple-element.862), channel_id=1, source_target_pairs={{0,1},{1,0},{2,3},{3,2},{4,5},{5,4},{6,7},{7,6},{8,9},{9,8},{10,11... | collective-permute-start | bytes 1572872 | tf_op jit(solution)/shard_map/ppermute | solution.py:109
  53.7 106.2 %collective-permute-start.1 = (bf16[128,2048]{1,0:T(8,128)(2,1)}, bf16[128,2048]{1,0:T(8,128)(2,1)}, u32[]{:S(2)}, u32[]{:S(2)}) collective-permute-start(bf16[128,2048]{1,0:T(8,128)(2,1)} %get-tuple-element.862), channel_id=1, source_target_pairs={{0,2},{1,3},{2,0},{3,1},{4,6},{5,7},{6,4},{7,5},{8,10},{9,11},{10,... | collective-permute-start | bytes 1572872 | tf_op jit(solution)/shard_map/ppermute | solution.py:109
  54.3 107.4 %collective-permute-start.2 = (bf16[128,2048]{1,0:T(8,128)(2,1)}, bf16[128,2048]{1,0:T(8,128)(2,1)S(1)}, u32[]{:S(2)}, u32[]{:S(2)}) collective-permute-start(bf16[128,2048]{1,0:T(8,128)(2,1)} %get-tuple-element.862), channel_id=1, source_target_pairs={{0,3},{1,2},{2,1},{3,0},{4,7},{5,6},{6,5},{7,4},{8,11},{9,10},{10,... | collective-permute-start | bytes 1572872 | tf_op jit(solution)/shard_map/ppermute | solution.py:109
  56.3 107.2 %collective-permute-start.4 = (s32[1,4]{1,0:T(1,128)S(1)}, s32[1,4]{1,0:T(1,128)S(1)}, u32[]{:S(2)}, u32[]{:S(2)}) collective-permute-start(s32[1,4]{1,0:T(1,128)S(1)} %copy-done.93), channel_id=1, source_target_pairs={{0,4},{4,0},{1,5},{5,1},{2,6},{6,2},{3,7},{7,3},{8,12},{12,8},{9,1... | collective-permute-start | bytes 56 | tf_op jit(solution)/shard_map/ppermute | solution.py:104
  62.4 101.9 %all-to-all-start.2 = ((bf16[8,64,1376]{2,1,0:T(8,128)(2,1)}), bf16[8,64,1376]{2,1,0:T(8,128)(2,1)}, u32[]{:S(2)}, u32[]{:S(2)}) async-start(bf16[8,64,1376]{2,1,0:T(8,128)(2,1)} %pad_maximum_fusion.16), calls=%async_computation.2 | async-start | bytes 2883584 | tf_op jit(solution)/shard_map/all_to_all | solution.py:143
  66.7 388.2 %all-gather.13.cloned.1.call-start = ((), (), s32[]{:S(2)}) async-start(), calls=%async_computation.14 | async-start | bytes 7208960 | tf_op jit(solution)/shard_map/all_gather | solution.py:144
  365.3 26.3 %collective-permute-start.7 = (bf16[128,2048]{1,0:T(8,128)(2,1)}, bf16[128,2048]{1,0:T(8,128)(2,1)}, u32[]{:S(2)}, u32[]{:S(2)}) collective-permute-start(bf16[128,2048]{1,0:T(8,128)(2,1)} %get-tuple-element.906), channel_id=1, source_target_pairs={{0,2},{1,3},{2,0},{3,1},{4,6},{5,7},{6,4},{7,5},{8,10},{9,11},{10,... | collective-permute-start | bytes 1572872 | tf_op jit(solution)/shard_map/ppermute | solution.py:109
  365.3 26.3 %collective-permute-start.8 = (bf16[128,2048]{1,0:T(8,128)(2,1)}, bf16[128,2048]{1,0:T(8,128)(2,1)}, u32[]{:S(2)}, u32[]{:S(2)}) collective-permute-start(bf16[128,2048]{1,0:T(8,128)(2,1)} %get-tuple-element.905), channel_id=1, source_target_pairs={{0,3},{1,2},{2,1},{3,0},{4,7},{5,6},{6,5},{7,4},{8,11},{9,10},{10,... | collective-permute-start | bytes 1572872 | tf_op jit(solution)/shard_map/ppermute | solution.py:109
  368.6 34.1 %collective-permute-start.17 = (bf16[128,2048]{1,0:T(8,128)(2,1)}, bf16[128,2048]{1,0:T(8,128)(2,1)}, u32[]{:S(2)}, u32[]{:S(2)}) collective-permute-start(bf16[128,2048]{1,0:T(8,128)(2,1)} %bitcast.38), channel_id=1, source_target_pairs={{0,1},{1,0},{2,3},{3,2},{4,5},{5,4},{6,7},{7,6},{8,9},{9,8},{10,11... | collective-permute-start | bytes 1572872 | tf_op jit(solution)/shard_map/ppermute | solution.py:109
  368.8 35.9 %collective-permute-start.18 = (bf16[128,2048]{1,0:T(8,128)(2,1)}, bf16[128,2048]{1,0:T(8,128)(2,1)}, u32[]{:S(2)}, u32[]{:S(2)}) collective-permute-start(bf16[128,2048]{1,0:T(8,128)(2,1)} %bitcast.38), channel_id=1, source_target_pairs={{0,2},{1,3},{2,0},{3,1},{4,6},{5,7},{6,4},{7,5},{8,10},{9,11},{10,... | collective-permute-start | bytes 1572872 | tf_op jit(solution)/shard_map/ppermute | solution.py:109
  372.7 72.9 %all-to-all-start.3 = ((bf16[8,64,688]{2,1,0:T(8,128)(2,1)}), bf16[8,64,688]{2,1,0:T(8,128)(2,1)}, u32[]{:S(2)}, u32[]{:S(2)}) async-start(bf16[8,64,688]{2,1,0:T(8,128)(2,1)} %bitcast.489), calls=%async_computation.3 | async-start | bytes 1572864 | tf_op jit(solution)/shard_map/all_to_all | solution.py:143
  376.9 136.8 %all-gather.15.cloned.1.call-start = ((), (), s32[]{:S(2)}) async-start(), calls=%async_computation.15 | async-start | bytes 3932160 | tf_op jit(solution)/shard_map/all_gather | solution.py:144
  380.4 40.1 %collective-permute-start.19 = (bf16[128,2048]{1,0:T(8,128)(2,1)}, bf16[128,2048]{1,0:T(8,128)(2,1)S(1)}, u32[]{:S(2)}, u32[]{:S(2)}) collective-permute-start(bf16[128,2048]{1,0:T(8,128)(2,1)} %bitcast.38), channel_id=1, source_target_pairs={{0,3},{1,2},{2,1},{3,0},{4,7},{5,6},{6,5},{7,4},{8,11},{9,10},{10,... | collective-permute-start | bytes 1572872 | tf_op jit(solution)/shard_map/ppermute | solution.py:109
  396.6 37.0 %collective-permute-start.9 = (bf16[128,2048]{1,0:T(8,128)(2,1)S(1)}, bf16[128,2048]{1,0:T(8,128)(2,1)S(1)}, u32[]{:S(2)}, u32[]{:S(2)}) collective-permute-start(bf16[128,2048]{1,0:T(8,128)(2,1)S(1)} %get-tuple-element.852), channel_id=1, source_target_pairs={{0,1},{1,0},{2,3},{3,2},{4,5},{5,4},{6,7},{7,6},{8,9},{9,8},{10,11... | collective-permute-start | bytes 1572872 | tf_op jit(solution)/shard_map/ppermute | solution.py:109
  404.6 39.3 %collective-permute-start.10 = (bf16[128,2048]{1,0:T(8,128)(2,1)S(1)}, bf16[128,2048]{1,0:T(8,128)(2,1)S(1)}, u32[]{:S(2)}, u32[]{:S(2)}) collective-permute-start(bf16[128,2048]{1,0:T(8,128)(2,1)S(1)} %get-tuple-element.852), channel_id=1, source_target_pairs={{0,2},{1,3},{2,0},{3,1},{4,6},{5,7},{6,4},{7,5},{8,10},{9,11},{10,... | collective-permute-start | bytes 1572872 | tf_op jit(solution)/shard_map/ppermute | solution.py:109
  406.5 38.2 %collective-permute-start.11 = (bf16[128,2048]{1,0:T(8,128)(2,1)S(1)}, bf16[128,2048]{1,0:T(8,128)(2,1)S(1)}, u32[]{:S(2)}, u32[]{:S(2)}) collective-permute-start(bf16[128,2048]{1,0:T(8,128)(2,1)S(1)} %get-tuple-element.852), channel_id=1, source_target_pairs={{0,3},{1,2},{2,1},{3,0},{4,7},{5,6},{6,5},{7,4},{8,11},{9,10},{10,... | collective-permute-start | bytes 1572872 | tf_op jit(solution)/shard_map/ppermute | solution.py:109
  421.4 24.7 %collective-permute-start.20 = (bf16[512,2048]{1,0:T(8,128)(2,1)}, bf16[512,2048]{1,0:T(8,128)(2,1)}, u32[]{:S(2)}, u32[]{:S(2)}) collective-permute-start(bf16[512,2048]{1,0:T(8,128)(2,1)} %constant_dynamic-update-slice_fusion.5), channel_id=1, source_target_pairs={{0,4},{4,0},{1,5},{5,1},{2,6},{6,2},{3,7},{7,3},{8,12},{12,8},{9,1... | collective-permute-start | bytes 6291464 | tf_op jit(solution)/shard_map/ppermute | solution.py:104
  445.6 629.5 %reduce-scatter.11.cloned.1.call-start = ((), (), s32[]{:S(2)}) async-start(), calls=%async_computation.20 | async-start | bytes 3522560 | tf_op jit(solution)/shard_map/reduce_scatter | solution.py:148
  540.5 550.7 %all-gather.17.cloned.1.call-start = ((), (), s32[]{:S(2)}) async-start(), calls=%async_computation.21 | async-start | bytes 4718592 | tf_op jit(solution)/shard_map/all_gather | solution.py:395
  545.8 24.6 %collective-permute-start.23 = (bf16[128,2048]{1,0:T(8,128)(2,1)S(1)}, bf16[128,2048]{1,0:T(8,128)(2,1)S(1)}, u32[]{:S(2)}, u32[]{:S(2)}) collective-permute-start(bf16[128,2048]{1,0:T(8,128)(2,1)S(1)} %get-tuple-element.896), channel_id=1, source_target_pairs={{0,2},{1,3},{2,0},{3,1},{4,6},{5,7},{6,4},{7,5},{8,10},{9,11},{10,... | collective-permute-start | bytes 1572872 | tf_op jit(solution)/shard_map/ppermute | solution.py:109
  576.6 23.8 %collective-permute-start.26 = (bf16[128,2048]{1,0:T(8,128)(2,1)S(1)}, bf16[128,2048]{1,0:T(8,128)(2,1)S(1)}, u32[]{:S(2)}, u32[]{:S(2)}) collective-permute-start(bf16[128,2048]{1,0:T(8,128)(2,1)S(1)} %get-tuple-element.849), channel_id=1, source_target_pairs={{0,2},{1,3},{2,0},{3,1},{4,6},{5,7},{6,4},{7,5},{8,10},{9,11},{10,... | collective-permute-start | bytes 1572872 | tf_op jit(solution)/shard_map/ppermute | solution.py:109
  577.4 23.8 %collective-permute-start.27 = (bf16[128,2048]{1,0:T(8,128)(2,1)S(1)}, bf16[128,2048]{1,0:T(8,128)(2,1)S(1)}, u32[]{:S(2)}, u32[]{:S(2)}) collective-permute-start(bf16[128,2048]{1,0:T(8,128)(2,1)S(1)} %get-tuple-element.849), channel_id=1, source_target_pairs={{0,3},{1,2},{2,1},{3,0},{4,7},{5,6},{6,5},{7,4},{8,11},{9,10},{10,... | collective-permute-start | bytes 1572872 | tf_op jit(solution)/shard_map/ppermute | solution.py:109
  611.3 508.8 %all-reduce.12.cloned.1.call-start = ((), (), s32[]{:S(2)}) async-start(), calls=%async_computation.16 | async-start | bytes 134144 | tf_op jit(solution)/shard_map/psum | solution.py:350
  1002.4 25.8 %collective-permute-start.31 = (bf16[128,2048]{1,0:T(8,128)(2,1)}, bf16[128,2048]{1,0:T(8,128)(2,1)}, u32[]{:S(2)}, u32[]{:S(2)}) collective-permute-start(bf16[128,2048]{1,0:T(8,128)(2,1)} %get-tuple-element.889), channel_id=1, source_target_pairs={{0,2},{1,3},{2,0},{3,1},{4,6},{5,7},{6,4},{7,5},{8,10},{9,11},{10,... | collective-permute-start | bytes 1572872 | tf_op jit(solution)/shard_map/ppermute | solution.py:109
  1003.8 24.3 %collective-permute-start.32 = (bf16[128,2048]{1,0:T(8,128)(2,1)}, bf16[128,2048]{1,0:T(8,128)(2,1)}, u32[]{:S(2)}, u32[]{:S(2)}) collective-permute-start(bf16[128,2048]{1,0:T(8,128)(2,1)} %get-tuple-element.888), channel_id=1, source_target_pairs={{0,3},{1,2},{2,1},{3,0},{4,7},{5,6},{6,5},{7,4},{8,11},{9,10},{10,... | collective-permute-start | bytes 1572872 | tf_op jit(solution)/shard_map/ppermute | solution.py:109
  1032.1 134.6 %reduce-scatter.9.cloned.1.call-start = ((), (), s32[]{:S(2)}) async-start(), calls=%async_computation.19 | async-start | bytes 7045120 | tf_op jit(solution)/shard_map/reduce_scatter | solution.py:148
  1042.4 203.9 %reduce-scatter.5.cloned.1.call-start = ((), (), s32[]{:S(2)}) async-start(), calls=%async_computation.17 | async-start | bytes 5242880 | tf_op jit(solution)/shard_map/reduce_scatter | solution.py:148
  1051.9 273.9 %reduce-scatter.7.cloned.1.call-start = ((), (), s32[]{:S(2)}) async-start(), calls=%async_computation.18 | async-start | bytes 5242880 | tf_op jit(solution)/shard_map/reduce_scatter | solution.py:148
  1091.2 24.9 %collective-permute-start.16 = (bf16[128,2048]{1,0:T(8,128)(2,1)}, bf16[128,2048]{1,0:T(8,128)(2,1)}, u32[]{:S(2)}, u32[]{:S(2)}) collective-permute-start(bf16[128,2048]{1,0:T(8,128)(2,1)} %get-tuple-element.900), channel_id=1, source_target_pairs={{0,3},{1,2},{2,1},{3,0},{4,7},{5,6},{6,5},{7,4},{8,11},{9,10},{10,... | collective-permute-start | bytes 1572872 | tf_op jit(solution)/shard_map/ppermute | solution.py:109
  1246.3 81.8 %all-to-all-start.4 = ((bf16[8,64,1024]{2,1,0:T(8,128)(2,1)}), bf16[8,64,1024]{2,1,0:T(8,128)(2,1)}, u32[]{:S(2)}, u32[]{:S(2)}) async-start(bf16[8,64,1024]{2,1,0:T(8,128)(2,1)} %bitcast.848), calls=%async_computation.5 | async-start | bytes 2097152 | tf_op jit(solution)/shard_map/all_to_all | solution.py:151
  (179 other events, 1771.7 us)
Sparse Core Ops, SparseCore 0:
  30.8 80.7 all-gather.8
  113.2 79.8 all-gather.10
  194.7 105.4 all-gather.12
  445.7 67.8 all-gather.14
  540.6 53.7 reduce-scatter.10
  611.4 34.9 all-gather.16
  1032.2 31.9 all-reduce.11
  1066.5 100.1 reduce-scatter.8
  1169.0 77.2 reduce-scatter.4
  1248.6 77.2 reduce-scatter.6

commit v2 on v1

v2 whole, which is shorter than its diff:
```python
import functools

import jax
import jax.numpy as jnp
from jax import lax
from jax.experimental import pallas as pl
from jax.experimental.pallas import tpu as pltpu
from jax.sharding import Mesh
from jax.sharding import PartitionSpec as P

HEADS = 16
FF = 5504
HK = 2048
HV = 4096
PLANE = ("core", "seq")
KEY = 128
VALUE = 256
CONV = 4
EPS = 1e-06
BLOCK = 128
F32 = jnp.float32
LOW = jnp.bfloat16


def halves(x):
    high = x.astype(LOW)
    return (high, (x - high.astype(F32)).astype(LOW))


def thirds(x):
    high = x.astype(LOW)
    rest = x - high.astype(F32)
    middle = rest.astype(LOW)
    return (high, middle, (rest - middle.astype(F32)).astype(LOW))


def product(left, right, left_dim=1, right_dim=0):
    total = None
    for i, a in enumerate(left):
        for j, b in enumerate(right):
            if i + j < max(len(left), len(right)):
                term = lax.dot_general(
                    a, b, (((left_dim,), (right_dim,)), ((), ())), preferred_element_type=F32
                )
                total = term if total is None else total + term
    return total


def places():
    row = lax.broadcasted_iota(jnp.int32, (BLOCK, BLOCK), 0)
    col = lax.broadcasted_iota(jnp.int32, (BLOCK, BLOCK), 1)
    return row, col


def running(aux, row, col):
    lower = (row >= col).astype(LOW)
    return product((lower,), thirds(aux))


def solved(negated, row, col):
    diagonal = jnp.where((row >> 4) == (col >> 4), negated, 0.0)
    inverse = (row == col).astype(F32) + diagonal
    power = diagonal
    for _ in range(3):
        parts = halves(power)
        power = product(parts, parts)
        inverse = inverse + product(halves(inverse), halves(power))
    for bits in (4, 5, 6):
        beside = jnp.logical_and(
            (row >> (bits + 1)) == (col >> (bits + 1)), (row >> bits) != (col >> bits)
        )
        off = jnp.where(beside, negated, 0.0)
        parts = halves(inverse)
        inverse = inverse + product(parts, halves(product(halves(off), parts)))
    return inverse


def decays(aux, row, col, heads):
    sums = running(aux, row, col)
    turned = sums.T
    aux_turned = aux.T
    seg_col, seg_row = sums[:, 2 * heads : 2 * heads + 1], turned[2 * heads : 2 * heads + 1, :]
    joined = jnp.logical_and(row >= col, seg_col == seg_row)
    seg_last = sums[BLOCK - 1 :, 2 * heads : 2 * heads + 1]
    out = []
    for h in range(heads):
        g_col, g_row = sums[:, h : h + 1], turned[h : h + 1, :]
        pair = jnp.where(joined, jnp.exp(jnp.where(joined, g_col - g_row, 0.0)), 0.0)
        alive_col = jnp.where(seg_col == 0.0, jnp.exp(g_col), 0.0)
        alive_row = jnp.where(seg_row == 0.0, jnp.exp(g_row), 0.0)
        last = jnp.where(seg_col == seg_last, jnp.exp(sums[BLOCK - 1 :, h : h + 1] - g_col), 0.0)
        out.append(
            dict(
                pair=pair,
                decay_col=alive_col,
                decay_row=alive_row,
                decay_last=alive_col[BLOCK - 1 :, :],
                last=last,
                beta_col=aux[:, heads + h : heads + h + 1],
                beta_row=aux_turned[heads + h : heads + h + 1, :],
            )
        )
    return out


def convolved(ext, taps, aux, heads):
    total = taps[CONV - 1 : CONV, :] * ext(0)
    for lag in range(1, CONV):
        keep = aux[:, 2 * heads + lag : 2 * heads + lag + 1]
        total = total + taps[CONV - 1 - lag : CONV - lag, :] * (ext(lag) * keep)
    return total


def unit(raw):
    factor = lax.rsqrt(jnp.sum(raw * raw, axis=1, keepdims=True) + EPS)
    return raw * factor, factor


def mix_kernel(
    heads, x_ref, taps_ref, aux_ref, mixed_ref, inv_ref, upd_ref, state_ref, final_ref, ext, state
):
    step = pl.program_id(0)
    hk = heads * KEY
    row, col = places()

    @pl.when(step == 0)
    def _():
        state[...] = jnp.zeros_like(state)
        ext[:, :8, :] = jnp.zeros_like(ext[:, :8, :])

    state_ref[0] = state[...]
    taps = taps_ref[...]
    for r in range(2):
        aux = aux_ref[r]
        ext[r, 8:, :] = x_ref[r].astype(F32)
        conv = convolved(lambda lag: ext[r, 8 - lag : 8 - lag + BLOCK, :], taps, aux, heads)
        act = conv * jax.nn.sigmoid(conv)
        ext[r, :8, :] = ext[r, BLOCK:, :]
        facts = decays(aux, row, col, heads)
        for h in range(heads):
            f = facts[h]
            at = r * heads + h
            vs = slice(h * VALUE, (h + 1) * VALUE)
            query = (unit(act[:, h * KEY : (h + 1) * KEY])[0] * KEY ** (-0.5)).astype(LOW)
            keys = unit(act[:, hk + h * KEY : hk + (h + 1) * KEY])[0].astype(LOW)
            values = act[:, 2 * hk + h * VALUE : 2 * hk + (h + 1) * VALUE].astype(LOW)
            pair = f["pair"]
            similar = product((keys,), (keys,), 1, 1)
            negated = jnp.where(row > col, -(f["beta_col"] * pair * similar), 0.0)
            inverse = solved(negated, row, col)
            inv_ref[0, at] = inverse
            scaled = inverse * f["beta_row"]
            old = state[at]
            old_parts = halves(old)
            weights = halves(product(halves(scaled * f["decay_row"]), (keys,)))
            updates = product(halves(scaled), (values,)) - product(weights, old_parts)
            upd_ref[r, :, vs] = updates
            seen = product((query,), (keys,), 1, 1) * pair
            mixed_ref[r, :, vs] = f["decay_col"] * product((query,), old_parts) + product(
                halves(seen), halves(updates)
            )
            state[at] = f["decay_last"] * old + product(
                (keys,), halves(f["last"] * updates), 0, 0
            )

    @pl.when(step == pl.num_programs(0) - 1)
    def _():
        for at in range(2 * heads):
            final_ref[at] = state[at].T


def mix(x, taps, aux, heads):
    length, chan = x.shape[1:]
    count = length // BLOCK
    hv = heads * VALUE
    here = lambda j: (0, j, 0)
    saved = lambda j: (j, 0, 0, 0)
    return pl.pallas_call(
        functools.partial(mix_kernel, heads),
        grid=(count,),
        in_specs=[
            pl.BlockSpec((2, BLOCK, chan), here),
            pl.BlockSpec((CONV, chan), lambda j: (0, 0)),
            pl.BlockSpec((2, BLOCK, 128), here),
        ],
        out_specs=[
            pl.BlockSpec((2, BLOCK, hv), here),
            pl.BlockSpec((1, 2 * heads, BLOCK, BLOCK), saved),
            pl.BlockSpec((2, BLOCK, hv), here),
            pl.BlockSpec((1, 2 * heads, KEY, VALUE), saved),
            pl.BlockSpec((2 * heads, VALUE, KEY), lambda j: (0, 0, 0)),
        ],
        out_shape=[
            jax.ShapeDtypeStruct((2, length, hv), F32),
            jax.ShapeDtypeStruct((count, 2 * heads, BLOCK, BLOCK), F32),
            jax.ShapeDtypeStruct((2, length, hv), F32),
            jax.ShapeDtypeStruct((count, 2 * heads, KEY, VALUE), F32),
            jax.ShapeDtypeStruct((2 * heads, VALUE, KEY), F32),
        ],
        scratch_shapes=[
            pltpu.VMEM((2, BLOCK + 8, chan), F32),
            pltpu.VMEM((2 * heads, KEY, VALUE), F32),
        ],
        compiler_params=pltpu.CompilerParams(
            dimension_semantics=("arbitrary",), vmem_limit_bytes=48 * 1024 * 1024
        ),
        cost_estimate=pl.CostEstimate(
            flops=40_000_000_000, bytes_accessed=12_000_000, transcendentals=2_000_000
        ),
        name="mix_forward",
    )(x, taps, aux)


def slope(value):
    logistic = jax.nn.sigmoid(value)
    return logistic, logistic * (1.0 + value * (1.0 - logistic))


def mix_back_kernel(
    heads,
    x_ref,
    halo_ref,
    taps_ref,
    aux_ref,
    gate_ref,
    gain_ref,
    mixed_ref,
    inv_ref,
    upd_ref,
    state_ref,
    d_branch_ref,
    d_x_ref,
    d_gate_ref,
    d_aux_ref,
    d_taps_ref,
    d_gain_ref,
    ext,
    d_ext,
    d_state,
):
    step = pl.program_id(0)
    first_block = step == pl.num_programs(0) - 1
    hk = heads * KEY
    row, col = places()
    lane = lax.broadcasted_iota(jnp.int32, (BLOCK, 128), 1)
    position = lax.broadcasted_iota(jnp.int32, (BLOCK, 1), 0)

    @pl.when(step == 0)
    def _():
        d_state[...] = jnp.zeros_like(d_state)
        d_ext[:, BLOCK:, :] = jnp.zeros_like(d_ext[:, BLOCK:, :])
        d_taps_ref[...] = jnp.zeros_like(d_taps_ref)
        d_gain_ref[...] = jnp.zeros_like(d_gain_ref)

    taps = taps_ref[...]
    gain = gain_ref[...]
    for r in range(2):
        aux = aux_ref[r]
        before = halo_ref[r][8:, :].astype(F32)
        ext[r, :8, :] = jnp.where(first_block, 0.0, before)
        ext[r, 8:, :] = x_ref[r].astype(F32)
        shifted = lambda lag: ext[r, 8 - lag : 8 - lag + BLOCK, :]
        conv = convolved(shifted, taps, aux, heads)
        logistic, conv_slope = slope(conv)
        act = conv * logistic
        facts = decays(aux, row, col, heads)
        columns = jnp.zeros((BLOCK, 128), F32)
        rows = []
        d_query_raw, d_key_raw, d_value_raw = [], [], []
        d_betas = []
        for h in range(heads):
            f = facts[h]
            at = r * heads + h
            vs = slice(h * VALUE, (h + 1) * VALUE)
            query_unit, query_factor = unit(act[:, h * KEY : (h + 1) * KEY])
            key_unit, key_factor = unit(act[:, hk + h * KEY : hk + (h + 1) * KEY])
            query = (query_unit * KEY ** (-0.5)).astype(LOW)
            keys = key_unit.astype(LOW)
            values = act[:, 2 * hk + h * VALUE : 2 * hk + (h + 1) * VALUE].astype(LOW)
            mixed = mixed_ref[r, :, vs]
            gate = gate_ref[r, :, vs]
            d_branch = d_branch_ref[r, :, vs]
            factor = lax.rsqrt(jnp.mean(mixed * mixed, axis=1, keepdims=True) + EPS)
            normed = mixed * factor
            gate_logistic, gate_slope = slope(gate)
            d_scaled = d_branch * (gate * gate_logistic)
            d_gain_ref[...] += jnp.sum(d_scaled * normed, axis=0, keepdims=True)
            d_gate_ref[r, :, vs] = (d_branch * normed * gain * gate_slope).astype(LOW)
            d_normed = d_scaled * gain
            d_out = factor * (
                d_normed - normed * jnp.mean(d_normed * normed, axis=1, keepdims=True)
            )
            pair, beta, decay = f["pair"], f["beta_col"], f["decay_col"]
            inverse, updates, old = halves(inv_ref[0, at]), upd_ref[r, :, vs], state_ref[0, at]
            upd_parts, old_parts, out_parts = halves(updates), halves(old), halves(d_out)
            d_new = d_state[at]
            d_new_parts = halves(d_new)
            similar = product((keys,), (keys,), 1, 1)
            seen = product((query,), (keys,), 1, 1) * pair
            carried = product((keys,), d_new_parts)
            d_updates = product(halves(seen), out_parts, 0, 0) + f["last"] * carried
            d_targets = product(inverse, halves(d_updates), 0, 0)
            target_parts = halves(d_targets)
            below = jnp.where(row > col, -product(target_parts, upd_parts, 1, 1), 0.0)
            d_seen = product(out_parts, upd_parts, 1, 1)
            below_pair = below * pair
            d_similar = halves(below_pair * beta)
            d_seen_pair = halves(d_seen * pair)
            target_state = product(target_parts, old_parts, 1, 1)
            out_state = product(out_parts, old_parts, 1, 1)
            keys_wide, query_wide = keys.astype(F32), query.astype(F32)
            d_query = decay * out_state + product(d_seen_pair, (keys,))
            d_keys = (
                product(d_similar, (keys,))
                + product(d_similar, (keys,), 0, 0)
                + product(d_seen_pair, (query,), 0, 0)
                + f["last"] * product(upd_parts, d_new_parts, 1, 1)
                - (beta * decay) * target_state
            )
            d_values = beta * d_targets
            key_target = jnp.sum(keys_wide * target_state, axis=1, keepdims=True)
            by_beta = below_pair * similar
            d_beta = (
                jnp.sum(d_targets * values.astype(F32), axis=1, keepdims=True)
                - decay * key_target
                + jnp.sum(by_beta, axis=1, keepdims=True)
            )
            d_pair = by_beta * beta + d_seen * seen
            d_decay = jnp.sum(query_wide * out_state, axis=1, keepdims=True) - beta * key_target
            d_last = f["last"] * jnp.sum(updates * carried, axis=1, keepdims=True)
            at_last = jnp.sum(d_last, axis=0, keepdims=True) + f["decay_last"] * jnp.sum(
                jnp.sum(d_new * old, axis=1, keepdims=True), axis=0, keepdims=True
            )
            d_sums = (
                jnp.sum(d_pair, axis=1, keepdims=True)
                + decay * d_decay
                - d_last
                + jnp.where(position == BLOCK - 1, at_last, 0.0)
            )
            columns = jnp.where(lane == h, d_sums, columns)
            rows.append(jnp.sum(d_pair, axis=0, keepdims=True))
            d_betas.append(d_beta)
            d_state[at] = (
                f["decay_last"] * d_new
                + product((query,), halves(decay * d_out), 0, 0)
                - product((keys,), halves((beta * decay) * d_targets), 0, 0)
            )
            d_query = d_query.astype(LOW).astype(F32) * KEY ** (-0.5)
            d_keys = d_keys.astype(LOW).astype(F32)
            d_query_raw.append(
                query_factor
                * (d_query - query_unit * jnp.sum(d_query * query_unit, axis=1, keepdims=True))
            )
            d_key_raw.append(
                key_factor * (d_keys - key_unit * jnp.sum(d_keys * key_unit, axis=1, keepdims=True))
            )
            d_value_raw.append(d_values.astype(LOW).astype(F32))
        turned = jnp.concatenate(
            rows + [jnp.zeros((128 - heads, BLOCK), F32)], axis=0
        ).T
        upper = (row <= col).astype(LOW)
        d_aux = product((upper,), thirds(columns - turned))
        for h in range(heads):
            d_aux = jnp.where(lane == heads + h, d_betas[h], d_aux)
        d_aux_ref[r] = d_aux
        d_conv = jnp.concatenate(d_query_raw + d_key_raw + d_value_raw, axis=1) * conv_slope
        d_ext_sum = taps[CONV - 1 : CONV, :] * d_conv
        d_taps_ref[CONV - 1 : CONV, :] += jnp.sum(d_conv * shifted(0), axis=0, keepdims=True)
        for lag in range(1, CONV):
            masked = d_conv * aux[:, 2 * heads + lag : 2 * heads + lag + 1]
            d_taps_ref[CONV - 1 - lag : CONV - lag, :] += jnp.sum(
                masked * shifted(lag), axis=0, keepdims=True
            )
            slot = r * (CONV - 1) + lag - 1
            d_ext[slot, :BLOCK, :] = masked
            d_ext_sum = (
                d_ext_sum + taps[CONV - 1 - lag : CONV - lag, :] * d_ext[slot, lag : lag + BLOCK, :]
            )
            d_ext[slot, BLOCK:, :] = d_ext[slot, :8, :]
        d_x_ref[r] = d_ext_sum.astype(LOW)


def mix_back(x, taps, aux, gate, gain, mixed, inverses, updates, states, d_branch, heads):
    length, chan = x.shape[1:]
    count = length // BLOCK
    hv = heads * VALUE
    here = lambda j: (0, count - 1 - j, 0)
    halo = lambda j: (0, jnp.maximum((count - 1 - j) * (BLOCK // 16) - 1, 0), 0)
    saved = lambda j: (count - 1 - j, 0, 0, 0)
    fixed = lambda j: (0, 0)
    return pl.pallas_call(
        functools.partial(mix_back_kernel, heads),
        grid=(count,),
        in_specs=[
            pl.BlockSpec((2, BLOCK, chan), here),
            pl.BlockSpec((2, 16, chan), halo),
            pl.BlockSpec((CONV, chan), fixed),
            pl.BlockSpec((2, BLOCK, 128), here),
            pl.BlockSpec((2, BLOCK, hv), here),
            pl.BlockSpec((1, VALUE), fixed),
            pl.BlockSpec((2, BLOCK, hv), here),
            pl.BlockSpec((1, 2 * heads, BLOCK, BLOCK), saved),
            pl.BlockSpec((2, BLOCK, hv), here),
            pl.BlockSpec((1, 2 * heads, KEY, VALUE), saved),
            pl.BlockSpec((2, BLOCK, hv), here),
        ],
        out_specs=[
            pl.BlockSpec((2, BLOCK, chan), here),
            pl.BlockSpec((2, BLOCK, hv), here),
            pl.BlockSpec((2, BLOCK, 128), here),
            pl.BlockSpec((CONV, chan), fixed),
            pl.BlockSpec((1, VALUE), fixed),
        ],
        out_shape=[
            jax.ShapeDtypeStruct((2, length, chan), LOW),
            jax.ShapeDtypeStruct((2, length, hv), LOW),
            jax.ShapeDtypeStruct((2, length, 128), F32),
            jax.ShapeDtypeStruct((CONV, chan), F32),
            jax.ShapeDtypeStruct((1, VALUE), F32),
        ],
        scratch_shapes=[
            pltpu.VMEM((2, BLOCK + 8, chan), F32),
            pltpu.VMEM((2 * (CONV - 1), BLOCK + 8, chan), F32),
            pltpu.VMEM((2 * heads, KEY, VALUE), F32),
        ],
        compiler_params=pltpu.CompilerParams(
            dimension_semantics=("arbitrary",), vmem_limit_bytes=48 * 1024 * 1024
        ),
        cost_estimate=pl.CostEstimate(
            flops=60_000_000_000, bytes_accessed=20_000_000, transcendentals=4_000_000
        ),
        name="mix_backward",
    )(x, x, taps, aux, gate, gain, mixed, inverses, updates, states, d_branch)


def contract_rows(left, right):
    return lax.dot_general(
        left, right, (((1,), (1,)), ((), ())), preferred_element_type=jnp.float32
    )


def contract_tokens(left, right):
    return lax.dot_general(
        left, right, (((0,), (0,)), ((), ())), preferred_element_type=jnp.float32
    )


def silu_slope(value):
    logistic = jax.nn.sigmoid(value)
    return logistic * (1.0 + value * (1.0 - logistic))


def norm_back(normed, factor, grad):
    return factor * (grad - normed * jnp.mean(grad * normed, axis=-1, keepdims=True))


def swap_core(x):
    return lax.ppermute(x, "core", [(0, 1), (1, 0)])


def from_peer(x, axis, distance):
    return lax.ppermute(x, axis, [(i, i ^ distance) for i in range(lax.axis_size(axis))])


def plane_gather(x, ordered):
    size, me = lax.axis_size("seq"), lax.axis_index("seq")
    blocks = [x] + [from_peer(x, "seq", k) for k in range(1, size)]
    others = [swap_core(b) for b in blocks]
    if not ordered:
        return jnp.concatenate(blocks + others, axis=0)
    tokens = x.shape[0]
    whole = jnp.zeros((2 * size * tokens,) + x.shape[1:], x.dtype)
    for k in range(size):
        whole = lax.dynamic_update_slice(whole, blocks[k], ((me ^ k) * tokens, 0))
        whole = lax.dynamic_update_slice(whole, others[k], ((size + (me ^ k)) * tokens, 0))
    return whole


def plane_sum(x, ordered):
    size, me = lax.axis_size("seq"), lax.axis_index("seq")
    half = x.shape[0] // 2
    tokens = half // size
    row = x[:half] + swap_core(x[half:].astype(jnp.bfloat16)).astype(jnp.float32)

    def block(k):
        at = (me ^ k) * tokens if ordered else k * tokens
        return lax.dynamic_slice_in_dim(row, at, tokens, 0)

    total = block(0)
    for k in range(1, size):
        total = total + from_peer(block(k).astype(jnp.bfloat16), "seq", k).astype(jnp.float32)
    return total


def by_holder(parts, split):
    rows = parts[0].shape[0]
    return jnp.concatenate(
        [jnp.swapaxes(p.reshape(rows, split, -1), 0, 1) for p in parts], axis=2
    )


def plane_exchange(blocks):
    got = lax.all_to_all(blocks, PLANE, 0, 0)
    return got.reshape(-1, got.shape[2])


def along_z(x):
    return lax.all_gather(x, "z", axis=0, tiled=True)


def shard_sum(partial):
    return lax.psum_scatter(partial, "z", scatter_dimension=0, tiled=True)


def to_holders(mine, split):
    blocks = lax.all_to_all(mine.reshape(split, -1, mine.shape[1]), PLANE, 0, 0)
    return jnp.swapaxes(blocks, 0, 1).astype(jnp.float32)


def butterfly(x, axis):
    distance = 1
    while distance < lax.axis_size(axis):
        x = x + from_peer(x, axis, distance)
        distance *= 2
    return x


def on_device(
    hidden_in,
    boundary,
    norm_gain,
    proj_weight,
    rate_weight,
    conv_weight,
    log_rate,
    rate_bias,
    head_gain,
    out_weight,
    ffn_norm_gain,
    gate_up_weight,
    down_weight,
    grad_out,
):
    own = hidden_in.shape[1]
    width = hidden_in.shape[2]
    seq = lax.axis_size("seq")
    split = 2 * seq
    length = own * seq
    tokens = 2 * length
    heads = HEADS // split
    hk, hv, ff = heads * KEY, heads * VALUE, FF // split
    chan = 2 * hk + hv
    me = lax.axis_index("seq")
    core = lax.axis_index("core")
    here = core * seq + me
    rows = proj_weight.shape[0]

    def own_columns(whole, count):
        return lax.dynamic_slice_in_dim(whole, here * count, count, whole.ndim - 1)

    mix_in = plane_exchange(
        by_holder(
            [
                proj_weight[:, :HK],
                proj_weight[:, HK : 2 * HK],
                proj_weight[:, 2 * HK : 2 * HK + HV],
                rate_weight[:, :HEADS],
                rate_weight[:, HEADS:],
            ],
            split,
        )
    )
    x = hidden_in[0].astype(jnp.float32)
    scale = lax.rsqrt(jnp.mean(x * x, axis=1, keepdims=True) + EPS)
    normed = x * scale
    first_in = plane_gather((normed * norm_gain).astype(jnp.bfloat16), True)
    others = by_holder(
        [
            proj_weight[:, 2 * HK + HV :],
            out_weight,
            gate_up_weight[:, :FF],
            gate_up_weight[:, FF:],
            down_weight,
        ],
        split,
    )
    first_in, others = lax.optimization_barrier((first_in, others))
    others = plane_exchange(others)
    mix_in = along_z(mix_in)
    gate_out = along_z(others[:, : 2 * hv])
    gate_in, out_cols = gate_out[:, :hv], gate_out[:, hv:]
    cut = -(-ff // 256) * 128
    parts = [slice(0, cut), slice(cut, ff)]
    gates = [others[:, 2 * hv :][:, p] for p in parts]
    ups = [others[:, 2 * hv + ff :][:, p] for p in parts]
    downs = [others[:, 2 * hv + 2 * ff :][:, p] for p in parts]
    ffn = [along_z(jnp.concatenate(w, axis=1)) for w in zip(gates, ups, downs)]
    cot = plane_gather(grad_out[0], False)

    bounds = jnp.concatenate([boundary, swap_core(boundary)], axis=0)
    positions = jnp.arange(length)
    start = jnp.logical_or(
        jnp.any(positions[None, :, None] == bounds[:, None, :], axis=2), positions == 0
    ).astype(jnp.float32)
    keep = jnp.ones((2, length), jnp.float32)
    keeps = []
    for lag in range(1, CONV):
        keep = keep * (1.0 - jnp.pad(start, ((0, 0), (lag - 1, 0)))[:, :length])
        keeps.append(keep)
    taps = jnp.concatenate(
        [
            own_columns(conv_weight[:, :HK], hk),
            own_columns(conv_weight[:, HK : 2 * HK], hk),
            own_columns(conv_weight[:, 2 * HK :], hv),
        ],
        axis=1,
    )
    own_rate, own_bias = own_columns(log_rate, heads), own_columns(rate_bias, heads)

    conv_in = jnp.dot(first_in, mix_in[:, :chan], preferred_element_type=jnp.float32)
    conv_in = conv_in.astype(jnp.bfloat16).reshape(2, length, chan)
    rates = jnp.dot(first_in, mix_in[:, chan:], preferred_element_type=jnp.float32)
    rates = rates.reshape(2, length, 2 * heads)
    rate_input = rates[:, :, :heads] + own_bias
    decay_log = -jnp.exp(own_rate) * jax.nn.softplus(rate_input)
    beta = jax.nn.sigmoid(rates[:, :, heads:])
    aux = jnp.concatenate([decay_log, beta] + [s[:, :, None] for s in [start] + keeps], axis=2)
    aux = jnp.pad(aux, ((0, 0), (0, 0), (0, 128 - aux.shape[2])))
    mixed, inverses, updates, states, final = mix(conv_in, taps, aux, heads)

    gate = jnp.dot(first_in, gate_in, preferred_element_type=jnp.float32).reshape(2, length, hv)
    branch = []
    for h in range(heads):
        part = mixed[:, :, h * VALUE : (h + 1) * VALUE]
        factor = lax.rsqrt(jnp.mean(part * part, axis=2, keepdims=True) + EPS)
        branch.append(
            part * factor * head_gain * jax.nn.silu(gate[:, :, h * VALUE : (h + 1) * VALUE])
        )
    branch = jnp.concatenate(branch, axis=2).astype(jnp.bfloat16).reshape(tokens, hv)
    hidden = x + plane_sum(contract_rows(branch, out_cols), True)

    scale_two = lax.rsqrt(jnp.mean(hidden * hidden, axis=1, keepdims=True) + EPS)
    normed_two = hidden * scale_two
    second_in = plane_gather((normed_two * ffn_norm_gain).astype(jnp.bfloat16), False)
    d_second = jnp.zeros((tokens, width), jnp.float32)
    fed = jnp.zeros((tokens, width), jnp.float32)
    grad_ffn = []
    for weight in ffn:
        units = weight.shape[1] // 3
        both_in, down_in = weight[:, : 2 * units], weight[:, 2 * units :]
        both = jnp.dot(second_in, both_in, preferred_element_type=jnp.float32)
        gate_part, up_part = both[:, :units], both[:, units:]
        gate_silu = jax.nn.silu(gate_part)
        inner = (gate_silu * up_part).astype(jnp.bfloat16)
        d_inner = jnp.dot(cot, down_in, preferred_element_type=jnp.float32)
        d_both = jnp.concatenate(
            [d_inner * up_part * silu_slope(gate_part), d_inner * gate_silu], axis=1
        ).astype(jnp.bfloat16)
        d_second = d_second + contract_rows(d_both, both_in)
        fed = fed + contract_rows(inner, down_in)
        grad_ffn.append(
            jnp.concatenate(
                [contract_tokens(second_in, d_both), contract_tokens(cot, inner)], axis=1
            ).astype(jnp.bfloat16)
        )
    grad_ffn[0] = shard_sum(grad_ffn[0])
    grad_ffn[1], grad_ffn[0] = lax.optimization_barrier((grad_ffn[1], grad_ffn[0]))
    grad_ffn[1] = shard_sum(grad_ffn[1])
    d_second = plane_sum(d_second, False)
    result = hidden + plane_sum(fed, False)
    grad_gain_two = jnp.sum(d_second * normed_two, axis=0)
    d_hidden = grad_out[0].astype(jnp.float32) + norm_back(
        normed_two, scale_two, d_second * ffn_norm_gain
    )

    d_mix = plane_gather(d_hidden.astype(jnp.bfloat16), True)
    d_branch = jnp.dot(d_mix, out_cols, preferred_element_type=jnp.float32)
    grad_out_cols = contract_tokens(d_mix, branch).astype(jnp.bfloat16)
    d_branch, grad_ffn[0] = lax.optimization_barrier((d_branch, grad_ffn[0]))
    d_conv_in, d_gate, d_aux, grad_taps, grad_head_gain = mix_back(
        conv_in,
        taps,
        aux,
        gate,
        head_gain[None],
        mixed,
        inverses,
        updates,
        states,
        d_branch.reshape(2, length, hv),
        heads,
    )
    d_conv_in = d_conv_in.reshape(tokens, chan)
    d_gate = d_gate.reshape(tokens, hv)
    d_decay, d_beta = d_aux[:, :, :heads], d_aux[:, :, heads : 2 * heads]
    d_rate_input = d_decay * -jnp.exp(own_rate) * jax.nn.sigmoid(rate_input)
    grad_log_rate = jnp.sum(d_decay * decay_log, axis=(0, 1))
    grad_rate_bias = jnp.sum(d_rate_input, axis=(0, 1))
    d_rates = jnp.concatenate([d_rate_input, d_beta * beta * (1.0 - beta)], axis=2)
    d_rates = d_rates.astype(jnp.bfloat16).reshape(tokens, 2 * heads)
    d_mix_in = jnp.concatenate([d_conv_in, d_rates], axis=1)
    grad_gate_out = jnp.concatenate(
        [contract_tokens(first_in, d_gate).astype(jnp.bfloat16), grad_out_cols], axis=1
    )
    grad_gate_out, grad_ffn[1] = lax.optimization_barrier((grad_gate_out, grad_ffn[1]))
    grad_gate_out = shard_sum(grad_gate_out)
    grad_mix_in = contract_tokens(first_in, d_mix_in).astype(jnp.bfloat16)
    grad_mix_in, grad_gate_out = lax.optimization_barrier((grad_mix_in, grad_gate_out))
    grad_mix_in = to_holders(shard_sum(grad_mix_in), split)
    grad_gate_out = to_holders(grad_gate_out, split)
    grad_ffn = [to_holders(g, split) for g in grad_ffn]
    d_first = contract_rows(d_mix_in, mix_in) + contract_rows(d_gate, gate_in)
    d_first = plane_sum(d_first, True)
    grad_gain_one = jnp.sum(d_first * normed, axis=0)
    d_row = d_hidden + norm_back(normed, scale, d_first * norm_gain)

    sides = jnp.pad(jnp.concatenate([grad_log_rate, grad_rate_bias]), (0, chan - 2 * heads))
    sides = butterfly(jnp.concatenate([grad_taps, sides[None]], axis=0), "z")
    blocks = [sides] + [from_peer(sides, "seq", k) for k in range(1, seq)]
    blocks = [[b, swap_core(b)] for b in blocks]
    sides = jnp.zeros((2, seq) + sides.shape, jnp.float32)
    for k in range(seq):
        for c in range(2):
            sides = lax.dynamic_update_slice(
                sides, blocks[k][c][None, None], (core ^ c, me ^ k, 0, 0)
            )
    sides = sides.reshape(split, CONV + 1, chan)
    grad_conv = jnp.swapaxes(sides[:, :CONV], 0, 1)
    grad_conv = jnp.concatenate(
        [
            grad_conv[:, :, :hk].reshape(CONV, HK),
            grad_conv[:, :, hk : 2 * hk].reshape(CONV, HK),
            grad_conv[:, :, 2 * hk :].reshape(CONV, HV),
        ],
        axis=1,
    )
    sums = jnp.concatenate([grad_gain_one, grad_gain_two, grad_head_gain[0]])
    sums = butterfly(butterfly(butterfly(sums, "core"), "seq"), "z")
    grad_proj = jnp.concatenate(
        [
            grad_mix_in[:, :, :hk].reshape(rows, HK),
            grad_mix_in[:, :, hk : 2 * hk].reshape(rows, HK),
            grad_mix_in[:, :, 2 * hk : chan].reshape(rows, HV),
            grad_gate_out[:, :, :hv].reshape(rows, HV),
        ],
        axis=1,
    )
    grad_rate = jnp.concatenate(
        [
            grad_mix_in[:, :, chan : chan + heads].reshape(rows, HEADS),
            grad_mix_in[:, :, chan + heads :].reshape(rows, HEADS),
        ],
        axis=1,
    )
    units = [g.shape[2] // 3 for g in grad_ffn]

    def hidden_columns(at):
        return jnp.concatenate(
            [g[:, :, at * u : (at + 1) * u] for g, u in zip(grad_ffn, units)], axis=2
        ).reshape(rows, FF)

    grad_gate_up = jnp.concatenate([hidden_columns(0), hidden_columns(1)], axis=1)

    final = final.reshape(2, heads, VALUE, KEY)
    other = swap_core(final[1].astype(jnp.bfloat16))
    pair = jnp.zeros((2, heads, VALUE, KEY), jnp.bfloat16)
    pair = lax.dynamic_update_index_in_dim(pair, final[0].astype(jnp.bfloat16), core, 0)
    pair = lax.dynamic_update_index_in_dim(pair, other, 1 - core, 0)
    final_state = jnp.zeros((2, seq, heads, VALUE, KEY), jnp.float32)
    for k in range(seq):
        block = from_peer(pair, "seq", k) if k else pair
        final_state = lax.dynamic_update_index_in_dim(
            final_state, block.astype(jnp.float32), me ^ k, 1
        )
    return (
        result.astype(jnp.bfloat16)[None],
        d_row.astype(jnp.bfloat16)[None],
        final_state.reshape(1, HEADS, VALUE, KEY),
        sums[:width],
        grad_proj,
        grad_rate,
        grad_conv,
        sides[:, CONV, :heads].reshape(HEADS),
        sides[:, CONV, heads : 2 * heads].reshape(HEADS),
        sums[2 * width :],
        grad_gate_out[:, :, hv:].reshape(rows, HV),
        sums[width : 2 * width],
        grad_gate_up,
        hidden_columns(2),
    )


def solution(mesh):
    dp, seq = mesh.shape["dp"], mesh.shape["seq"]
    planes = Mesh(mesh.devices.reshape(dp // 2, 2, seq), ("z", "core", "seq"))
    row = ("z", "core")
    every = ("z", "core", "seq")
    in_specs = (
        P(row, "seq", None),
        P(row, None),
        P(),
        P(every, None),
        P(every, None),
        P(),
        P(),
        P(),
        P(),
        P(every, None),
        P(),
        P(every, None),
        P(every, None),
        P(row, "seq", None),
    )
    out_specs = (
        P(row, "seq", None),
        P(row, "seq", None),
        P(row, None, None, None),
        P(),
        P(every, None),
        P(every, None),
        P(),
        P(),
        P(),
        P(),
        P(every, None),
        P(),
        P(every, None),
        P(every, None),
    )
    return jax.shard_map(
        on_device, mesh=planes, in_specs=in_specs, out_specs=out_specs, check_vma=False
    )
```

time: 1370 us -> 785 us (0.57)
  matrix products: 392 us -> 105 us
  local copies, waits for them, and re-layouts: 249 us -> 129 us
  blocking collectives: 152 us -> 41.7 us
  other arithmetic: 137 us -> 57.3 us
  Pallas kernels: 0 us -> 75.2 us
  waiting for transfers between devices: 340 us -> 271 us
  starting transfers between devices: 65.6 us -> 79.5 us
    dot_general x533 -> x7, matrix products: 328 us -> 35.9 us  [the longest x2 12.3 us: on_device(): both = jnp.dot(second_in, both_in, preferred_element_type=jnp.float32)]
    reduce_scatter x4, waiting for transfers between devices: 141 us -> 23 us  [shard_sum(): return lax.psum_scatter(partial, 'z', scatter_dimension=0, tiled=True)]
    all_gather x2 -> x0, blocking collectives: 114 us -> none  [the longest x1 89.4 us: on_device(): lax.all_gather(rate_weight, ('z', 'core', 'seq'), axis=0, tiled=True)]
    pallas_call x0 -> x2, Pallas kernels: none -> 75.2 us  [the longest x1 44.2 us: mix(): pl.pallas_call(functools.partial(mix_kernel, heads), grid=(count,), in_sp...]
    squeeze x72 -> x0, local copies, waits for them, and re-layouts: 67.9 us -> none  [seq_pass(): final, outputs = lax.scan(jax.checkpoint(group_pass), state, pieces)]
    ppermute x24 -> x37, waiting for transfers between devices: 114 us -> 152 us  [from_peer(): lax.ppermute(x, axis, [(i, i ^ distance) for i in range(lax.axis_size(axi...]
    reshape x21 -> x12, local copies, waits for them, and re-layouts: 35.9 us -> 11 us  [the longest x7 6.82 us: by_holder(): p.reshape(rows, split, -1)]
    reduce_sum x23 -> x1, other arithmetic: 21.2 us -> 0.35 us  [on_device(): factor = lax.rsqrt(jnp.mean(part * part, axis=2, keepdims=True) + EPS)]
  transfers between devices with their start and end apart: 49 -> 76, of which waited for: 22 -> 35; matrix products, arithmetic and copies ran while one was open for 54% -> 33% of each run, Pallas kernels for 0% -> 10%
where the time goes in v2:
time: 785 us; the launch traced here: 776 us
  waiting for transfers between devices  271 us (35%)
  local copies, waits for them, and re-layouts  129 us (16%)
  matrix products  105 us (13%)
  starting transfers between devices  79.5 us (10%)
  Pallas kernels  75.2 us (10%)
  other arithmetic  57.3 us (7%)
  blocking collectives  41.7 us (5%)
  between operations  16.3 us (2%)
    ppermute x37, waiting for transfers between devices, from_peer(): lax.ppermute(x, axis, [(i, i ^ distance) for i in range(lax.axis_size(axi...  152 us
    all_gather x4, waiting for transfers between devices, along_z(): return lax.all_gather(x, 'z', axis=0, tiled=True)  61.3 us
    ppermute x37, starting transfers between devices, from_peer(): lax.ppermute(x, axis, [(i, i ^ distance) for i in range(lax.axis_size(axi...  53.5 us
    pallas_call x1, Pallas kernels, mix(): pl.pallas_call(functools.partial(mix_kernel, heads), grid=(count,), in_sp...  44.2 us
    all_to_all x1, blocking collectives, plane_exchange(): got = lax.all_to_all(blocks, PLANE, 0, 0)  41.7 us
    dot_general x7, matrix products, contract_rows(): lax.dot_general(left, right, (((1,), (1,)), ((), ())), preferred_element_...  39.4 us
    unnamed x193, local copies, waits for them, and re-layouts  33.9 us
    pallas_call x1, Pallas kernels, mix_back(): pl.pallas_call(functools.partial(mix_back_kernel, heads), grid=(count,),...  30.9 us
  transfers between devices with their start and end apart: 76, of which 35 were waited for; matrix products, arithmetic and copies ran while one was open for 33% of the time, Pallas kernels for 10%

profile of v2, /device:TPU:0, one launch (start us, length us, event | category | flops | bytes accessed | tf_op | source)
XLA Modules:
  0.0 775.8 jit_solution(9014647315071705003)
XLA Ops:
  25.5 9.7 %all-to-all-done = bf16[8,64,1028]{2,1,0:T(8,128)(2,1)S(1)} async-done(((bf16[8,64,1028]{2,1,0:T(8,128)(2,1)}), bf16[8,64,1028]{2,1,0:T(8,128)(2,1)S(1)}, u32[]{:S(2)}, u32[]{:S(2)}) %all-to-all-start) | async-done | bytes 1052704 | tf_op jit(solution)/shard_map/all_to_all | solution.py:503
  51.6 5.6 concatenate.96
  69.4 41.7 %all_to_all.30 = bf16[8,64,3088]{2,1,0:T(8,128)(2,1)S(1)} all-to-all(bf16[8,64,3088]{2,1,0:T(8,128)(2,1)S(1)} %copy-done.14), channel_id=1, replica_groups=mesh['z'=4,'core'=2,'seq'=4] {'core','seq'}, dimensions={0} | all-to-all | bytes 6324224 | tf_op jit(solution)/shard_map/all_to_all | solution.py:503
  120.0 6.0 all-gather.5.cloned.1.call-done
  133.6 10.1 %fusion.9 = bf16[1024,1024]{1,0:T(8,128)(2,1)} fusion(bf16[1024,2048]{1,0:T(8,128)(2,1)} %constant_dynamic-update-slice_fusion.24, bf16[2048,1028]{1,0:T(8,128)(2,1)} %all-gather.5.cloned.1.call-done), kind=kOutput, calls=%fused_computation.36 | convolution fusion | flops 4296015872 | bytes 10485760 | tf_op jit(solution)/shard_map/dot_general | solution.py:620
  143.7 44.2 %mix_forward.1 = (f32[2,512,512]{2,1,0:T(8,128)S(1)}, f32[4,4,128,128]{3,2,1,0:T(8,128)S(1)}, f32[2,512,512]{2,1,0:T(8,128)}, f32[4,4,128,256]{3,2,1,0:T(8,128)}, f32[4,256,128]{2,1,0:T(8,128)S(1)}) custom-call(bf16[2,512,1024]{2,1,0:T(8,128)(2,1)} %bitcast.237, f32[4,1024]{1,0:T(4,128)S(1)} %pad_maximum_fusion.22.taps_ref, f32[2,512,128]{2,1,0:T(8,128)S(1)} %pad.18.aux_ref), custom_call_target="tpu_custom_call" | custom-call | flops 40000000000 | bytes 12000000 | tf_op jit(solution)/shard_map/mix_forward/pallas_call | solution.py:178
  190.1 17.4 %all-gather.7.cloned.1.call-done = bf16[2048,1024]{1,0:T(8,128)(2,1)} async-done(((bf16[512,1024]{1,0:T(8,128)(2,1)}), bf16[2048,1024]{1,0:T(8,128)(2,1)}) %all-gather.7.cloned.1.call-update) | async-done | bytes 4194320 | tf_op jit(solution)/shard_map/all_gather | solution.py:508
  226.9 12.2 %collective-permute-done.25 = bf16[128,2048]{1,0:T(8,128)(2,1)} collective-permute-done((bf16[128,2048]{1,0:T(8,128)(2,1)S(1)}, bf16[128,2048]{1,0:T(8,128)(2,1)}, u32[]{:S(2)}, u32[]{:S(2)}) %collective-permute-start.25) | collective-permute-done | bytes 524320 | tf_op jit(solution)/shard_map/ppermute | solution.py:462
  239.2 10.9 %collective-permute-done.23 = bf16[128,2048]{1,0:T(8,128)(2,1)} collective-permute-done((bf16[128,2048]{1,0:T(8,128)(2,1)S(1)}, bf16[128,2048]{1,0:T(8,128)(2,1)}, u32[]{:S(2)}, u32[]{:S(2)}) %collective-permute-start.23) | collective-permute-done | bytes 524320 | tf_op jit(solution)/shard_map/ppermute | solution.py:462
  263.8 7.2 collective-permute-done.9
  271.0 11.0 %collective-permute-done.11 = bf16[128,2048]{1,0:T(8,128)(2,1)S(1)} collective-permute-done((bf16[128,2048]{1,0:T(8,128)(2,1)S(1)}, bf16[128,2048]{1,0:T(8,128)(2,1)S(1)}, u32[]{:S(2)}, u32[]{:S(2)}) %collective-permute-start.11) | collective-permute-done | bytes 524320 | tf_op jit(solution)/shard_map/ppermute | solution.py:462
  293.8 7.0 collective-permute-done.14
  300.9 9.4 %collective-permute-done.13 = bf16[128,2048]{1,0:T(8,128)(2,1)} collective-permute-done((bf16[128,2048]{1,0:T(8,128)(2,1)S(1)}, bf16[128,2048]{1,0:T(8,128)(2,1)}, u32[]{:S(2)}, u32[]{:S(2)}) %collective-permute-start.13) | collective-permute-done | bytes 524320 | tf_op jit(solution)/shard_map/ppermute | solution.py:462
  319.8 6.5 fusion.4
  340.3 37.9 %all-gather.11.cloned.1.call-done = bf16[2048,912]{1,0:T(8,128)(2,1)} async-done(((bf16[512,912]{1,0:T(8,128)(2,1)}), bf16[2048,912]{1,0:T(8,128)(2,1)}) %all-gather.11.cloned.1.call-update) | async-done | bytes 3735568 | tf_op jit(solution)/shard_map/all_gather | solution.py:508
  378.3 5.7 fusion.7
  386.5 5.7 fusion.2
  392.3 6.0 convolution_add_fusion.2
  407.6 11.3 %collective-permute-done.31 = bf16[128,2048]{1,0:T(8,128)(2,1)S(1)} collective-permute-done((bf16[128,2048]{1,0:T(8,128)(2,1)S(1)}, bf16[128,2048]{1,0:T(8,128)(2,1)S(1)}, u32[]{:S(2)}, u32[]{:S(2)}) %collective-permute-start.31) | collective-permute-done | bytes 524320 | tf_op jit(solution)/shard_map/ppermute | solution.py:462
  418.9 11.5 %collective-permute-done.33 = bf16[128,2048]{1,0:T(8,128)(2,1)S(1)} collective-permute-done((bf16[128,2048]{1,0:T(8,128)(2,1)S(1)}, bf16[128,2048]{1,0:T(8,128)(2,1)S(1)}, u32[]{:S(2)}, u32[]{:S(2)}) %collective-permute-start.33) | collective-permute-done | bytes 524320 | tf_op jit(solution)/shard_map/ppermute | solution.py:462
  448.3 15.3 %collective-permute-done.37 = bf16[128,2048]{1,0:T(8,128)(2,1)S(1)} collective-permute-done((bf16[128,2048]{1,0:T(8,128)(2,1)}, bf16[128,2048]{1,0:T(8,128)(2,1)S(1)}, u32[]{:S(2)}, u32[]{:S(2)}) %collective-permute-start.37) | collective-permute-done | bytes 524320 | tf_op jit(solution)/shard_map/ppermute | solution.py:462
  480.3 30.9 %mix_backward.1 = (bf16[2,512,1024]{2,1,0:T(8,128)(2,1)S(1)}, bf16[2,512,512]{2,1,0:T(8,128)(2,1)S(1)}, f32[2,512,128]{2,1,0:T(8,128)S(1)}, f32[4,1024]{1,0:T(4,128)S(1)}, f32[1,256]{1,0:T(1,128)S(1)}) custom-call(bf16[2,512,1024]{2,1,0:T(8,128)(2,1)} %bitcast.238, bf16[2,512,1024]{2,1,0:T(8,128)(2,1)} %bitcast.239, ...), custom_call_target="tpu_custom_call" | custom-call | flops 60000002048 | bytes 20000000 | tf_op jit(solution)/shard_map/mix_backward/pallas_call | solution.py:391
  516.2 22.2 %reduce-scatter.7.cloned.1.call-done = bf16[512,912]{0,1:T(8,128)(2,1)} async-done(((bf16[2048,912]{0,1:T(8,128)(2,1)}), bf16[512,912]{0,1:T(8,128)(2,1)}) %reduce-scatter.7.cloned.1.call-update) | async-done | bytes 933904 | tf_op jit(solution)/shard_map/reduce_scatter | solution.py:512
  574.6 6.8 fusion.75
  588.3 10.4 %fusion.91 = f32[1024,2048]{1,0:T(8,128)} fusion(bf16[1024,1028]{1,0:T(8,128)(2,1)} %concatenate.114, bf16[2048,1028]{1,0:T(8,128)(2,1)} %all-gather.5.cloned.1.call-done), kind=kOutput, calls=%fused_computation.243 | convolution fusion | flops 4311744512 | bytes 14704640 | tf_op jit(solution)/shard_map/dot_general | solution.py:437
  598.7 6.4 convolution_convert_fusion
  607.1 6.5 convolution_add_fusion.1
  639.3 7.8 %collective-permute-start.22 = (bf16[128,2048]{1,0:T(8,128)(2,1)}, bf16[128,2048]{1,0:T(8,128)(2,1)}, u32[]{:S(2)}, u32[]{:S(2)}) collective-permute-start(bf16[128,2048]{1,0:T(8,128)(2,1)} %get-tuple-element.114), channel_id=1, source_target_pairs={{0,3},{1,2},{2,1},{3,0},{4,7},{5,6},{6,5},{7,4},{8,11},{9,10},{10,... | collective-permute-start | bytes 1572872 | tf_op jit(solution)/shard_map/ppermute | solution.py:462
  665.1 10.6 %collective-permute-done.42 = bf16[128,2048]{1,0:T(8,128)(2,1)S(1)} collective-permute-done((bf16[128,2048]{1,0:T(8,128)(2,1)S(1)}, bf16[128,2048]{1,0:T(8,128)(2,1)S(1)}, u32[]{:S(2)}, u32[]{:S(2)}) %collective-permute-start.42) | collective-permute-done | bytes 524320 | tf_op jit(solution)/shard_map/ppermute | solution.py:462
  676.4 9.8 %collective-permute-done.44 = bf16[128,2048]{1,0:T(8,128)(2,1)S(1)} collective-permute-done((bf16[128,2048]{1,0:T(8,128)(2,1)S(1)}, bf16[128,2048]{1,0:T(8,128)(2,1)S(1)}, u32[]{:S(2)}, u32[]{:S(2)}) %collective-permute-start.44) | collective-permute-done | bytes 524320 | tf_op jit(solution)/shard_map/ppermute | solution.py:462
  715.8 6.6 all-to-all-done.5
  753.5 8.6 %all-to-all-done.2 = bf16[8,64,1028]{2,1,0:T(8,128)(2,1)} async-done(((bf16[8,64,1028]{2,1,0:T(8,128)(2,1)}), bf16[8,64,1028]{2,1,0:T(8,128)(2,1)}, u32[]{:S(2)}, u32[]{:S(2)}) %all-to-all-start.2) | async-done | bytes 1052704 | tf_op jit(solution)/shard_map/all_to_all | solution.py:516
  (508 shorter events, 340.3 us)
Async XLA Ops:
  18.8 107.3 %all-gather.5.cloned.1.call-start = ((), (), s32[]{:S(2)}) async-start(), calls=%async_computation.10 | async-start | bytes 5898240 | tf_op jit(solution)/shard_map/all_gather | solution.py:508
  20.6 36.6 %collective-permute-start.3 = (bf16[128,2048]{1,0:T(8,128)(2,1)}, bf16[128,2048]{1,0:T(8,128)(2,1)}, u32[]{:S(2)}, u32[]{:S(2)}) collective-permute-start(bf16[128,2048]{1,0:T(8,128)(2,1)} %get-tuple-element.77), channel_id=1, source_target_pairs={{0,2},{1,3},{2,0},{3,1},{4,6},{5,7},{6,4},{7,5},{8,10},{9,11},{10,... | collective-permute-start | bytes 1572872 | tf_op jit(solution)/shard_map/ppermute | solution.py:462
  22.6 24.0 %collective-permute-start.1 = (bf16[128,2048]{1,0:T(8,128)(2,1)}, bf16[128,2048]{1,0:T(8,128)(2,1)}, u32[]{:S(2)}, u32[]{:S(2)}) collective-permute-start(bf16[128,2048]{1,0:T(8,128)(2,1)} %get-tuple-element.77), channel_id=1, source_target_pairs={{0,1},{1,0},{2,3},{3,2},{4,5},{5,4},{6,7},{7,6},{8,9},{9,8},{10,11... | collective-permute-start | bytes 1572872 | tf_op jit(solution)/shard_map/ppermute | solution.py:462
  24.0 34.2 %collective-permute-start = (bf16[128,2048]{1,0:T(8,128)(2,1)}, bf16[128,2048]{1,0:T(8,128)(2,1)}, u32[]{:S(2)}, u32[]{:S(2)}) collective-permute-start(bf16[128,2048]{1,0:T(8,128)(2,1)} %get-tuple-element.77), channel_id=1, source_target_pairs={{0,4},{4,0},{1,5},{5,1},{2,6},{6,2},{3,7},{7,3},{8,12},{12,8},{9,1... | collective-permute-start | bytes 1572872 | tf_op jit(solution)/shard_map/ppermute | solution.py:458
  24.0 34.1 %collective-permute-start.5 = (bf16[128,2048]{1,0:T(8,128)(2,1)}, bf16[128,2048]{1,0:T(8,128)(2,1)}, u32[]{:S(2)}, u32[]{:S(2)}) collective-permute-start(bf16[128,2048]{1,0:T(8,128)(2,1)} %get-tuple-element.77), channel_id=1, source_target_pairs={{0,3},{1,2},{2,1},{3,0},{4,7},{5,6},{6,5},{7,4},{8,11},{9,10},{10,... | collective-permute-start | bytes 1572872 | tf_op jit(solution)/shard_map/ppermute | solution.py:462
  36.2 171.2 %all-gather.7.cloned.1.call-start = ((), (), s32[]{:S(2)}) async-start(), calls=%async_computation.11 | async-start | bytes 5242880 | tf_op jit(solution)/shard_map/all_gather | solution.py:508
  112.4 207.4 %all-gather.9.cloned.1.call-start = ((), (), s32[]{:S(2)}) async-start(), calls=%async_computation.12 | async-start | bytes 5898240 | tf_op jit(solution)/shard_map/all_gather | solution.py:508
  119.8 258.5 %all-gather.11.cloned.1.call-start = ((), (), s32[]{:S(2)}) async-start(), calls=%async_computation.13 | async-start | bytes 5242880 | tf_op jit(solution)/shard_map/all_gather | solution.py:508
  223.4 29.0 %collective-permute-start.8 = (bf16[512,2048]{1,0:T(8,128)(2,1)}, bf16[512,2048]{1,0:T(8,128)(2,1)}, u32[]{:S(2)}, u32[]{:S(2)}) collective-permute-start(bf16[512,2048]{1,0:T(8,128)(2,1)} %slice.471), channel_id=1, source_target_pairs={{0,4},{4,0},{1,5},{5,1},{2,6},{6,2},{3,7},{7,3},{8,12},{12,8},{9,1... | collective-permute-start | bytes 6291464 | tf_op jit(solution)/shard_map/ppermute | solution.py:458
  225.8 24.2 %collective-permute-start.23 = (bf16[128,2048]{1,0:T(8,128)(2,1)S(1)}, bf16[128,2048]{1,0:T(8,128)(2,1)}, u32[]{:S(2)}, u32[]{:S(2)}) collective-permute-start(bf16[128,2048]{1,0:T(8,128)(2,1)S(1)} %bitcast.198), channel_id=1, source_target_pairs={{0,1},{1,0},{2,3},{3,2},{4,5},{5,4},{6,7},{7,6},{8,9},{9,8},{10,11... | collective-permute-start | bytes 1572872 | tf_op jit(solution)/shard_map/ppermute | solution.py:462
  226.3 24.8 %collective-permute-start.24 = (bf16[128,2048]{1,0:T(8,128)(2,1)S(1)}, bf16[128,2048]{1,0:T(8,128)(2,1)S(1)}, u32[]{:S(2)}, u32[]{:S(2)}) collective-permute-start(bf16[128,2048]{1,0:T(8,128)(2,1)S(1)} %bitcast.199), channel_id=1, source_target_pairs={{0,2},{1,3},{2,0},{3,1},{4,6},{5,7},{6,4},{7,5},{8,10},{9,11},{10,... | collective-permute-start | bytes 1572872 | tf_op jit(solution)/shard_map/ppermute | solution.py:462
  226.9 31.4 %collective-permute-start.26 = (bf16[128,2048]{1,0:T(8,128)(2,1)S(1)}, bf16[128,2048]{1,0:T(8,128)(2,1)}, u32[]{:S(2)}, u32[]{:S(2)}) collective-permute-start(bf16[128,2048]{1,0:T(8,128)(2,1)S(1)} %bitcast.200), channel_id=1, source_target_pairs={{0,4},{4,0},{1,5},{5,1},{2,6},{6,2},{3,7},{7,3},{8,12},{12,8},{9,1... | collective-permute-start | bytes 1572872 | tf_op jit(solution)/shard_map/ppermute | solution.py:458
  239.2 52.8 %collective-permute-start.29 = (bf16[128,2048]{1,0:T(8,128)(2,1)}, bf16[128,2048]{1,0:T(8,128)(2,1)}, u32[]{:S(2)}, u32[]{:S(2)}) collective-permute-start(bf16[128,2048]{1,0:T(8,128)(2,1)} %collective-permute-done.25), channel_id=1, source_target_pairs={{0,4},{4,0},{1,5},{5,1},{2,6},{6,2},{3,7},{7,3},{8,12},{12,8},{9,1... | collective-permute-start | bytes 1572872 | tf_op jit(solution)/shard_map/ppermute | solution.py:458
  257.7 24.2 %collective-permute-start.11 = (bf16[128,2048]{1,0:T(8,128)(2,1)S(1)}, bf16[128,2048]{1,0:T(8,128)(2,1)S(1)}, u32[]{:S(2)}, u32[]{:S(2)}) collective-permute-start(bf16[128,2048]{1,0:T(8,128)(2,1)S(1)} %get-tuple-element.86), channel_id=1, source_target_pairs={{0,3},{1,2},{2,1},{3,0},{4,7},{5,6},{6,5},{7,4},{8,11},{9,10},{10,... | collective-permute-start | bytes 1572872 | tf_op jit(solution)/shard_map/ppermute | solution.py:462
  258.3 25.0 %collective-permute-start.10 = (bf16[128,2048]{1,0:T(8,128)(2,1)S(1)}, bf16[128,2048]{1,0:T(8,128)(2,1)S(1)}, u32[]{:S(2)}, u32[]{:S(2)}) collective-permute-start(bf16[128,2048]{1,0:T(8,128)(2,1)S(1)} %get-tuple-element.87), channel_id=1, source_target_pairs={{0,2},{1,3},{2,0},{3,1},{4,6},{5,7},{6,4},{7,5},{8,10},{9,11},{10,... | collective-permute-start | bytes 1572872 | tf_op jit(solution)/shard_map/ppermute | solution.py:462
  260.9 29.1 %collective-permute-start.28 = (bf16[128,2048]{1,0:T(8,128)(2,1)}, bf16[128,2048]{1,0:T(8,128)(2,1)}, u32[]{:S(2)}, u32[]{:S(2)}) collective-permute-start(bf16[128,2048]{1,0:T(8,128)(2,1)} %copy-done.52), channel_id=1, source_target_pairs={{0,4},{4,0},{1,5},{5,1},{2,6},{6,2},{3,7},{7,3},{8,12},{12,8},{9,1... | collective-permute-start | bytes 1572872 | tf_op jit(solution)/shard_map/ppermute | solution.py:458
  287.3 22.9 %collective-permute-start.13 = (bf16[128,2048]{1,0:T(8,128)(2,1)S(1)}, bf16[128,2048]{1,0:T(8,128)(2,1)}, u32[]{:S(2)}, u32[]{:S(2)}) collective-permute-start(bf16[128,2048]{1,0:T(8,128)(2,1)S(1)} %get-tuple-element.73), channel_id=1, source_target_pairs={{0,2},{1,3},{2,0},{3,1},{4,6},{5,7},{6,4},{7,5},{8,10},{9,11},{10,... | collective-permute-start | bytes 1572872 | tf_op jit(solution)/shard_map/ppermute | solution.py:462
  290.0 181.2 %reduce-scatter.5.cloned.1.call-start = ((), (), s32[]{:S(2)}) async-start(), calls=%async_computation.14 | async-start | bytes 5898240 | tf_op jit(solution)/shard_map/reduce_scatter | solution.py:512
  340.3 198.2 %reduce-scatter.7.cloned.1.call-start = ((), (), s32[]{:S(2)}) async-start(), calls=%async_computation.15 | async-start | bytes 4669440 | tf_op jit(solution)/shard_map/reduce_scatter | solution.py:512
  405.7 24.7 %collective-permute-start.33 = (bf16[128,2048]{1,0:T(8,128)(2,1)S(1)}, bf16[128,2048]{1,0:T(8,128)(2,1)S(1)}, u32[]{:S(2)}, u32[]{:S(2)}) collective-permute-start(bf16[128,2048]{1,0:T(8,128)(2,1)S(1)} %get-tuple-element.111), channel_id=1, source_target_pairs={{0,3},{1,2},{2,1},{3,0},{4,7},{5,6},{6,5},{7,4},{8,11},{9,10},{10,... | collective-permute-start | bytes 1572872 | tf_op jit(solution)/shard_map/ppermute | solution.py:462
  407.1 24.6 %collective-permute-start.32 = (bf16[128,2048]{1,0:T(8,128)(2,1)S(1)}, bf16[128,2048]{1,0:T(8,128)(2,1)S(1)}, u32[]{:S(2)}, u32[]{:S(2)}) collective-permute-start(bf16[128,2048]{1,0:T(8,128)(2,1)S(1)} %get-tuple-element.112), channel_id=1, source_target_pairs={{0,2},{1,3},{2,0},{3,1},{4,6},{5,7},{6,4},{7,5},{8,10},{9,11},{10,... | collective-permute-start | bytes 1572872 | tf_op jit(solution)/shard_map/ppermute | solution.py:462
  440.3 23.4 %collective-permute-start.37 = (bf16[128,2048]{1,0:T(8,128)(2,1)}, bf16[128,2048]{1,0:T(8,128)(2,1)S(1)}, u32[]{:S(2)}, u32[]{:S(2)}) collective-permute-start(bf16[128,2048]{1,0:T(8,128)(2,1)} %get-tuple-element.66), channel_id=1, source_target_pairs={{0,2},{1,3},{2,0},{3,1},{4,6},{5,7},{6,4},{7,5},{8,10},{9,11},{10,... | collective-permute-start | bytes 1572872 | tf_op jit(solution)/shard_map/ppermute | solution.py:462
  442.4 24.0 %collective-permute-start.39 = (bf16[128,2048]{1,0:T(8,128)(2,1)}, bf16[128,2048]{1,0:T(8,128)(2,1)S(1)}, u32[]{:S(2)}, u32[]{:S(2)}) collective-permute-start(bf16[128,2048]{1,0:T(8,128)(2,1)} %get-tuple-element.66), channel_id=1, source_target_pairs={{0,3},{1,2},{2,1},{3,0},{4,7},{5,6},{6,5},{7,4},{8,11},{9,10},{10,... | collective-permute-start | bytes 1572872 | tf_op jit(solution)/shard_map/ppermute | solution.py:462
  471.2 148.3 %reduce-scatter.9.cloned.1.call-start = ((), (), s32[]{:S(2)}) async-start(), calls=%async_computation.16 | async-start | bytes 5242880 | tf_op jit(solution)/shard_map/reduce_scatter | solution.py:512
  538.5 198.4 %reduce-scatter.11.cloned.1.call-start = ((), (), s32[]{:S(2)}) async-start(), calls=%async_computation.17 | async-start | bytes 5283840 | tf_op jit(solution)/shard_map/reduce_scatter | solution.py:512
  618.7 38.4 %collective-permute-start.41 = (bf16[512,2048]{1,0:T(8,128)(2,1)}, bf16[512,2048]{1,0:T(8,128)(2,1)}, u32[]{:S(2)}, u32[]{:S(2)}) collective-permute-start(bf16[512,2048]{1,0:T(8,128)(2,1)} %slice.468), channel_id=1, source_target_pairs={{0,4},{4,0},{1,5},{5,1},{2,6},{6,2},{3,7},{7,3},{8,12},{12,8},{9,1... | collective-permute-start | bytes 6291464 | tf_op jit(solution)/shard_map/ppermute | solution.py:458
  623.5 86.0 %collective-permute-start.20 = (bf16[128,2048]{1,0:T(8,128)(2,1)}, bf16[128,2048]{1,0:T(8,128)(2,1)}, u32[]{:S(2)}, u32[]{:S(2)}) collective-permute-start(bf16[128,2048]{1,0:T(8,128)(2,1)} %get-tuple-element.113), channel_id=1, source_target_pairs={{0,1},{1,0},{2,3},{3,2},{4,5},{5,4},{6,7},{7,6},{8,9},{9,8},{10,11... | collective-permute-start | bytes 1572872 | tf_op jit(solution)/shard_map/ppermute | solution.py:462
  625.4 66.7 %all-to-all-start.4 = ((bf16[8,64,1152]{2,1,0:T(8,128)(2,1)}), bf16[8,64,1152]{2,1,0:T(8,128)(2,1)S(1)}, u32[]{:S(2)}, u32[]{:S(2)}) async-start(bf16[8,64,1152]{2,1,0:T(8,128)(2,1)} %bitcast.57), calls=%async_computation.8 | async-start | bytes 2359296 | tf_op jit(solution)/shard_map/all_to_all | solution.py:516
  639.3 70.2 %collective-permute-start.22 = (bf16[128,2048]{1,0:T(8,128)(2,1)}, bf16[128,2048]{1,0:T(8,128)(2,1)}, u32[]{:S(2)}, u32[]{:S(2)}) collective-permute-start(bf16[128,2048]{1,0:T(8,128)(2,1)} %get-tuple-element.114), channel_id=1, source_target_pairs={{0,3},{1,2},{2,1},{3,0},{4,7},{5,6},{6,5},{7,4},{8,11},{9,10},{10,... | collective-permute-start | bytes 1572872 | tf_op jit(solution)/shard_map/ppermute | solution.py:462
  661.6 24.6 %collective-permute-start.44 = (bf16[128,2048]{1,0:T(8,128)(2,1)S(1)}, bf16[128,2048]{1,0:T(8,128)(2,1)S(1)}, u32[]{:S(2)}, u32[]{:S(2)}) collective-permute-start(bf16[128,2048]{1,0:T(8,128)(2,1)S(1)} %get-tuple-element.83), channel_id=1, source_target_pairs={{0,3},{1,2},{2,1},{3,0},{4,7},{5,6},{6,5},{7,4},{8,11},{9,10},{10,... | collective-permute-start | bytes 1572872 | tf_op jit(solution)/shard_map/ppermute | solution.py:462
  663.0 25.8 %collective-permute-start.43 = (bf16[128,2048]{1,0:T(8,128)(2,1)S(1)}, bf16[128,2048]{1,0:T(8,128)(2,1)S(1)}, u32[]{:S(2)}, u32[]{:S(2)}) collective-permute-start(bf16[128,2048]{1,0:T(8,128)(2,1)S(1)} %get-tuple-element.84), channel_id=1, source_target_pairs={{0,2},{1,3},{2,0},{3,1},{4,6},{5,7},{6,4},{7,5},{8,10},{9,11},{10,... | collective-permute-start | bytes 1572872 | tf_op jit(solution)/shard_map/ppermute | solution.py:462
  675.8 33.8 %collective-permute-start.21 = (bf16[128,2048]{1,0:T(8,128)(2,1)}, bf16[128,2048]{1,0:T(8,128)(2,1)}, u32[]{:S(2)}, u32[]{:S(2)}) collective-permute-start(bf16[128,2048]{1,0:T(8,128)(2,1)} %get-tuple-element.115), channel_id=1, source_target_pairs={{0,2},{1,3},{2,0},{3,1},{4,6},{5,7},{6,4},{7,5},{8,10},{9,11},{10,... | collective-permute-start | bytes 1572872 | tf_op jit(solution)/shard_map/ppermute | solution.py:462
  (131 other events, 1817.4 us)
Sparse Core Ops, SparseCore 0:
  36.3 89.6 all-gather.4
  128.2 79.2 all-gather.6
  209.0 87.9 all-gather.8
  299.0 79.2 all-gather.10
  380.4 83.7 reduce-scatter.4
  471.3 67.1 reduce-scatter.6
  540.8 78.5 reduce-scatter.8
  621.7 77.7 reduce-scatter.10

commit v3 on v2

--- a/solution.py
+++ b/solution.py
@@ -58,20 +58,22 @@
 
 
 def solved(negated, row, col):
-    diagonal = jnp.where((row >> 4) == (col >> 4), negated, 0.0)
-    inverse = (row == col).astype(F32) + diagonal
-    power = diagonal
+    same = (row >> 4) == (col >> 4)
+    power = [jnp.where(same, n, 0.0) for n in negated]
+    inverse = [(row == col).astype(F32) + p for p in power]
     for _ in range(3):
-        parts = halves(power)
-        power = product(parts, parts)
-        inverse = inverse + product(halves(inverse), halves(power))
+        parts = [halves(p) for p in power]
+        power = [product(p, p) for p in parts]
+        parts = [(halves(i), halves(p)) for i, p in zip(inverse, power)]
+        inverse = [i + product(*p) for i, p in zip(inverse, parts)]
     for bits in (4, 5, 6):
         beside = jnp.logical_and(
             (row >> (bits + 1)) == (col >> (bits + 1)), (row >> bits) != (col >> bits)
         )
-        off = jnp.where(beside, negated, 0.0)
-        parts = halves(inverse)
-        inverse = inverse + product(parts, halves(product(halves(off), parts)))
+        off = [halves(jnp.where(beside, n, 0.0)) for n in negated]
+        parts = [halves(i) for i in inverse]
+        off = [halves(product(o, p)) for o, p in zip(off, parts)]
+        inverse = [i + product(p, o) for i, p, o in zip(inverse, parts, off)]
     return inverse
 
 
@@ -130,38 +132,53 @@
 
     state_ref[0] = state[...]
     taps = taps_ref[...]
+    facts, query, keys, values, spans = [], [], [], [], []
     for r in range(2):
         aux = aux_ref[r]
         ext[r, 8:, :] = x_ref[r].astype(F32)
         conv = convolved(lambda lag: ext[r, 8 - lag : 8 - lag + BLOCK, :], taps, aux, heads)
         act = conv * jax.nn.sigmoid(conv)
         ext[r, :8, :] = ext[r, BLOCK:, :]
-        facts = decays(aux, row, col, heads)
+        facts += decays(aux, row, col, heads)
         for h in range(heads):
-            f = facts[h]
-            at = r * heads + h
-            vs = slice(h * VALUE, (h + 1) * VALUE)
-            query = (unit(act[:, h * KEY : (h + 1) * KEY])[0] * KEY ** (-0.5)).astype(LOW)
-            keys = unit(act[:, hk + h * KEY : hk + (h + 1) * KEY])[0].astype(LOW)
-            values = act[:, 2 * hk + h * VALUE : 2 * hk + (h + 1) * VALUE].astype(LOW)
-            pair = f["pair"]
-            similar = product((keys,), (keys,), 1, 1)
-            negated = jnp.where(row > col, -(f["beta_col"] * pair * similar), 0.0)
-            inverse = solved(negated, row, col)
-            inv_ref[0, at] = inverse
-            scaled = inverse * f["beta_row"]
-            old = state[at]
-            old_parts = halves(old)
-            weights = halves(product(halves(scaled * f["decay_row"]), (keys,)))
-            updates = product(halves(scaled), (values,)) - product(weights, old_parts)
-            upd_ref[r, :, vs] = updates
-            seen = product((query,), (keys,), 1, 1) * pair
-            mixed_ref[r, :, vs] = f["decay_col"] * product((query,), old_parts) + product(
-                halves(seen), halves(updates)
-            )
-            state[at] = f["decay_last"] * old + product(
-                (keys,), halves(f["last"] * updates), 0, 0
-            )
+            spans.append((r, slice(h * VALUE, (h + 1) * VALUE)))
+            query.append(
+                (unit(act[:, h * KEY : (h + 1) * KEY])[0] * KEY ** (-0.5)).astype(LOW)
+            )
+            keys.append(unit(act[:, hk + h * KEY : hk + (h + 1) * KEY])[0].astype(LOW))
+            values.append(act[:, 2 * hk + h * VALUE : 2 * hk + (h + 1) * VALUE].astype(LOW))
+    every = range(2 * heads)
+    similar = [product((k,), (k,), 1, 1) for k in keys]
+    inverse = solved(
+        [
+            jnp.where(row > col, -(f["beta_col"] * f["pair"] * s), 0.0)
+            for f, s in zip(facts, similar)
+        ],
+        row,
+        col,
+    )
+    seen = [product((q,), (k,), 1, 1) * f["pair"] for q, k, f in zip(query, keys, facts)]
+    old = [state[at] for at in every]
+    old_parts = [halves(o) for o in old]
+    asked = [product((q,), o) for q, o in zip(query, old_parts)]
+    scaled = [i * f["beta_row"] for i, f in zip(inverse, facts)]
+    weights = [
+        halves(product(halves(s * f["decay_row"]), (k,))) for s, f, k in zip(scaled, facts, keys)
+    ]
+    updates = [product(halves(s), (v,)) for s, v in zip(scaled, values)]
+    updates = [u - product(w, o) for u, w, o in zip(updates, weights, old_parts)]
+    for at in every:
+        f, (r, vs) = facts[at], spans[at]
+        inv_ref[0, at] = inverse[at]
+        upd_ref[r, :, vs] = updates[at]
+        state[at] = f["decay_last"] * old[at] + product(
+            (keys[at],), halves(f["last"] * updates[at]), 0, 0
+        )
+    for at in every:
+        r, vs = spans[at]
+        mixed_ref[r, :, vs] = facts[at]["decay_col"] * asked[at] + product(
+            halves(seen[at]), halves(updates[at])
+        )
 
     @pl.when(step == pl.num_programs(0) - 1)
     def _():
@@ -205,7 +222,7 @@
             dimension_semantics=("arbitrary",), vmem_limit_bytes=48 * 1024 * 1024
         ),
         cost_estimate=pl.CostEstimate(
-            flops=40_000_000_000, bytes_accessed=12_000_000, transcendentals=2_000_000
+            flops=1_000_000, bytes_accessed=1_000_000, transcendentals=0
         ),
         name="mix_forward",
     )(x, taps, aux)
@@ -222,6 +239,7 @@
     halo_ref,
     taps_ref,
     aux_ref,
+    factor_ref,
     gate_ref,
     gain_ref,
     mixed_ref,
@@ -229,18 +247,18 @@
     upd_ref,
     state_ref,
     d_branch_ref,
-    d_x_ref,
-    d_gate_ref,
-    d_aux_ref,
+    d_all_ref,
     d_taps_ref,
     d_gain_ref,
+    d_rate_ref,
     ext,
     d_ext,
     d_state,
 ):
     step = pl.program_id(0)
     first_block = step == pl.num_programs(0) - 1
-    hk = heads * KEY
+    hk, hv = heads * KEY, heads * VALUE
+    chan = 2 * hk + hv
     row, col = places()
     lane = lax.broadcasted_iota(jnp.int32, (BLOCK, 128), 1)
     position = lax.broadcasted_iota(jnp.int32, (BLOCK, 1), 0)
@@ -251,6 +269,7 @@
         d_ext[:, BLOCK:, :] = jnp.zeros_like(d_ext[:, BLOCK:, :])
         d_taps_ref[...] = jnp.zeros_like(d_taps_ref)
         d_gain_ref[...] = jnp.zeros_like(d_gain_ref)
+        d_rate_ref[...] = jnp.zeros_like(d_rate_ref)
 
     taps = taps_ref[...]
     gain = gain_ref[...]
@@ -285,7 +304,9 @@
             gate_logistic, gate_slope = slope(gate)
             d_scaled = d_branch * (gate * gate_logistic)
             d_gain_ref[...] += jnp.sum(d_scaled * normed, axis=0, keepdims=True)
-            d_gate_ref[r, :, vs] = (d_branch * normed * gain * gate_slope).astype(LOW)
+            d_all_ref[r, :, chan + h * VALUE : chan + (h + 1) * VALUE] = (
+                d_branch * normed * gain * gate_slope
+            ).astype(LOW)
             d_normed = d_scaled * gain
             d_out = factor * (
                 d_normed - normed * jnp.mean(d_normed * normed, axis=1, keepdims=True)
@@ -362,7 +383,10 @@
         d_aux = product((upper,), thirds(columns - turned))
         for h in range(heads):
             d_aux = jnp.where(lane == heads + h, d_betas[h], d_aux)
-        d_aux_ref[r] = d_aux
+        d_rate = d_aux * factor_ref[r]
+        d_all_ref[r, :, chan + hv :] = d_rate.astype(LOW)
+        d_rate_ref[0:1, :] += jnp.sum(d_aux * aux, axis=0, keepdims=True)
+        d_rate_ref[1:2, :] += jnp.sum(d_rate, axis=0, keepdims=True)
         d_conv = jnp.concatenate(d_query_raw + d_key_raw + d_value_raw, axis=1) * conv_slope
         d_ext_sum = taps[CONV - 1 : CONV, :] * d_conv
         d_taps_ref[CONV - 1 : CONV, :] += jnp.sum(d_conv * shifted(0), axis=0, keepdims=True)
@@ -377,10 +401,12 @@
                 d_ext_sum + taps[CONV - 1 - lag : CONV - lag, :] * d_ext[slot, lag : lag + BLOCK, :]
             )
             d_ext[slot, BLOCK:, :] = d_ext[slot, :8, :]
-        d_x_ref[r] = d_ext_sum.astype(LOW)
-
-
-def mix_back(x, taps, aux, gate, gain, mixed, inverses, updates, states, d_branch, heads):
+        d_all_ref[r, :, :chan] = d_ext_sum.astype(LOW)
+
+
+def mix_back(
+    x, taps, aux, factor, gate, gain, mixed, inverses, updates, states, d_branch, heads
+):
     length, chan = x.shape[1:]
     count = length // BLOCK
     hv = heads * VALUE
@@ -396,6 +422,7 @@
             pl.BlockSpec((2, 16, chan), halo),
             pl.BlockSpec((CONV, chan), fixed),
             pl.BlockSpec((2, BLOCK, 128), here),
+            pl.BlockSpec((2, BLOCK, 128), here),
             pl.BlockSpec((2, BLOCK, hv), here),
             pl.BlockSpec((1, VALUE), fixed),
             pl.BlockSpec((2, BLOCK, hv), here),
@@ -405,18 +432,16 @@
             pl.BlockSpec((2, BLOCK, hv), here),
         ],
         out_specs=[
-            pl.BlockSpec((2, BLOCK, chan), here),
-            pl.BlockSpec((2, BLOCK, hv), here),
-            pl.BlockSpec((2, BLOCK, 128), here),
+            pl.BlockSpec((2, BLOCK, chan + hv + 128), here),
             pl.BlockSpec((CONV, chan), fixed),
             pl.BlockSpec((1, VALUE), fixed),
+            pl.BlockSpec((8, 128), fixed),
         ],
         out_shape=[
-            jax.ShapeDtypeStruct((2, length, chan), LOW),
-            jax.ShapeDtypeStruct((2, length, hv), LOW),
-            jax.ShapeDtypeStruct((2, length, 128), F32),
+            jax.ShapeDtypeStruct((2, length, chan + hv + 128), LOW),
             jax.ShapeDtypeStruct((CONV, chan), F32),
             jax.ShapeDtypeStruct((1, VALUE), F32),
+            jax.ShapeDtypeStruct((8, 128), F32),
         ],
         scratch_shapes=[
             pltpu.VMEM((2, BLOCK + 8, chan), F32),
@@ -427,10 +452,10 @@
             dimension_semantics=("arbitrary",), vmem_limit_bytes=48 * 1024 * 1024
         ),
         cost_estimate=pl.CostEstimate(
-            flops=60_000_000_000, bytes_accessed=20_000_000, transcendentals=4_000_000
+            flops=1_000_000, bytes_accessed=1_000_000, transcendentals=0
         ),
         name="mix_backward",
-    )(x, x, taps, aux, gate, gain, mixed, inverses, updates, states, d_branch)
+    )(x, x, taps, aux, factor, gate, gain, mixed, inverses, updates, states, d_branch)
 
 
 def contract_rows(left, right):
@@ -462,25 +487,36 @@
     return lax.ppermute(x, axis, [(i, i ^ distance) for i in range(lax.axis_size(axis))])
 
 
-def plane_gather(x, ordered):
+def plane_blocks(x):
+    blocks = [x] + [from_peer(x, "seq", k) for k in range(1, lax.axis_size("seq"))]
+    return blocks + [swap_core(b) for b in blocks]
+
+
+def plane_gather(x):
     size, me = lax.axis_size("seq"), lax.axis_index("seq")
-    blocks = [x] + [from_peer(x, "seq", k) for k in range(1, size)]
-    others = [swap_core(b) for b in blocks]
-    if not ordered:
-        return jnp.concatenate(blocks + others, axis=0)
     tokens = x.shape[0]
     whole = jnp.zeros((2 * size * tokens,) + x.shape[1:], x.dtype)
-    for k in range(size):
-        whole = lax.dynamic_update_slice(whole, blocks[k], ((me ^ k) * tokens, 0))
-        whole = lax.dynamic_update_slice(whole, others[k], ((size + (me ^ k)) * tokens, 0))
+    for k, block in enumerate(plane_blocks(x)):
+        at = (k // size * size + (me ^ (k % size))) * tokens
+        whole = lax.dynamic_update_slice(whole, block, (at, 0))
     return whole
 
 
-def plane_sum(x, ordered):
+def product_rows(left, right, first):
+    half = left[0].shape[0] // 2
+    at = slice(0, half) if first else slice(half, None)
+    return sum(contract_rows(a[at], b) for a, b in zip(left, right))
+
+
+def row_sum(left, right, far=None, kind=jnp.bfloat16):
+    if far is None:
+        far = product_rows(left, right, False).astype(kind)
+    return product_rows(left, right, True) + swap_core(far).astype(jnp.float32)
+
+
+def block_sum(row, ordered, kind=jnp.bfloat16):
     size, me = lax.axis_size("seq"), lax.axis_index("seq")
-    half = x.shape[0] // 2
-    tokens = half // size
-    row = x[:half] + swap_core(x[half:].astype(jnp.bfloat16)).astype(jnp.float32)
+    tokens = row.shape[0] // size
 
     def block(k):
         at = (me ^ k) * tokens if ordered else k * tokens
@@ -488,8 +524,17 @@
 
     total = block(0)
     for k in range(1, size):
-        total = total + from_peer(block(k).astype(jnp.bfloat16), "seq", k).astype(jnp.float32)
+        total = total + from_peer(block(k).astype(kind), "seq", k).astype(jnp.float32)
     return total
+
+
+def laid_out(x, axis):
+    size, me = lax.axis_size(axis), lax.axis_index(axis)
+    whole = jnp.zeros((size,) + x.shape, x.dtype)
+    for k in range(size):
+        block = from_peer(x, axis, k) if k else x
+        whole = lax.dynamic_update_index_in_dim(whole, block, me ^ k, 0)
+    return whole
 
 
 def by_holder(parts, split):
@@ -517,12 +562,19 @@
     return jnp.swapaxes(blocks, 0, 1).astype(jnp.float32)
 
 
-def butterfly(x, axis):
-    distance = 1
-    while distance < lax.axis_size(axis):
-        x = x + from_peer(x, axis, distance)
-        distance *= 2
-    return x
+def after(x, *done):
+    return lax.optimization_barrier((x,) + done)[0]
+
+
+def axis_sum(x, axis):
+    blocks = [x] + [from_peer(x, axis, k) for k in range(1, lax.axis_size(axis))]
+    while len(blocks) > 1:
+        blocks = [p + q for p, q in zip(blocks[::2], blocks[1::2])]
+    return blocks[0]
+
+
+def all_sum(x):
+    return axis_sum(axis_sum(axis_sum(x, "seq"), "core"), "z")
 
 
 def on_device(
@@ -544,6 +596,7 @@
     own = hidden_in.shape[1]
     width = hidden_in.shape[2]
     seq = lax.axis_size("seq")
+    planes = lax.axis_size("z")
     split = 2 * seq
     length = own * seq
     tokens = 2 * length
@@ -552,50 +605,59 @@
     chan = 2 * hk + hv
     me = lax.axis_index("seq")
     core = lax.axis_index("core")
+    plane = lax.axis_index("z")
     here = core * seq + me
     rows = proj_weight.shape[0]
 
     def own_columns(whole, count):
         return lax.dynamic_slice_in_dim(whole, here * count, count, whole.ndim - 1)
 
-    mix_in = plane_exchange(
-        by_holder(
-            [
-                proj_weight[:, :HK],
-                proj_weight[:, HK : 2 * HK],
-                proj_weight[:, 2 * HK : 2 * HK + HV],
-                rate_weight[:, :HEADS],
-                rate_weight[:, HEADS:],
-            ],
-            split,
-        )
+    mix_in = by_holder(
+        [
+            proj_weight[:, :HK],
+            proj_weight[:, HK : 2 * HK],
+            proj_weight[:, 2 * HK : 2 * HK + HV],
+        ],
+        split,
+    )
+    others, hidden_in, mix_in = lax.optimization_barrier(
+        ((proj_weight[:, 2 * HK + HV :], out_weight, gate_up_weight, down_weight), hidden_in, mix_in)
+    )
+    mix_in = lax.all_gather(mix_in, "z", axis=0)
+    others = by_holder(
+        [
+            others[0],
+            others[1],
+            others[2][:, :FF],
+            others[2][:, FF:],
+            others[3],
+            rate_weight[:, :HEADS],
+            rate_weight[:, HEADS:],
+        ],
+        split,
     )
     x = hidden_in[0].astype(jnp.float32)
     scale = lax.rsqrt(jnp.mean(x * x, axis=1, keepdims=True) + EPS)
     normed = x * scale
-    first_in = plane_gather((normed * norm_gain).astype(jnp.bfloat16), True)
-    others = by_holder(
-        [
-            proj_weight[:, 2 * HK + HV :],
-            out_weight,
-            gate_up_weight[:, :FF],
-            gate_up_weight[:, FF:],
-            down_weight,
-        ],
-        split,
-    )
-    first_in, others = lax.optimization_barrier((first_in, others))
-    others = plane_exchange(others)
-    mix_in = along_z(mix_in)
+    first_in = plane_gather((normed * norm_gain).astype(jnp.bfloat16))
+    others = plane_exchange(after(others, first_in))
+    at = 2 * hv + 3 * ff
+    rate_rows = others[:, at : at + 2 * heads].T
+    rate_in = jnp.zeros((2 * heads, width), jnp.bfloat16)
+    for k in range(planes):
+        block = from_peer(rate_rows, "z", k) if k else rate_rows
+        rate_in = lax.dynamic_update_slice_in_dim(
+            rate_in, block, (plane ^ k) * rows * split, 1
+        )
+    cut = ff * 3 // 4 // 128 * 128
+    ffn = [
+        jnp.concatenate([others[:, 2 * hv + i * ff : 2 * hv + (i + 1) * ff][:, p] for i in range(3)], axis=1)
+        for p in (slice(0, cut), slice(cut, ff))
+    ]
+    mix_in = lax.all_to_all(jnp.swapaxes(mix_in, 0, 1), PLANE, 0, 0)
+    mix_in = jnp.swapaxes(mix_in, 0, 1).reshape(width, chan)
     gate_out = along_z(others[:, : 2 * hv])
     gate_in, out_cols = gate_out[:, :hv], gate_out[:, hv:]
-    cut = -(-ff // 256) * 128
-    parts = [slice(0, cut), slice(cut, ff)]
-    gates = [others[:, 2 * hv :][:, p] for p in parts]
-    ups = [others[:, 2 * hv + ff :][:, p] for p in parts]
-    downs = [others[:, 2 * hv + 2 * ff :][:, p] for p in parts]
-    ffn = [along_z(jnp.concatenate(w, axis=1)) for w in zip(gates, ups, downs)]
-    cot = plane_gather(grad_out[0], False)
 
     bounds = jnp.concatenate([boundary, swap_core(boundary)], axis=0)
     positions = jnp.arange(length)
@@ -617,70 +679,96 @@
     )
     own_rate, own_bias = own_columns(log_rate, heads), own_columns(rate_bias, heads)
 
-    conv_in = jnp.dot(first_in, mix_in[:, :chan], preferred_element_type=jnp.float32)
-    conv_in = conv_in.astype(jnp.bfloat16).reshape(2, length, chan)
-    rates = jnp.dot(first_in, mix_in[:, chan:], preferred_element_type=jnp.float32)
+    rates = contract_rows(first_in, rate_in)
     rates = rates.reshape(2, length, 2 * heads)
     rate_input = rates[:, :, :heads] + own_bias
-    decay_log = -jnp.exp(own_rate) * jax.nn.softplus(rate_input)
+    speed = -jnp.exp(own_rate)
+    decay_log = speed * jax.nn.softplus(rate_input)
     beta = jax.nn.sigmoid(rates[:, :, heads:])
     aux = jnp.concatenate([decay_log, beta] + [s[:, :, None] for s in [start] + keeps], axis=2)
     aux = jnp.pad(aux, ((0, 0), (0, 0), (0, 128 - aux.shape[2])))
+    factor = jnp.concatenate([speed * jax.nn.sigmoid(rate_input), beta * (1.0 - beta)], axis=2)
+    factor = jnp.pad(factor, ((0, 0), (0, 0), (0, 128 - 2 * heads)))
+    mix_in, aux, factor, grad_out = lax.optimization_barrier((mix_in, aux, factor, grad_out))
+    cot = plane_blocks(grad_out[0])
+    conv_in = jnp.dot(first_in, mix_in, preferred_element_type=jnp.float32)
+    conv_in = conv_in.astype(jnp.bfloat16).reshape(2, length, chan)
     mixed, inverses, updates, states, final = mix(conv_in, taps, aux, heads)
 
+    mixed, gate_in, ffn = lax.optimization_barrier((mixed, gate_in, ffn))
+    ffn = [along_z(w) for w in ffn]
     gate = jnp.dot(first_in, gate_in, preferred_element_type=jnp.float32).reshape(2, length, hv)
     branch = []
     for h in range(heads):
         part = mixed[:, :, h * VALUE : (h + 1) * VALUE]
-        factor = lax.rsqrt(jnp.mean(part * part, axis=2, keepdims=True) + EPS)
+        norm = lax.rsqrt(jnp.mean(part * part, axis=2, keepdims=True) + EPS)
         branch.append(
-            part * factor * head_gain * jax.nn.silu(gate[:, :, h * VALUE : (h + 1) * VALUE])
+            part * norm * head_gain * jax.nn.silu(gate[:, :, h * VALUE : (h + 1) * VALUE])
         )
     branch = jnp.concatenate(branch, axis=2).astype(jnp.bfloat16).reshape(tokens, hv)
-    hidden = x + plane_sum(contract_rows(branch, out_cols), True)
+    branch, cot = lax.optimization_barrier((branch, cot))
+    cot = jnp.concatenate(cot, axis=0)
+    hidden = x + block_sum(row_sum([branch], [out_cols], None, F32), True, F32)
 
     scale_two = lax.rsqrt(jnp.mean(hidden * hidden, axis=1, keepdims=True) + EPS)
     normed_two = hidden * scale_two
-    second_in = plane_gather((normed_two * ffn_norm_gain).astype(jnp.bfloat16), False)
-    d_second = jnp.zeros((tokens, width), jnp.float32)
-    fed = jnp.zeros((tokens, width), jnp.float32)
-    grad_ffn = []
-    for weight in ffn:
+    second_in = jnp.concatenate(
+        plane_blocks((normed_two * ffn_norm_gain).astype(jnp.bfloat16)), axis=0
+    )
+    inner, d_both = [], []
+    grad_ffn = jnp.zeros((width, 3 * ff), jnp.bfloat16)
+    for part in range(2):
+        if part:
+            grad_ffn, ffn[1] = lax.optimization_barrier((grad_ffn, ffn[1]))
+        weight = ffn[part]
         units = weight.shape[1] // 3
         both_in, down_in = weight[:, : 2 * units], weight[:, 2 * units :]
         both = jnp.dot(second_in, both_in, preferred_element_type=jnp.float32)
         gate_part, up_part = both[:, :units], both[:, units:]
         gate_silu = jax.nn.silu(gate_part)
-        inner = (gate_silu * up_part).astype(jnp.bfloat16)
+        inner.append((gate_silu * up_part).astype(jnp.bfloat16))
         d_inner = jnp.dot(cot, down_in, preferred_element_type=jnp.float32)
-        d_both = jnp.concatenate(
-            [d_inner * up_part * silu_slope(gate_part), d_inner * gate_silu], axis=1
-        ).astype(jnp.bfloat16)
-        d_second = d_second + contract_rows(d_both, both_in)
-        fed = fed + contract_rows(inner, down_in)
-        grad_ffn.append(
+        d_both.append(
             jnp.concatenate(
-                [contract_tokens(second_in, d_both), contract_tokens(cot, inner)], axis=1
+                [d_inner * up_part * silu_slope(gate_part), d_inner * gate_silu], axis=1
             ).astype(jnp.bfloat16)
         )
-    grad_ffn[0] = shard_sum(grad_ffn[0])
-    grad_ffn[1], grad_ffn[0] = lax.optimization_barrier((grad_ffn[1], grad_ffn[0]))
-    grad_ffn[1] = shard_sum(grad_ffn[1])
-    d_second = plane_sum(d_second, False)
-    result = hidden + plane_sum(fed, False)
+        for at, grad in (
+            (0, contract_tokens(second_in, d_both[-1])),
+            (2 * units, contract_tokens(cot, inner[-1])),
+        ):
+            grad_ffn = lax.dynamic_update_slice(
+                grad_ffn, grad.astype(jnp.bfloat16), (0, 3 * cut * part + at)
+            )
+    ups = [w[:, : 2 * w.shape[1] // 3] for w in ffn]
+    downs = [w[:, 2 * w.shape[1] // 3 :] for w in ffn]
+    d_both = after(d_both, grad_ffn)
+    grad_ffn = shard_sum(grad_ffn)
+    d_second = block_sum(row_sum(d_both, ups), False)
     grad_gain_two = jnp.sum(d_second * normed_two, axis=0)
     d_hidden = grad_out[0].astype(jnp.float32) + norm_back(
         normed_two, scale_two, d_second * ffn_norm_gain
     )
 
-    d_mix = plane_gather(d_hidden.astype(jnp.bfloat16), True)
+    d_mix = plane_gather(d_hidden.astype(jnp.bfloat16))
     d_branch = jnp.dot(d_mix, out_cols, preferred_element_type=jnp.float32)
-    grad_out_cols = contract_tokens(d_mix, branch).astype(jnp.bfloat16)
-    d_branch, grad_ffn[0] = lax.optimization_barrier((d_branch, grad_ffn[0]))
-    d_conv_in, d_gate, d_aux, grad_taps, grad_head_gain = mix_back(
+    fed = product_rows(inner, downs, False).astype(jnp.bfloat16)
+    d_branch, fed, final = lax.optimization_barrier((d_branch, fed, final))
+    result = hidden + block_sum(row_sum(inner, downs, fed), False)
+    result = result.astype(jnp.bfloat16)
+    final = final.reshape(2, heads, VALUE, KEY).astype(jnp.bfloat16)
+    other = swap_core(final[1])
+    pair = jnp.zeros((2, heads, VALUE, KEY), jnp.bfloat16)
+    pair = lax.dynamic_update_index_in_dim(pair, final[0], core, 0)
+    pair = lax.dynamic_update_index_in_dim(pair, other, 1 - core, 0)
+    final_state = jnp.swapaxes(laid_out(pair, "seq"), 0, 1).astype(jnp.float32)
+    final_state = final_state.reshape(1, HEADS, VALUE, KEY)
+
+    d_all, grad_taps, grad_head_gain, rate_sums = mix_back(
         conv_in,
         taps,
         aux,
+        factor,
         gate,
         head_gain[None],
         mixed,
@@ -690,42 +778,42 @@
         d_branch.reshape(2, length, hv),
         heads,
     )
-    d_conv_in = d_conv_in.reshape(tokens, chan)
-    d_gate = d_gate.reshape(tokens, hv)
-    d_decay, d_beta = d_aux[:, :, :heads], d_aux[:, :, heads : 2 * heads]
-    d_rate_input = d_decay * -jnp.exp(own_rate) * jax.nn.sigmoid(rate_input)
-    grad_log_rate = jnp.sum(d_decay * decay_log, axis=(0, 1))
-    grad_rate_bias = jnp.sum(d_rate_input, axis=(0, 1))
-    d_rates = jnp.concatenate([d_rate_input, d_beta * beta * (1.0 - beta)], axis=2)
-    d_rates = d_rates.astype(jnp.bfloat16).reshape(tokens, 2 * heads)
-    d_mix_in = jnp.concatenate([d_conv_in, d_rates], axis=1)
-    grad_gate_out = jnp.concatenate(
-        [contract_tokens(first_in, d_gate).astype(jnp.bfloat16), grad_out_cols], axis=1
-    )
-    grad_gate_out, grad_ffn[1] = lax.optimization_barrier((grad_gate_out, grad_ffn[1]))
-    grad_gate_out = shard_sum(grad_gate_out)
-    grad_mix_in = contract_tokens(first_in, d_mix_in).astype(jnp.bfloat16)
-    grad_mix_in, grad_gate_out = lax.optimization_barrier((grad_mix_in, grad_gate_out))
-    grad_mix_in = to_holders(shard_sum(grad_mix_in), split)
-    grad_gate_out = to_holders(grad_gate_out, split)
-    grad_ffn = [to_holders(g, split) for g in grad_ffn]
-    d_first = contract_rows(d_mix_in, mix_in) + contract_rows(d_gate, gate_in)
-    d_first = plane_sum(d_first, True)
-    grad_gain_one = jnp.sum(d_first * normed, axis=0)
-    d_row = d_hidden + norm_back(normed, scale, d_first * norm_gain)
-
-    sides = jnp.pad(jnp.concatenate([grad_log_rate, grad_rate_bias]), (0, chan - 2 * heads))
-    sides = butterfly(jnp.concatenate([grad_taps, sides[None]], axis=0), "z")
-    blocks = [sides] + [from_peer(sides, "seq", k) for k in range(1, seq)]
-    blocks = [[b, swap_core(b)] for b in blocks]
-    sides = jnp.zeros((2, seq) + sides.shape, jnp.float32)
-    for k in range(seq):
-        for c in range(2):
-            sides = lax.dynamic_update_slice(
-                sides, blocks[k][c][None, None], (core ^ c, me ^ k, 0, 0)
-            )
-    sides = sides.reshape(split, CONV + 1, chan)
-    grad_conv = jnp.swapaxes(sides[:, :CONV], 0, 1)
+    d_all = d_all.reshape(tokens, chan + hv + 128)
+    whole_in = jnp.concatenate(
+        [mix_in, gate_in, jnp.pad(rate_in.T, ((0, 0), (0, 128 - 2 * heads)))], axis=1
+    )
+    row_first = row_sum([d_all], [whole_in])
+    grad_proj = contract_tokens(first_in, d_all[:, : chan + hv]).astype(jnp.bfloat16)
+    grad_proj = jnp.concatenate(
+        [grad_proj, contract_tokens(d_mix, branch).astype(jnp.bfloat16)], axis=1
+    )
+    grad_proj, grad_ffn, row_first = lax.optimization_barrier((grad_proj, grad_ffn, row_first))
+    d_first = block_sum(row_first, True)
+    grad_proj = shard_sum(grad_proj)
+    grad_ffn = to_holders(grad_ffn, split)
+    def hidden_columns(at):
+        first, second = grad_ffn[:, :, : 3 * cut], grad_ffn[:, :, 3 * cut :]
+        return jnp.concatenate(
+            [g[:, :, at * u : (at + 1) * u] for g, u in ((first, cut), (second, ff - cut))], axis=2
+        ).reshape(rows, FF)
+
+    grad_gate_up = jnp.concatenate([hidden_columns(0), hidden_columns(1)], axis=1)
+    grad_down = hidden_columns(2)
+
+    grad_rate = lax.dot_general(
+        d_all[:, chan + hv :], first_in, (((0,), (0,)), ((), ())), preferred_element_type=jnp.float32
+    )[: 2 * heads]
+    small = jnp.concatenate(
+        [
+            grad_taps,
+            grad_rate.reshape(-1, chan),
+            jnp.pad(rate_sums[:2].reshape(1, -1), ((0, 0), (0, chan - 256))),
+        ],
+        axis=0,
+    )
+    small = laid_out(laid_out(axis_sum(small, "z"), "seq"), "core")
+    small = small.reshape((split,) + small.shape[2:])
+    grad_conv = jnp.swapaxes(small[:, :CONV], 0, 1)
     grad_conv = jnp.concatenate(
         [
             grad_conv[:, :, :hk].reshape(CONV, HK),
@@ -734,59 +822,41 @@
         ],
         axis=1,
     )
-    sums = jnp.concatenate([grad_gain_one, grad_gain_two, grad_head_gain[0]])
-    sums = butterfly(butterfly(butterfly(sums, "core"), "seq"), "z")
+    rate_sums = small[:, -1, :256].reshape(split, 2, 128)
+    grad_rate = small[:, CONV:-1].reshape(split, 2, heads, width)
+    grad_rate = jnp.swapaxes(grad_rate, 0, 1).reshape(2 * HEADS, width)
+    grad_rate = lax.dynamic_slice_in_dim(grad_rate, (plane * split + here) * rows, rows, 1).T
+
+    d_first, result, final_state = lax.optimization_barrier((d_first, result, final_state))
+    grad_gain_one = jnp.sum(d_first * normed, axis=0)
+    sums = all_sum(jnp.concatenate([grad_gain_one, grad_gain_two, grad_head_gain[0]]))
+    d_row = d_hidden + norm_back(normed, scale, d_first * norm_gain)
+    d_row = d_row.astype(jnp.bfloat16)
+    holders_proj = to_holders(grad_proj, split)
     grad_proj = jnp.concatenate(
         [
-            grad_mix_in[:, :, :hk].reshape(rows, HK),
-            grad_mix_in[:, :, hk : 2 * hk].reshape(rows, HK),
-            grad_mix_in[:, :, 2 * hk : chan].reshape(rows, HV),
-            grad_gate_out[:, :, :hv].reshape(rows, HV),
+            holders_proj[:, :, :hk].reshape(rows, HK),
+            holders_proj[:, :, hk : 2 * hk].reshape(rows, HK),
+            holders_proj[:, :, 2 * hk : chan].reshape(rows, HV),
+            holders_proj[:, :, chan : chan + hv].reshape(rows, HV),
         ],
         axis=1,
     )
-    grad_rate = jnp.concatenate(
-        [
-            grad_mix_in[:, :, chan : chan + heads].reshape(rows, HEADS),
-            grad_mix_in[:, :, chan + heads :].reshape(rows, HEADS),
-        ],
-        axis=1,
-    )
-    units = [g.shape[2] // 3 for g in grad_ffn]
-
-    def hidden_columns(at):
-        return jnp.concatenate(
-            [g[:, :, at * u : (at + 1) * u] for g, u in zip(grad_ffn, units)], axis=2
-        ).reshape(rows, FF)
-
-    grad_gate_up = jnp.concatenate([hidden_columns(0), hidden_columns(1)], axis=1)
-
-    final = final.reshape(2, heads, VALUE, KEY)
-    other = swap_core(final[1].astype(jnp.bfloat16))
-    pair = jnp.zeros((2, heads, VALUE, KEY), jnp.bfloat16)
-    pair = lax.dynamic_update_index_in_dim(pair, final[0].astype(jnp.bfloat16), core, 0)
-    pair = lax.dynamic_update_index_in_dim(pair, other, 1 - core, 0)
-    final_state = jnp.zeros((2, seq, heads, VALUE, KEY), jnp.float32)
-    for k in range(seq):
-        block = from_peer(pair, "seq", k) if k else pair
-        final_state = lax.dynamic_update_index_in_dim(
-            final_state, block.astype(jnp.float32), me ^ k, 1
-        )
     return (
-        result.astype(jnp.bfloat16)[None],
-        d_row.astype(jnp.bfloat16)[None],
-        final_state.reshape(1, HEADS, VALUE, KEY),
+        result[None],
+        d_row[None],
+        final_state,
         sums[:width],
         grad_proj,
         grad_rate,
         grad_conv,
-        sides[:, CONV, :heads].reshape(HEADS),
-        sides[:, CONV, heads : 2 * heads].reshape(HEADS),
+        rate_sums[:, 0, :heads].reshape(HEADS),
+        rate_sums[:, 1, :heads].reshape(HEADS),
         sums[2 * width :],
-        grad_gate_out[:, :, hv:].reshape(rows, HV),
+        holders_proj[:, :, chan + hv :].reshape(rows, HV),
         sums[width : 2 * width],
         grad_gate_up,
-        hidden_columns(2),
+        grad_down,
     )
 
 

time: 785 us -> 734 us (0.935)
  waiting for transfers between devices: 271 us -> 224 us
  matrix products: 105 us -> 135 us
  Pallas kernels: 75.2 us -> 49.5 us
  other arithmetic: 57.3 us -> 46.2 us
    all_gather x4 -> x3, waiting for transfers between devices: 61.3 us -> 9.7 us  [along_z(): return lax.all_gather(x, 'z', axis=0, tiled=True)]
    pallas_call x1, Pallas kernels: 44.2 us -> 20.2 us  [mix(): pl.pallas_call(functools.partial(mix_kernel, heads), grid=(count,), in_sp...]
    unnamed x193 -> x141, local copies, waits for them, and re-layouts: 33.9 us -> 14.9 us
    all_to_all x4 -> x2, waiting for transfers between devices: 17.5 us -> 2.14 us  [to_holders(): blocks = lax.all_to_all(mine.reshape(split, -1, mine.shape[1]), PLANE, 0, 0)]
    ppermute x37 -> x44, waiting for transfers between devices: 152 us -> 166 us  [from_peer(): lax.ppermute(x, axis, [(i, i ^ distance) for i in range(lax.axis_size(axi...]
    dot_general x7 -> x6, matrix products: 24.9 us -> 39 us  [contract_tokens(): lax.dot_general(left, right, (((0,), (0,)), ((), ())), preferred_element_...]
    ppermute x37 -> x44, starting transfers between devices: 53.5 us -> 65.3 us  [from_peer(): lax.ppermute(x, axis, [(i, i ^ distance) for i in range(lax.axis_size(axi...]
    dot_general x7 -> x13, matrix products: 39.4 us -> 50.7 us  [contract_rows(): lax.dot_general(left, right, (((1,), (1,)), ((), ())), preferred_element_...]
  transfers between devices with their start and end apart: 76 -> 75, of which waited for: 35 -> 36; matrix products, arithmetic and copies ran while one was open for 33% -> 37% of each run, Pallas kernels for 10% -> 7%
where the time goes in v3:
time: 734 us; the launch traced here: 725 us
  waiting for transfers between devices  224 us (31%)
  matrix products  135 us (18%)
  local copies, waits for them, and re-layouts  129 us (18%)
  starting transfers between devices  83.7 us (11%)
  Pallas kernels  49.5 us (7%)
  other arithmetic  46.2 us (6%)
  blocking collectives  42.4 us (6%)
  between operations  16 us (2%)
    ppermute x44, waiting for transfers between devices, from_peer(): lax.ppermute(x, axis, [(i, i ^ distance) for i in range(lax.axis_size(axi...  166 us
    ppermute x44, starting transfers between devices, from_peer(): lax.ppermute(x, axis, [(i, i ^ distance) for i in range(lax.axis_size(axi...  65.3 us
    dot_general x13, matrix products, contract_rows(): lax.dot_general(left, right, (((1,), (1,)), ((), ())), preferred_element_...  50.7 us
    all_to_all x1, blocking collectives, plane_exchange(): got = lax.all_to_all(blocks, PLANE, 0, 0)  42.4 us
    dot_general x6, matrix products, contract_tokens(): lax.dot_general(left, right, (((0,), (0,)), ((), ())), preferred_element_...  39 us
    pallas_call x1, Pallas kernels, mix_back(): pl.pallas_call(functools.partial(mix_back_kernel, heads), grid=(count,),...  29.3 us
    pallas_call x1, Pallas kernels, mix(): pl.pallas_call(functools.partial(mix_kernel, heads), grid=(count,), in_sp...  20.2 us
    all_to_all x1, waiting for transfers between devices, on_device(): mix_in = lax.all_to_all(jnp.swapaxes(mix_in, 0, 1), PLANE, 0, 0)  15.2 us
  transfers between devices with their start and end apart: 75, of which 36 were waited for; matrix products, arithmetic and copies ran while one was open for 37% of the time, Pallas kernels for 7%

profile of v3, /device:TPU:0, one launch (start us, length us, event | category | flops | bytes accessed | tf_op | source)
XLA Modules:
  0.0 725.4 jit_solution(11062263908315289513)
XLA Ops:
  32.9 5.3 concatenate.78
  53.3 42.4 %all_to_all.20 = bf16[8,64,3092]{2,1,0:T(8,128)(2,1)} all-to-all(bf16[8,64,3092]{2,1,0:T(8,128)(2,1)S(1)} %concatenate.78), channel_id=1, replica_groups=mesh['z'=4,'core'=2,'seq'=4] {'core','seq'}, dimensions={0} | all-to-all | bytes 6332416 | tf_op jit(solution)/shard_map/all_to_all | solution.py:548
  146.7 15.2 %all-to-all-done = bf16[8,4,64,1024]{3,2,1,0:T(8,128)(2,1)} async-done(((bf16[8,4,64,1024]{3,2,1,0:T(8,128)(2,1)}), bf16[8,4,64,1024]{3,2,1,0:T(8,128)(2,1)}, u32[]{:S(2)}, u32[]{:S(2)}) %all-to-all-start) | async-done | bytes 4194336 | tf_op jit(solution)/shard_map/all_to_all | solution.py:657
  164.5 9.4 %convolution_convert_fusion.7 = bf16[1024,1024]{1,0:T(8,128)(2,1)} fusion(bf16[1024,2048]{1,0:T(8,128)(2,1)} %constant_dynamic-update-slice_fusion.28, bf16[2048,1024]{1,0:T(8,128)(2,1)S(1)} %bitcast.198), kind=kOutput, calls=%fused_computation.38 | convolution fusion | flops 4296015872 | bytes 10485760 | tf_op jit(solution)/shard_map/dot_general | solution.py:694
  173.9 20.2 %mix_forward.1 = (f32[2,512,512]{2,1,0:T(8,128)S(1)}, f32[4,4,128,128]{3,2,1,0:T(8,128)S(1)}, f32[2,512,512]{2,1,0:T(8,128)}, f32[4,4,128,256]{3,2,1,0:T(8,128)}, f32[4,256,128]{2,1,0:T(8,128)S(1)}) custom-call(bf16[2,512,1024]{2,1,0:T(8,128)(2,1)} %bitcast.181, f32[4,1024]{1,0:T(4,128)S(1)} %pad_maximum_fusion.14.taps_ref, f32[2,512,128]{2,1,0:T(8,128)S(1)} %pad.27.aux_ref), custom_call_target="tpu_custom_call" | custom-call | flops 1000000 | bytes 1000000 | tf_op jit(solution)/shard_map/mix_forward/pallas_call | solution.py:195
  203.9 5.9 fusion.111
  214.9 11.2 %collective-permute-done.12 = bf16[128,2048]{1,0:T(8,128)(2,1)S(1)} collective-permute-done((bf16[128,2048]{1,0:T(8,128)(2,1)}, bf16[128,2048]{1,0:T(8,128)(2,1)S(1)}, u32[]{:S(2)}, u32[]{:S(2)}) %collective-permute-start.12) | collective-permute-done | bytes 524320 | tf_op jit(solution)/shard_map/ppermute | solution.py:487
  232.4 7.3 %collective-permute-done.18 = f32[512,2048]{1,0:T(8,128)} collective-permute-done((f32[512,2048]{1,0:T(8,128)}, f32[512,2048]{1,0:T(8,128)}, u32[]{:S(2)}, u32[]{:S(2)}) %collective-permute-start.18) | collective-permute-done | bytes 4194336 | tf_op jit(solution)/shard_map/ppermute | solution.py:483
  252.1 18.2 %collective-permute-done.19 = f32[128,2048]{1,0:T(8,128)S(1)} collective-permute-done((f32[128,2048]{1,0:T(8,128)S(1)}, f32[128,2048]{1,0:T(8,128)S(1)}, u32[]{:S(2)}, u32[]{:S(2)}) %collective-permute-start.19) | collective-permute-done | bytes 1048608 | tf_op jit(solution)/shard_map/ppermute | solution.py:487
  270.3 22.9 %collective-permute-done.20 = f32[128,2048]{1,0:T(8,128)S(1)} collective-permute-done((f32[128,2048]{1,0:T(8,128)S(1)}, f32[128,2048]{1,0:T(8,128)S(1)}, u32[]{:S(2)}, u32[]{:S(2)}) %collective-permute-start.20) | collective-permute-done | bytes 1048608 | tf_op jit(solution)/shard_map/ppermute | solution.py:487
  300.8 8.8 %collective-permute-done.22 = bf16[128,2048]{1,0:T(8,128)(2,1)S(1)} collective-permute-done((bf16[128,2048]{1,0:T(8,128)(2,1)S(1)}, bf16[128,2048]{1,0:T(8,128)(2,1)S(1)}, u32[]{:S(2)}, u32[]{:S(2)}) %collective-permute-start.22) | collective-permute-done | bytes 524320 | tf_op jit(solution)/shard_map/ppermute | solution.py:487
  310.4 9.3 %collective-permute-done.23 = bf16[128,2048]{1,0:T(8,128)(2,1)S(1)} collective-permute-done((bf16[128,2048]{1,0:T(8,128)(2,1)S(1)}, bf16[128,2048]{1,0:T(8,128)(2,1)S(1)}, u32[]{:S(2)}, u32[]{:S(2)}) %collective-permute-start.23) | collective-permute-done | bytes 524320 | tf_op jit(solution)/shard_map/ppermute | solution.py:487
  325.3 7.6 %fusion.6 = f32[1024,1024]{0,1:T(8,128)S(1)} fusion(bf16[1024,2048]{1,0:T(8,128)(2,1)} %constant_dynamic-update-slice_fusion.8, bf16[2048,1536]{1,0:T(8,128)(2,1)} %all-gather.8.cloned.1.call-done), kind=kOutput, calls=%fused_computation.19 | convolution fusion | flops 4294967296 | bytes 12582912 | tf_op jit(solution)/shard_map/dot_general | solution.py:726
  332.9 6.0 multiply_convert_fusion.2
  339.0 9.1 %convolution_convert_fusion.1 = bf16[2048,1024]{0,1:T(8,128)(2,1)S(1)} fusion(bf16[1024,2048]{1,0:T(8,128)(2,1)} %constant_dynamic-update-slice_fusion.8, bf16[1024,512]{0,1:T(8,128)(2,1)S(1)} %get-tuple-element.122, bf16[1024,512]{0,1:T(8,128)(2,1)S(1)} %get-tuple-element.121), kind=kOutput, calls=%fused_computation.13 | convolution fusion | flops 4301258752 | bytes 10485760 | tf_op jit(solution)/shard_map/dot_general | solution.py:468
  352.4 5.9 fusion.9
  358.3 9.4 %all-gather.10.cloned.1.call-done = bf16[2048,528]{1,0:T(8,128)(2,1)} async-done(((bf16[512,528]{1,0:T(8,128)(2,1)}), bf16[2048,528]{1,0:T(8,128)(2,1)}) %all-gather.10.cloned.1.call-update) | async-done | bytes 2162704 | tf_op jit(solution)/shard_map/all_gather | solution.py:553
  376.8 5.2 fusion.10
  389.4 5.5 fusion.2
  405.5 11.3 %collective-permute-done.30 = bf16[128,2048]{1,0:T(8,128)(2,1)S(1)} collective-permute-done((bf16[128,2048]{1,0:T(8,128)(2,1)S(1)}, bf16[128,2048]{1,0:T(8,128)(2,1)S(1)}, u32[]{:S(2)}, u32[]{:S(2)}) %collective-permute-start.30) | collective-permute-done | bytes 524320 | tf_op jit(solution)/shard_map/ppermute | solution.py:487
  416.8 11.4 %collective-permute-done.31 = bf16[128,2048]{1,0:T(8,128)(2,1)S(1)} collective-permute-done((bf16[128,2048]{1,0:T(8,128)(2,1)S(1)}, bf16[128,2048]{1,0:T(8,128)(2,1)S(1)}, u32[]{:S(2)}, u32[]{:S(2)}) %collective-permute-start.31) | collective-permute-done | bytes 524320 | tf_op jit(solution)/shard_map/ppermute | solution.py:487
  437.1 7.5 %collective-permute-done.33 = bf16[128,2048]{1,0:T(8,128)(2,1)S(1)} collective-permute-done((bf16[128,2048]{1,0:T(8,128)(2,1)S(1)}, bf16[128,2048]{1,0:T(8,128)(2,1)S(1)}, u32[]{:S(2)}, u32[]{:S(2)}) %collective-permute-start.33) | collective-permute-done | bytes 524320 | tf_op jit(solution)/shard_map/ppermute | solution.py:487
  444.7 11.5 %collective-permute-done.34 = bf16[128,2048]{1,0:T(8,128)(2,1)S(1)} collective-permute-done((bf16[128,2048]{1,0:T(8,128)(2,1)S(1)}, bf16[128,2048]{1,0:T(8,128)(2,1)S(1)}, u32[]{:S(2)}, u32[]{:S(2)}) %collective-permute-start.34) | collective-permute-done | bytes 524320 | tf_op jit(solution)/shard_map/ppermute | solution.py:487
  462.8 29.3 %mix_backward.1 = (bf16[2,512,1664]{2,1,0:T(8,128)(2,1)}, f32[4,1024]{1,0:T(4,128)S(1)}, f32[1,256]{1,0:T(1,128)S(1)}, f32[8,128]{1,0:T(8,128)S(1)}) custom-call(bf16[2,512,1024]{2,1,0:T(8,128)(2,1)S(1)} %bitcast.182, bf16[2,512,1024]{2,1,0:T(8,128)(2,1)S(1)} %bitcast.183, f32[4,1024]{1,0:T(4,128)S(1)} %pad_maximum_fusion.14.taps_ref, ...), custom_call_target="tpu_custom_call" | custom-call | flops 1000000 | bytes 1000000 | tf_op jit(solution)/shard_map/mix_backward/pallas_call | solution.py:417
  492.1 7.1 convolution_convert_fusion.4
  503.1 11.1 %convolution_convert_fusion = bf16[2048,1536]{0,1:T(8,128)(2,1)} fusion(bf16[1024,2048]{1,0:T(8,128)(2,1)} %constant_dynamic-update-slice_fusion.28, bf16[1024,1664]{1,0:T(8,128)(2,1)S(1)} %bitcast.235), kind=kOutput, calls=%fused_computation.3 | convolution fusion | flops 6445596672 | bytes 13631488 | tf_op jit(solution)/shard_map/dot_general | solution.py:468
  514.1 8.4 %pad_maximum_fusion = bf16[2048,2048]{0,1:T(8,128)(2,1)} fusion(bf16[2048,512]{0,1:T(8,128)(2,1)} %convolution_convert_fusion.3, bf16[2048,1536]{0,1:T(8,128)(2,1)} %convolution_convert_fusion), kind=kLoop, calls=%fused_computation.2 | loop fusion | flops 16777216 | bytes 16777216 | tf_op jit(solution)/shard_map/concatenate | solution.py:787
  522.5 8.3 %convert_add_fusion.1 = f32[512,2048]{1,0:T(8,128)} fusion(bf16[512,2048]{1,0:T(8,128)(2,1)} %collective-permute-done.40, bf16[2,512,1664]{2,1,0:T(8,128)(2,1)} %get-tuple-element.94, bf16[2048,4]{1,0:T(8,128)(2,1)S(1)} %bitcast.211, bf16[2048,512]{1,0:T(8,128)(2,1)} %slice.356, bf16[2048,1024]{1,0:T(8,128)(2,1)} %bitcast.199), kind=kOutput, calls=%fused_computation.9 | convolution fusion | flops 3519021056 | bytes 14303232 | tf_op jit(solution)/shard_map/dot_general | solution.py:462
  587.0 11.3 %collective-permute-done.46 = bf16[128,2048]{1,0:T(8,128)(2,1)S(1)} collective-permute-done((bf16[128,2048]{1,0:T(8,128)(2,1)S(1)}, bf16[128,2048]{1,0:T(8,128)(2,1)S(1)}, u32[]{:S(2)}, u32[]{:S(2)}) %collective-permute-start.46) | collective-permute-done | bytes 524320 | tf_op jit(solution)/shard_map/ppermute | solution.py:487
  608.3 11.6 %collective-permute-done.42 = bf16[128,2048]{1,0:T(8,128)(2,1)} collective-permute-done((bf16[128,2048]{1,0:T(8,128)(2,1)}, bf16[128,2048]{1,0:T(8,128)(2,1)}, u32[]{:S(2)}, u32[]{:S(2)}) %collective-permute-start.42) | collective-permute-done | bytes 524320 | tf_op jit(solution)/shard_map/ppermute | solution.py:487
  623.2 10.9 %collective-permute-start.52 = (f32[4352]{0:T(1024)S(1)}, f32[4352]{0:T(1024)S(1)}, u32[]{:S(2)}, u32[]{:S(2)}) collective-permute-start(f32[4352]{0:T(1024)S(1)} %pad_maximum_fusion.13), channel_id=1, source_target_pairs={{0,1},{1,0},{2,3},{3,2},{4,5},{5,4},{6,7},{7,6},{8,9},{9,8},{10,11... | collective-permute-start | bytes 52232 | tf_op jit(solution)/shard_map/ppermute | solution.py:487
  666.3 13.8 %reduce-scatter.5.cloned.1.call-done = bf16[512,2048]{0,1:T(8,128)(2,1)} async-done(((bf16[2048,2048]{0,1:T(8,128)(2,1)}), bf16[512,2048]{0,1:T(8,128)(2,1)}) %reduce-scatter.5.cloned.1.call-update) | async-done | bytes 2097168 | tf_op jit(solution)/shard_map/reduce_scatter | solution.py:557
  (460 shorter events, 331.1 us)
Async XLA Ops:
  7.2 96.5 %all-gather.12.cloned.1.call-start = ((), (), s32[]{:S(2)}) async-start(), calls=%async_computation.11 | async-start | bytes 5242880 | tf_op jit(solution)/shard_map/all_gather | solution.py:626
  14.8 23.5 %collective-permute-start = (bf16[128,2048]{1,0:T(8,128)(2,1)}, bf16[128,2048]{1,0:T(8,128)(2,1)}, u32[]{:S(2)}, u32[]{:S(2)}) collective-permute-start(bf16[128,2048]{1,0:T(8,128)(2,1)} %get-tuple-element.120), channel_id=1, source_target_pairs={{0,1},{1,0},{2,3},{3,2},{4,5},{5,4},{6,7},{7,6},{8,9},{9,8},{10,11... | collective-permute-start | bytes 1572872 | tf_op jit(solution)/shard_map/ppermute | solution.py:487
  17.7 24.9 %collective-permute-start.1 = (bf16[128,2048]{1,0:T(8,128)(2,1)}, bf16[128,2048]{1,0:T(8,128)(2,1)}, u32[]{:S(2)}, u32[]{:S(2)}) collective-permute-start(bf16[128,2048]{1,0:T(8,128)(2,1)} %get-tuple-element.120), channel_id=1, source_target_pairs={{0,2},{1,3},{2,0},{3,1},{4,6},{5,7},{6,4},{7,5},{8,10},{9,11},{10,... | collective-permute-start | bytes 1572872 | tf_op jit(solution)/shard_map/ppermute | solution.py:487
  19.3 23.3 %collective-permute-start.2 = (bf16[128,2048]{1,0:T(8,128)(2,1)}, bf16[128,2048]{1,0:T(8,128)(2,1)}, u32[]{:S(2)}, u32[]{:S(2)}) collective-permute-start(bf16[128,2048]{1,0:T(8,128)(2,1)} %get-tuple-element.120), channel_id=1, source_target_pairs={{0,3},{1,2},{2,1},{3,0},{4,7},{5,6},{6,5},{7,4},{8,11},{9,10},{10,... | collective-permute-start | bytes 1572872 | tf_op jit(solution)/shard_map/ppermute | solution.py:487
  19.3 29.5 %collective-permute-start.3 = (bf16[128,2048]{1,0:T(8,128)(2,1)}, bf16[128,2048]{1,0:T(8,128)(2,1)}, u32[]{:S(2)}, u32[]{:S(2)}) collective-permute-start(bf16[128,2048]{1,0:T(8,128)(2,1)} %get-tuple-element.120), channel_id=1, source_target_pairs={{0,4},{4,0},{1,5},{5,1},{2,6},{6,2},{3,7},{7,3},{8,12},{12,8},{9,1... | collective-permute-start | bytes 1572872 | tf_op jit(solution)/shard_map/ppermute | solution.py:483
  20.9 175.3 %all-gather.6.cloned.1.call-start = ((), (), s32[]{:S(2)}) async-start(), calls=%async_computation.6 | async-start | bytes 5242880 | tf_op jit(solution)/shard_map/all_gather | solution.py:553
  108.7 53.2 %all-to-all-start = ((bf16[8,4,64,1024]{3,2,1,0:T(8,128)(2,1)}), bf16[8,4,64,1024]{3,2,1,0:T(8,128)(2,1)}, u32[]{:S(2)}, u32[]{:S(2)}) async-start(bf16[8,4,64,1024]{3,2,1,0:T(8,128)(2,1)} %bitcast.187), calls=%async_computation | async-start | bytes 8388608 | tf_op jit(solution)/shard_map/all_to_all | solution.py:657
  113.3 212.0 %all-gather.8.cloned.1.call-start = ((), (), s32[]{:S(2)}) async-start(), calls=%async_computation.7 | async-start | bytes 7864320 | tf_op jit(solution)/shard_map/all_gather | solution.py:553
  199.7 168.0 %all-gather.10.cloned.1.call-start = ((), (), s32[]{:S(2)}) async-start(), calls=%async_computation.8 | async-start | bytes 3276800 | tf_op jit(solution)/shard_map/all_gather | solution.py:553
  201.1 25.1 %collective-permute-start.12 = (bf16[128,2048]{1,0:T(8,128)(2,1)}, bf16[128,2048]{1,0:T(8,128)(2,1)S(1)}, u32[]{:S(2)}, u32[]{:S(2)}) collective-permute-start(bf16[128,2048]{1,0:T(8,128)(2,1)} %bitcast.194), channel_id=1, source_target_pairs={{0,2},{1,3},{2,0},{3,1},{4,6},{5,7},{6,4},{7,5},{8,10},{9,11},{10,... | collective-permute-start | bytes 1572872 | tf_op jit(solution)/shard_map/ppermute | solution.py:487
  202.5 23.6 %collective-permute-start.13 = (bf16[128,2048]{1,0:T(8,128)(2,1)}, bf16[128,2048]{1,0:T(8,128)(2,1)S(1)}, u32[]{:S(2)}, u32[]{:S(2)}) collective-permute-start(bf16[128,2048]{1,0:T(8,128)(2,1)} %bitcast.195), channel_id=1, source_target_pairs={{0,3},{1,2},{2,1},{3,0},{4,7},{5,6},{6,5},{7,4},{8,11},{9,10},{10,... | collective-permute-start | bytes 1572872 | tf_op jit(solution)/shard_map/ppermute | solution.py:487
  203.5 23.9 %collective-permute-start.14 = (bf16[128,2048]{1,0:T(8,128)(2,1)}, bf16[128,2048]{1,0:T(8,128)(2,1)S(1)}, u32[]{:S(2)}, u32[]{:S(2)}) collective-permute-start(bf16[128,2048]{1,0:T(8,128)(2,1)} %bitcast.196), channel_id=1, source_target_pairs={{0,4},{4,0},{1,5},{5,1},{2,6},{6,2},{3,7},{7,3},{8,12},{12,8},{9,1... | collective-permute-start | bytes 1572872 | tf_op jit(solution)/shard_map/ppermute | solution.py:483
  232.3 298.5 %reduce-scatter.3.cloned.1.call-start = ((), (), s32[]{:S(2)}) async-start(), calls=%async_computation.9 | async-start | bytes 10567680 | tf_op jit(solution)/shard_map/reduce_scatter | solution.py:557
  244.2 26.1 %collective-permute-start.19 = (f32[128,2048]{1,0:T(8,128)S(1)}, f32[128,2048]{1,0:T(8,128)S(1)}, u32[]{:S(2)}, u32[]{:S(2)}) collective-permute-start(f32[128,2048]{1,0:T(8,128)S(1)} %get-tuple-element.140), channel_id=1, source_target_pairs={{0,1},{1,0},{2,3},{3,2},{4,5},{5,4},{6,7},{7,6},{8,9},{9,8},{10,11... | collective-permute-start | bytes 3145736 | tf_op jit(solution)/shard_map/ppermute | solution.py:487
  245.8 47.4 %collective-permute-start.20 = (f32[128,2048]{1,0:T(8,128)S(1)}, f32[128,2048]{1,0:T(8,128)S(1)}, u32[]{:S(2)}, u32[]{:S(2)}) collective-permute-start(f32[128,2048]{1,0:T(8,128)S(1)} %get-tuple-element.142), channel_id=1, source_target_pairs={{0,2},{1,3},{2,0},{3,1},{4,6},{5,7},{6,4},{7,5},{8,10},{9,11},{10,... | collective-permute-start | bytes 3145736 | tf_op jit(solution)/shard_map/ppermute | solution.py:487
  245.8 47.4 %collective-permute-start.21 = (f32[128,2048]{1,0:T(8,128)S(1)}, f32[128,2048]{1,0:T(8,128)S(1)}, u32[]{:S(2)}, u32[]{:S(2)}) collective-permute-start(f32[128,2048]{1,0:T(8,128)S(1)} %get-tuple-element.141), channel_id=1, source_target_pairs={{0,3},{1,2},{2,1},{3,0},{4,7},{5,6},{6,5},{7,4},{8,11},{9,10},{10,... | collective-permute-start | bytes 3145736 | tf_op jit(solution)/shard_map/ppermute | solution.py:487
  296.1 23.6 %collective-permute-start.23 = (bf16[128,2048]{1,0:T(8,128)(2,1)S(1)}, bf16[128,2048]{1,0:T(8,128)(2,1)S(1)}, u32[]{:S(2)}, u32[]{:S(2)}) collective-permute-start(bf16[128,2048]{1,0:T(8,128)(2,1)S(1)} %get-tuple-element.116), channel_id=1, source_target_pairs={{0,2},{1,3},{2,0},{3,1},{4,6},{5,7},{6,4},{7,5},{8,10},{9,11},{10,... | collective-permute-start | bytes 1572872 | tf_op jit(solution)/shard_map/ppermute | solution.py:487
  298.2 22.4 %collective-permute-start.24 = (bf16[128,2048]{1,0:T(8,128)(2,1)S(1)}, bf16[128,2048]{1,0:T(8,128)(2,1)S(1)}, u32[]{:S(2)}, u32[]{:S(2)}) collective-permute-start(bf16[128,2048]{1,0:T(8,128)(2,1)S(1)} %get-tuple-element.116), channel_id=1, source_target_pairs={{0,3},{1,2},{2,1},{3,0},{4,7},{5,6},{6,5},{7,4},{8,11},{9,10},{10,... | collective-permute-start | bytes 1572872 | tf_op jit(solution)/shard_map/ppermute | solution.py:487
  386.0 294.2 %reduce-scatter.5.cloned.1.call-start = ((), (), s32[]{:S(2)}) async-start(), calls=%async_computation.10 | async-start | bytes 10485760 | tf_op jit(solution)/shard_map/reduce_scatter | solution.py:557
  403.3 24.9 %collective-permute-start.31 = (bf16[128,2048]{1,0:T(8,128)(2,1)S(1)}, bf16[128,2048]{1,0:T(8,128)(2,1)S(1)}, u32[]{:S(2)}, u32[]{:S(2)}) collective-permute-start(bf16[128,2048]{1,0:T(8,128)(2,1)S(1)} %get-tuple-element.156), channel_id=1, source_target_pairs={{0,2},{1,3},{2,0},{3,1},{4,6},{5,7},{6,4},{7,5},{8,10},{9,11},{10,... | collective-permute-start | bytes 1572872 | tf_op jit(solution)/shard_map/ppermute | solution.py:487
  404.7 23.4 %collective-permute-start.32 = (bf16[128,2048]{1,0:T(8,128)(2,1)S(1)}, bf16[128,2048]{1,0:T(8,128)(2,1)S(1)}, u32[]{:S(2)}, u32[]{:S(2)}) collective-permute-start(bf16[128,2048]{1,0:T(8,128)(2,1)S(1)} %get-tuple-element.155), channel_id=1, source_target_pairs={{0,3},{1,2},{2,1},{3,0},{4,7},{5,6},{6,5},{7,4},{8,11},{9,10},{10,... | collective-permute-start | bytes 1572872 | tf_op jit(solution)/shard_map/ppermute | solution.py:487
  432.0 24.2 %collective-permute-start.34 = (bf16[128,2048]{1,0:T(8,128)(2,1)S(1)}, bf16[128,2048]{1,0:T(8,128)(2,1)S(1)}, u32[]{:S(2)}, u32[]{:S(2)}) collective-permute-start(bf16[128,2048]{1,0:T(8,128)(2,1)S(1)} %get-tuple-element.113), channel_id=1, source_target_pairs={{0,2},{1,3},{2,0},{3,1},{4,6},{5,7},{6,4},{7,5},{8,10},{9,11},{10,... | collective-permute-start | bytes 1572872 | tf_op jit(solution)/shard_map/ppermute | solution.py:487
  432.9 23.3 %collective-permute-start.35 = (bf16[128,2048]{1,0:T(8,128)(2,1)S(1)}, bf16[128,2048]{1,0:T(8,128)(2,1)S(1)}, u32[]{:S(2)}, u32[]{:S(2)}) collective-permute-start(bf16[128,2048]{1,0:T(8,128)(2,1)S(1)} %get-tuple-element.113), channel_id=1, source_target_pairs={{0,3},{1,2},{2,1},{3,0},{4,7},{5,6},{6,5},{7,4},{8,11},{9,10},{10,... | collective-permute-start | bytes 1572872 | tf_op jit(solution)/shard_map/ppermute | solution.py:487
  499.2 23.3 %collective-permute-start.40 = (bf16[512,2048]{1,0:T(8,128)(2,1)}, bf16[512,2048]{1,0:T(8,128)(2,1)}, u32[]{:S(2)}, u32[]{:S(2)}) collective-permute-start(bf16[512,2048]{1,0:T(8,128)(2,1)} %convolution_convert_fusion.4), channel_id=1, source_target_pairs={{0,4},{4,0},{1,5},{5,1},{2,6},{6,2},{3,7},{7,3},{8,12},{12,8},{9,1... | collective-permute-start | bytes 6291464 | tf_op jit(solution)/shard_map/ppermute | solution.py:483
  543.6 22.1 %collective-permute-start.44 = (bf16[512,2048]{1,0:T(8,128)(2,1)}, bf16[512,2048]{1,0:T(8,128)(2,1)}, u32[]{:S(2)}, u32[]{:S(2)}) collective-permute-start(bf16[512,2048]{1,0:T(8,128)(2,1)} %add_convert_fusion), channel_id=1, source_target_pairs={{0,4},{4,0},{1,5},{5,1},{2,6},{6,2},{3,7},{7,3},{8,12},{12,8},{9,1... | collective-permute-start | bytes 6291464 | tf_op jit(solution)/shard_map/ppermute | solution.py:483
  572.2 26.1 %collective-permute-start.46 = (bf16[128,2048]{1,0:T(8,128)(2,1)S(1)}, bf16[128,2048]{1,0:T(8,128)(2,1)S(1)}, u32[]{:S(2)}, u32[]{:S(2)}) collective-permute-start(bf16[128,2048]{1,0:T(8,128)(2,1)S(1)} %get-tuple-element.153), channel_id=1, source_target_pairs={{0,2},{1,3},{2,0},{3,1},{4,6},{5,7},{6,4},{7,5},{8,10},{9,11},{10,... | collective-permute-start | bytes 1572872 | tf_op jit(solution)/shard_map/ppermute | solution.py:487
  572.7 25.6 %collective-permute-start.47 = (bf16[128,2048]{1,0:T(8,128)(2,1)S(1)}, bf16[128,2048]{1,0:T(8,128)(2,1)S(1)}, u32[]{:S(2)}, u32[]{:S(2)}) collective-permute-start(bf16[128,2048]{1,0:T(8,128)(2,1)S(1)} %get-tuple-element.152), channel_id=1, source_target_pairs={{0,3},{1,2},{2,1},{3,0},{4,7},{5,6},{6,5},{7,4},{8,11},{9,10},{10,... | collective-permute-start | bytes 1572872 | tf_op jit(solution)/shard_map/ppermute | solution.py:487
  580.9 27.4 %collective-permute-start.41 = (bf16[128,2048]{1,0:T(8,128)(2,1)}, bf16[128,2048]{1,0:T(8,128)(2,1)}, u32[]{:S(2)}, u32[]{:S(2)}) collective-permute-start(bf16[128,2048]{1,0:T(8,128)(2,1)} %get-tuple-element.136), channel_id=1, source_target_pairs={{0,1},{1,0},{2,3},{3,2},{4,5},{5,4},{6,7},{7,6},{8,9},{9,8},{10,11... | collective-permute-start | bytes 1572872 | tf_op jit(solution)/shard_map/ppermute | solution.py:487
  582.3 37.6 %collective-permute-start.42 = (bf16[128,2048]{1,0:T(8,128)(2,1)}, bf16[128,2048]{1,0:T(8,128)(2,1)}, u32[]{:S(2)}, u32[]{:S(2)}) collective-permute-start(bf16[128,2048]{1,0:T(8,128)(2,1)} %get-tuple-element.138), channel_id=1, source_target_pairs={{0,2},{1,3},{2,0},{3,1},{4,6},{5,7},{6,4},{7,5},{8,10},{9,11},{10,... | collective-permute-start | bytes 1572872 | tf_op jit(solution)/shard_map/ppermute | solution.py:487
  585.7 34.2 %collective-permute-start.43 = (bf16[128,2048]{1,0:T(8,128)(2,1)}, bf16[128,2048]{1,0:T(8,128)(2,1)}, u32[]{:S(2)}, u32[]{:S(2)}) collective-permute-start(bf16[128,2048]{1,0:T(8,128)(2,1)} %get-tuple-element.137), channel_id=1, source_target_pairs={{0,3},{1,2},{2,1},{3,0},{4,7},{5,6},{6,5},{7,4},{8,11},{9,10},{10,... | collective-permute-start | bytes 1572872 | tf_op jit(solution)/shard_map/ppermute | solution.py:487
  603.5 55.0 %all-to-all-start.3 = ((bf16[8,64,2064]{2,1,0:T(8,128)(2,1)}), bf16[8,64,2064]{2,1,0:T(8,128)(2,1)}, u32[]{:S(2)}, u32[]{:S(2)}) async-start(bf16[8,64,2064]{2,1,0:T(8,128)(2,1)} %bitcast.188), calls=%async_computation.5 | async-start | bytes 4456448 | tf_op jit(solution)/shard_map/all_to_all | solution.py:561
  684.1 30.0 %all-to-all-start.2 = ((bf16[8,64,2048]{2,1,0:T(8,128)(2,1)}), bf16[8,64,2048]{2,1,0:T(8,128)(2,1)S(1)}, u32[]{:S(2)}, u32[]{:S(2)}) async-start(bf16[8,64,2048]{2,1,0:T(8,128)(2,1)} %bitcast.191), calls=%async_computation.4 | async-start | bytes 4194304 | tf_op jit(solution)/shard_map/all_to_all | solution.py:561
  (103 other events, 1492.0 us)
Sparse Core Ops, SparseCore 0:
  21.0 82.6 all-gather.11
  105.8 90.2 all-gather.5
  199.8 113.3 all-gather.7
  314.6 53.0 all-gather.9
  386.1 144.2 reduce-scatter.2
  532.6 147.4 reduce-scatter.4

commit v4 on v3

--- a/solution.py
+++ b/solution.py
@@ -273,112 +273,141 @@
 
     taps = taps_ref[...]
     gain = gain_ref[...]
+    conv_slope, facts, spans = [], [], []
+    query_unit, query_factor, key_unit, key_factor, values = [], [], [], [], []
     for r in range(2):
         aux = aux_ref[r]
-        before = halo_ref[r][8:, :].astype(F32)
+        before = halo_ref[r].astype(F32)[8:, :]
         ext[r, :8, :] = jnp.where(first_block, 0.0, before)
         ext[r, 8:, :] = x_ref[r].astype(F32)
-        shifted = lambda lag: ext[r, 8 - lag : 8 - lag + BLOCK, :]
-        conv = convolved(shifted, taps, aux, heads)
-        logistic, conv_slope = slope(conv)
+        conv = convolved(lambda lag: ext[r, 8 - lag : 8 - lag + BLOCK, :], taps, aux, heads)
+        logistic, conv_grad = slope(conv)
+        conv_slope.append(conv_grad)
         act = conv * logistic
-        facts = decays(aux, row, col, heads)
+        facts += decays(aux, row, col, heads)
+        for h in range(heads):
+            spans.append((r, slice(h * VALUE, (h + 1) * VALUE)))
+            normal, factor = unit(act[:, h * KEY : (h + 1) * KEY])
+            query_unit.append(normal)
+            query_factor.append(factor)
+            normal, factor = unit(act[:, hk + h * KEY : hk + (h + 1) * KEY])
+            key_unit.append(normal)
+            key_factor.append(factor)
+            values.append(act[:, 2 * hk + h * VALUE : 2 * hk + (h + 1) * VALUE].astype(LOW))
+    every = range(2 * heads)
+    query = [(q * KEY ** (-0.5)).astype(LOW) for q in query_unit]
+    keys = [k.astype(LOW) for k in key_unit]
+
+    d_out = []
+    for r, vs in spans:
+        mixed = mixed_ref[r, :, vs]
+        gate = gate_ref[r, :, vs]
+        d_branch = d_branch_ref[r, :, vs]
+        factor = lax.rsqrt(jnp.mean(mixed * mixed, axis=1, keepdims=True) + EPS)
+        normed = mixed * factor
+        gate_logistic, gate_slope = slope(gate)
+        d_scaled = d_branch * (gate * gate_logistic)
+        d_gain_ref[...] += jnp.sum(d_scaled * normed, axis=0, keepdims=True)
+        d_all_ref[r, :, chan + vs.start : chan + vs.stop] = (
+            d_branch * normed * gain * gate_slope
+        ).astype(LOW)
+        d_normed = d_scaled * gain
+        d_out.append(
+            factor * (d_normed - normed * jnp.mean(d_normed * normed, axis=1, keepdims=True))
+        )
+
+    pair = [f["pair"] for f in facts]
+    beta = [f["beta_col"] for f in facts]
+    decay = [f["decay_col"] for f in facts]
+    last = [f["last"] for f in facts]
+    inverse = [halves(inv_ref[0, at]) for at in every]
+    old = [state_ref[0, at] for at in every]
+    d_new = [d_state[at] for at in every]
+    out_parts = [halves(d) for d in d_out]
+    d_new_parts = [halves(d) for d in d_new]
+    seen = [product((q,), (k,), 1, 1) * p for q, k, p in zip(query, keys, pair)]
+    carried = [product((k,), d) for k, d in zip(keys, d_new_parts)]
+    d_updates = [
+        product(halves(s), o, 0, 0) + t * c
+        for s, o, t, c in zip(seen, out_parts, last, carried)
+    ]
+    d_targets = [product(i, halves(d), 0, 0) for i, d in zip(inverse, d_updates)]
+    for at in every:
+        d_state[at] = (
+            facts[at]["decay_last"] * d_new[at]
+            + product((query[at],), halves(decay[at] * d_out[at]), 0, 0)
+            - product((keys[at],), halves((beta[at] * decay[at]) * d_targets[at]), 0, 0)
+        )
+
+    updates = [upd_ref[r, :, vs] for r, vs in spans]
+    upd_parts = [halves(u) for u in updates]
+    old_parts = [halves(o) for o in old]
+    target_parts = [halves(d) for d in d_targets]
+    similar = [product((k,), (k,), 1, 1) for k in keys]
+    below_pair = [
+        jnp.where(row > col, -product(t, u, 1, 1), 0.0) * p
+        for t, u, p in zip(target_parts, upd_parts, pair)
+    ]
+    d_seen = [product(o, u, 1, 1) for o, u in zip(out_parts, upd_parts)]
+    target_state = [product(t, o, 1, 1) for t, o in zip(target_parts, old_parts)]
+    out_state = [product(d, o, 1, 1) for d, o in zip(out_parts, old_parts)]
+    d_similar = [halves(b * t) for b, t in zip(below_pair, beta)]
+    d_seen_pair = [halves(d * p) for d, p in zip(d_seen, pair)]
+    d_query = [
+        d * o + product(s, (k,)) for d, o, s, k in zip(decay, out_state, d_seen_pair, keys)
+    ]
+    d_keys = [
+        product(d_similar[at], (keys[at],))
+        + product(d_similar[at], (keys[at],), 0, 0)
+        + product(d_seen_pair[at], (query[at],), 0, 0)
+        + last[at] * product(upd_parts[at], d_new_parts[at], 1, 1)
+        - (beta[at] * decay[at]) * target_state[at]
+        for at in every
+    ]
+
+    for r in range(2):
+        aux = aux_ref[r]
         columns = jnp.zeros((BLOCK, 128), F32)
-        rows = []
+        rows, d_betas = [], []
         d_query_raw, d_key_raw, d_value_raw = [], [], []
-        d_betas = []
         for h in range(heads):
-            f = facts[h]
             at = r * heads + h
-            vs = slice(h * VALUE, (h + 1) * VALUE)
-            query_unit, query_factor = unit(act[:, h * KEY : (h + 1) * KEY])
-            key_unit, key_factor = unit(act[:, hk + h * KEY : hk + (h + 1) * KEY])
-            query = (query_unit * KEY ** (-0.5)).astype(LOW)
-            keys = key_unit.astype(LOW)
-            values = act[:, 2 * hk + h * VALUE : 2 * hk + (h + 1) * VALUE].astype(LOW)
-            mixed = mixed_ref[r, :, vs]
-            gate = gate_ref[r, :, vs]
-            d_branch = d_branch_ref[r, :, vs]
-            factor = lax.rsqrt(jnp.mean(mixed * mixed, axis=1, keepdims=True) + EPS)
-            normed = mixed * factor
-            gate_logistic, gate_slope = slope(gate)
-            d_scaled = d_branch * (gate * gate_logistic)
-            d_gain_ref[...] += jnp.sum(d_scaled * normed, axis=0, keepdims=True)
-            d_all_ref[r, :, chan + h * VALUE : chan + (h + 1) * VALUE] = (
-                d_branch * normed * gain * gate_slope
-            ).astype(LOW)
-            d_normed = d_scaled * gain
-            d_out = factor * (
-                d_normed - normed * jnp.mean(d_normed * normed, axis=1, keepdims=True)
-            )
-            pair, beta, decay = f["pair"], f["beta_col"], f["decay_col"]
-            inverse, updates, old = halves(inv_ref[0, at]), upd_ref[r, :, vs], state_ref[0, at]
-            upd_parts, old_parts, out_parts = halves(updates), halves(old), halves(d_out)
-            d_new = d_state[at]
-            d_new_parts = halves(d_new)
-            similar = product((keys,), (keys,), 1, 1)
-            seen = product((query,), (keys,), 1, 1) * pair
-            carried = product((keys,), d_new_parts)
-            d_updates = product(halves(seen), out_parts, 0, 0) + f["last"] * carried
-            d_targets = product(inverse, halves(d_updates), 0, 0)
-            target_parts = halves(d_targets)
-            below = jnp.where(row > col, -product(target_parts, upd_parts, 1, 1), 0.0)
-            d_seen = product(out_parts, upd_parts, 1, 1)
-            below_pair = below * pair
-            d_similar = halves(below_pair * beta)
-            d_seen_pair = halves(d_seen * pair)
-            target_state = product(target_parts, old_parts, 1, 1)
-            out_state = product(out_parts, old_parts, 1, 1)
-            keys_wide, query_wide = keys.astype(F32), query.astype(F32)
-            d_query = decay * out_state + product(d_seen_pair, (keys,))
-            d_keys = (
-                product(d_similar, (keys,))
-                + product(d_similar, (keys,), 0, 0)
-                + product(d_seen_pair, (query,), 0, 0)
-                + f["last"] * product(upd_parts, d_new_parts, 1, 1)
-                - (beta * decay) * target_state
-            )
-            d_values = beta * d_targets
-            key_target = jnp.sum(keys_wide * target_state, axis=1, keepdims=True)
-            by_beta = below_pair * similar
-            d_beta = (
-                jnp.sum(d_targets * values.astype(F32), axis=1, keepdims=True)
-                - decay * key_target
+            key_target = jnp.sum(keys[at].astype(F32) * target_state[at], axis=1, keepdims=True)
+            by_beta = below_pair[at] * similar[at]
+            d_betas.append(
+                jnp.sum(d_targets[at] * values[at].astype(F32), axis=1, keepdims=True)
+                - decay[at] * key_target
                 + jnp.sum(by_beta, axis=1, keepdims=True)
             )
-            d_pair = by_beta * beta + d_seen * seen
-            d_decay = jnp.sum(query_wide * out_state, axis=1, keepdims=True) - beta * key_target
-            d_last = f["last"] * jnp.sum(updates * carried, axis=1, keepdims=True)
-            at_last = jnp.sum(d_last, axis=0, keepdims=True) + f["decay_last"] * jnp.sum(
-                jnp.sum(d_new * old, axis=1, keepdims=True), axis=0, keepdims=True
+            d_pair = by_beta * beta[at] + d_seen[at] * seen[at]
+            d_decay = (
+                jnp.sum(query[at].astype(F32) * out_state[at], axis=1, keepdims=True)
+                - beta[at] * key_target
+            )
+            d_last = last[at] * jnp.sum(updates[at] * carried[at], axis=1, keepdims=True)
+            at_last = jnp.sum(d_last, axis=0, keepdims=True) + facts[at]["decay_last"] * jnp.sum(
+                jnp.sum(d_new[at] * old[at], axis=1, keepdims=True), axis=0, keepdims=True
             )
             d_sums = (
                 jnp.sum(d_pair, axis=1, keepdims=True)
-                + decay * d_decay
+                + decay[at] * d_decay
                 - d_last
                 + jnp.where(position == BLOCK - 1, at_last, 0.0)
             )
             columns = jnp.where(lane == h, d_sums, columns)
             rows.append(jnp.sum(d_pair, axis=0, keepdims=True))
-            d_betas.append(d_beta)
-            d_state[at] = (
-                f["decay_last"] * d_new
-                + product((query,), halves(decay * d_out), 0, 0)
-                - product((keys,), halves((beta * decay) * d_targets), 0, 0)
-            )
-            d_query = d_query.astype(LOW).astype(F32) * KEY ** (-0.5)
-            d_keys = d_keys.astype(LOW).astype(F32)
+            d_unit = d_query[at].astype(LOW).astype(F32) * KEY ** (-0.5)
             d_query_raw.append(
-                query_factor
-                * (d_query - query_unit * jnp.sum(d_query * query_unit, axis=1, keepdims=True))
-            )
+                query_factor[at]
+                * (d_unit - query_unit[at] * jnp.sum(d_unit * query_unit[at], axis=1, keepdims=True))
+            )
+            d_unit = d_keys[at].astype(LOW).astype(F32)
             d_key_raw.append(
-                key_factor * (d_keys - key_unit * jnp.sum(d_keys * key_unit, axis=1, keepdims=True))
-            )
-            d_value_raw.append(d_values.astype(LOW).astype(F32))
-        turned = jnp.concatenate(
-            rows + [jnp.zeros((128 - heads, BLOCK), F32)], axis=0
-        ).T
+                key_factor[at]
+                * (d_unit - key_unit[at] * jnp.sum(d_unit * key_unit[at], axis=1, keepdims=True))
+            )
+            d_value_raw.append((beta[at] * d_targets[at]).astype(LOW).astype(F32))
+        turned = jnp.concatenate(rows + [jnp.zeros((128 - heads, BLOCK), F32)], axis=0).T
         upper = (row <= col).astype(LOW)
         d_aux = product((upper,), thirds(columns - turned))
         for h in range(heads):
@@ -387,13 +416,13 @@
         d_all_ref[r, :, chan + hv :] = d_rate.astype(LOW)
         d_rate_ref[0:1, :] += jnp.sum(d_aux * aux, axis=0, keepdims=True)
         d_rate_ref[1:2, :] += jnp.sum(d_rate, axis=0, keepdims=True)
-        d_conv = jnp.concatenate(d_query_raw + d_key_raw + d_value_raw, axis=1) * conv_slope
+        d_conv = jnp.concatenate(d_query_raw + d_key_raw + d_value_raw, axis=1) * conv_slope[r]
         d_ext_sum = taps[CONV - 1 : CONV, :] * d_conv
-        d_taps_ref[CONV - 1 : CONV, :] += jnp.sum(d_conv * shifted(0), axis=0, keepdims=True)
+        d_taps_ref[CONV - 1 : CONV, :] += jnp.sum(d_conv * ext[r, 8:, :], axis=0, keepdims=True)
         for lag in range(1, CONV):
             masked = d_conv * aux[:, 2 * heads + lag : 2 * heads + lag + 1]
             d_taps_ref[CONV - 1 - lag : CONV - lag, :] += jnp.sum(
-                masked * shifted(lag), axis=0, keepdims=True
+                masked * ext[r, 8 - lag : 8 - lag + BLOCK, :], axis=0, keepdims=True
             )
             slot = r * (CONV - 1) + lag - 1
             d_ext[slot, :BLOCK, :] = masked
@@ -744,7 +773,7 @@
     downs = [w[:, 2 * w.shape[1] // 3 :] for w in ffn]
     d_both = after(d_both, grad_ffn)
     grad_ffn = shard_sum(grad_ffn)
-    d_second = block_sum(row_sum(d_both, ups), False)
+    d_second = block_sum(row_sum(d_both, ups, None, F32), False)
     grad_gain_two = jnp.sum(d_second * normed_two, axis=0)
     d_hidden = grad_out[0].astype(jnp.float32) + norm_back(
         normed_two, scale_two, d_second * ffn_norm_gain
@@ -783,13 +812,19 @@
         [mix_in, gate_in, jnp.pad(rate_in.T, ((0, 0), (0, 128 - 2 * heads)))], axis=1
     )
     row_first = row_sum([d_all], [whole_in])
-    grad_proj = contract_tokens(first_in, d_all[:, : chan + hv]).astype(jnp.bfloat16)
-    grad_proj = jnp.concatenate(
-        [grad_proj, contract_tokens(d_mix, branch).astype(jnp.bfloat16)], axis=1
-    )
-    grad_proj, grad_ffn, row_first = lax.optimization_barrier((grad_proj, grad_ffn, row_first))
+    grad_most = jnp.concatenate(
+        [
+            contract_tokens(first_in, d_all[:, 2 * hk : chan + hv]).astype(jnp.bfloat16),
+            contract_tokens(d_mix, branch).astype(jnp.bfloat16),
+        ],
+        axis=1,
+    )
+    grad_most, grad_ffn, row_first = lax.optimization_barrier((grad_most, grad_ffn, row_first))
     d_first = block_sum(row_first, True)
-    grad_proj = shard_sum(grad_proj)
+    grad_most = shard_sum(grad_most)
+    grad_last = contract_tokens(first_in, d_all[:, : 2 * hk]).astype(jnp.bfloat16)
+    grad_last = to_holders(shard_sum(after(grad_last, grad_most)), split)
+    grad_most = to_holders(grad_most, split)
     grad_ffn = to_holders(grad_ffn, split)
     def hidden_columns(at):
         first, second = grad_ffn[:, :, : 3 * cut], grad_ffn[:, :, 3 * cut :]
@@ -832,13 +867,12 @@
     sums = all_sum(jnp.concatenate([grad_gain_one, grad_gain_two, grad_head_gain[0]]))
     d_row = d_hidden + norm_back(normed, scale, d_first * norm_gain)
     d_row = d_row.astype(jnp.bfloat16)
-    holders_proj = to_holders(grad_proj, split)
     grad_proj = jnp.concatenate(
         [
-            holders_proj[:, :, :hk].reshape(rows, HK),
-            holders_proj[:, :, hk : 2 * hk].reshape(rows, HK),
-            holders_proj[:, :, 2 * hk : chan].reshape(rows, HV),
-            holders_proj[:, :, chan : chan + hv].reshape(rows, HV),
+            grad_last[:, :, :hk].reshape(rows, HK),
+            grad_last[:, :, hk:].reshape(rows, HK),
+            grad_most[:, :, :hv].reshape(rows, HV),
+            grad_most[:, :, hv : 2 * hv].reshape(rows, HV),
         ],
         axis=1,
     )
@@ -853,7 +887,7 @@
         rate_sums[:, 0, :heads].reshape(HEADS),
         rate_sums[:, 1, :heads].reshape(HEADS),
         sums[2 * width :],
-        holders_proj[:, :, chan + hv :].reshape(rows, HV),
+        grad_most[:, :, 2 * hv :].reshape(rows, HV),
         sums[width : 2 * width],
         grad_gate_up,
         grad_down,

time: 734 us -> 733 us (level)
  waiting for transfers between devices: 224 us -> 233 us
  local copies, waits for them, and re-layouts: 129 us -> 121 us
    dot_general x6 -> x7, matrix products: 39 us -> 41.5 us  [contract_tokens(): lax.dot_general(left, right, (((0,), (0,)), ((), ())), preferred_element_...]
    unnamed x141 -> x147, local copies, waits for them, and re-layouts: 14.9 us -> 14.8 us
  transfers between devices with their start and end apart: 75 -> 77, of which waited for: 36 -> 41; matrix products, arithmetic and copies ran while one was open for 37% -> 36% of each run, Pallas kernels for 7% -> 7%
where the time goes in v4:
time: 733 us; the launch traced here: 725 us
  waiting for transfers between devices  233 us (32%)
  matrix products  137 us (19%)
  local copies, waits for them, and re-layouts  121 us (17%)
  starting transfers between devices  87.5 us (12%)
  Pallas kernels  48.5 us (7%)
  blocking collectives  42.4 us (6%)
  other arithmetic  39.6 us (5%)
  between operations  16 us (2%)
    ppermute x44, waiting for transfers between devices, from_peer(): lax.ppermute(x, axis, [(i, i ^ distance) for i in range(lax.axis_size(axi...  168 us
    ppermute x44, starting transfers between devices, from_peer(): lax.ppermute(x, axis, [(i, i ^ distance) for i in range(lax.axis_size(axi...  64.9 us
    dot_general x13, matrix products, contract_rows(): lax.dot_general(left, right, (((1,), (1,)), ((), ())), preferred_element_...  50.4 us
    all_to_all x1, blocking collectives, plane_exchange(): got = lax.all_to_all(blocks, PLANE, 0, 0)  42.4 us
    dot_general x7, matrix products, contract_tokens(): lax.dot_general(left, right, (((0,), (0,)), ((), ())), preferred_element_...  41.5 us
    pallas_call x1, Pallas kernels, mix_back(): pl.pallas_call(functools.partial(mix_back_kernel, heads), grid=(count,),...  28.3 us
    pallas_call x1, Pallas kernels, mix(): pl.pallas_call(functools.partial(mix_kernel, heads), grid=(count,), in_sp...  20.2 us
    all_to_all x1, waiting for transfers between devices, on_device(): mix_in = lax.all_to_all(jnp.swapaxes(mix_in, 0, 1), PLANE, 0, 0)  15.2 us
  transfers between devices with their start and end apart: 77, of which 41 were waited for; matrix products, arithmetic and copies ran while one was open for 36% of the time, Pallas kernels for 7%

profile of v4, /device:TPU:0, one launch (start us, length us, event | category | flops | bytes accessed | tf_op | source)
XLA Modules:
  0.0 724.6 jit_solution(11613393947344362138)
XLA Ops:
  53.3 42.4 %all_to_all.25 = bf16[8,64,3092]{2,1,0:T(8,128)(2,1)} all-to-all(bf16[8,64,3092]{2,1,0:T(8,128)(2,1)S(1)} %concatenate.78), channel_id=1, replica_groups=mesh['z'=4,'core'=2,'seq'=4] {'core','seq'}, dimensions={0} | all-to-all | bytes 6332416 | tf_op jit(solution)/shard_map/all_to_all | solution.py:577
  146.5 15.2 %all-to-all-done = bf16[8,4,64,1024]{3,2,1,0:T(8,128)(2,1)} async-done(((bf16[8,4,64,1024]{3,2,1,0:T(8,128)(2,1)}), bf16[8,4,64,1024]{3,2,1,0:T(8,128)(2,1)}, u32[]{:S(2)}, u32[]{:S(2)}) %all-to-all-start) | async-done | bytes 4194336 | tf_op jit(solution)/shard_map/all_to_all | solution.py:686
  164.4 9.4 %convolution_convert_fusion.8 = bf16[1024,1024]{1,0:T(8,128)(2,1)} fusion(bf16[1024,2048]{1,0:T(8,128)(2,1)} %constant_dynamic-update-slice_fusion.28, bf16[2048,1024]{1,0:T(8,128)(2,1)S(1)} %bitcast.201), kind=kOutput, calls=%fused_computation.39 | convolution fusion | flops 4296015872 | bytes 10485760 | tf_op jit(solution)/shard_map/dot_general | solution.py:723
  173.8 20.2 %mix_forward.1 = (f32[2,512,512]{2,1,0:T(8,128)S(1)}, f32[4,4,128,128]{3,2,1,0:T(8,128)S(1)}, f32[2,512,512]{2,1,0:T(8,128)}, f32[4,4,128,256]{3,2,1,0:T(8,128)}, f32[4,256,128]{2,1,0:T(8,128)S(1)}) custom-call(bf16[2,512,1024]{2,1,0:T(8,128)(2,1)} %bitcast.185, f32[4,1024]{1,0:T(4,128)S(1)} %pad_maximum_fusion.14.taps_ref, f32[2,512,128]{2,1,0:T(8,128)S(1)} %pad.27.aux_ref), custom_call_target="tpu_custom_call" | custom-call | flops 1000000 | bytes 1000000 | tf_op jit(solution)/shard_map/mix_forward/pallas_call | solution.py:195
  203.7 5.9 fusion.112
  214.7 11.2 %collective-permute-done.12 = bf16[128,2048]{1,0:T(8,128)(2,1)S(1)} collective-permute-done((bf16[128,2048]{1,0:T(8,128)(2,1)}, bf16[128,2048]{1,0:T(8,128)(2,1)S(1)}, u32[]{:S(2)}, u32[]{:S(2)}) %collective-permute-start.12) | collective-permute-done | bytes 524320 | tf_op jit(solution)/shard_map/ppermute | solution.py:516
  232.3 7.3 %collective-permute-done.18 = f32[512,2048]{1,0:T(8,128)} collective-permute-done((f32[512,2048]{1,0:T(8,128)}, f32[512,2048]{1,0:T(8,128)}, u32[]{:S(2)}, u32[]{:S(2)}) %collective-permute-start.18) | collective-permute-done | bytes 4194336 | tf_op jit(solution)/shard_map/ppermute | solution.py:512
  252.0 18.3 %collective-permute-done.19 = f32[128,2048]{1,0:T(8,128)S(1)} collective-permute-done((f32[128,2048]{1,0:T(8,128)S(1)}, f32[128,2048]{1,0:T(8,128)S(1)}, u32[]{:S(2)}, u32[]{:S(2)}) %collective-permute-start.19) | collective-permute-done | bytes 1048608 | tf_op jit(solution)/shard_map/ppermute | solution.py:516
  270.2 22.9 %collective-permute-done.20 = f32[128,2048]{1,0:T(8,128)S(1)} collective-permute-done((f32[128,2048]{1,0:T(8,128)S(1)}, f32[128,2048]{1,0:T(8,128)S(1)}, u32[]{:S(2)}, u32[]{:S(2)}) %collective-permute-start.20) | collective-permute-done | bytes 1048608 | tf_op jit(solution)/shard_map/ppermute | solution.py:516
  300.6 8.8 %collective-permute-done.22 = bf16[128,2048]{1,0:T(8,128)(2,1)S(1)} collective-permute-done((bf16[128,2048]{1,0:T(8,128)(2,1)S(1)}, bf16[128,2048]{1,0:T(8,128)(2,1)S(1)}, u32[]{:S(2)}, u32[]{:S(2)}) %collective-permute-start.22) | collective-permute-done | bytes 524320 | tf_op jit(solution)/shard_map/ppermute | solution.py:516
  310.3 9.3 %collective-permute-done.23 = bf16[128,2048]{1,0:T(8,128)(2,1)S(1)} collective-permute-done((bf16[128,2048]{1,0:T(8,128)(2,1)S(1)}, bf16[128,2048]{1,0:T(8,128)(2,1)S(1)}, u32[]{:S(2)}, u32[]{:S(2)}) %collective-permute-start.23) | collective-permute-done | bytes 524320 | tf_op jit(solution)/shard_map/ppermute | solution.py:516
  325.2 7.6 %fusion.6 = f32[1024,1024]{0,1:T(8,128)S(1)} fusion(bf16[1024,2048]{1,0:T(8,128)(2,1)} %constant_dynamic-update-slice_fusion.8, bf16[2048,1536]{1,0:T(8,128)(2,1)} %all-gather.8.cloned.1.call-done), kind=kOutput, calls=%fused_computation.18 | convolution fusion | flops 4294967296 | bytes 12582912 | tf_op jit(solution)/shard_map/dot_general | solution.py:755
  332.9 6.0 multiply_convert_fusion.2
  338.9 9.1 %convolution_convert_fusion = bf16[2048,1024]{0,1:T(8,128)(2,1)S(1)} fusion(bf16[1024,2048]{1,0:T(8,128)(2,1)} %constant_dynamic-update-slice_fusion.8, bf16[1024,512]{0,1:T(8,128)(2,1)S(1)} %get-tuple-element.124, bf16[1024,512]{0,1:T(8,128)(2,1)S(1)} %get-tuple-element.123), kind=kOutput, calls=%fused_computation.10 | convolution fusion | flops 4301258752 | bytes 10485760 | tf_op jit(solution)/shard_map/dot_general | solution.py:497
  352.3 5.9 fusion.8
  358.2 9.3 %all-gather.10.cloned.1.call-done = bf16[2048,528]{1,0:T(8,128)(2,1)} async-done(((bf16[512,528]{1,0:T(8,128)(2,1)}), bf16[2048,528]{1,0:T(8,128)(2,1)}) %all-gather.10.cloned.1.call-update) | async-done | bytes 2162704 | tf_op jit(solution)/shard_map/all_gather | solution.py:582
  389.2 5.5 fusion.2
  408.3 11.3 %collective-permute-done.30 = bf16[128,2048]{1,0:T(8,128)(2,1)S(1)} collective-permute-done((bf16[128,2048]{1,0:T(8,128)(2,1)S(1)}, bf16[128,2048]{1,0:T(8,128)(2,1)S(1)}, u32[]{:S(2)}, u32[]{:S(2)}) %collective-permute-start.30) | collective-permute-done | bytes 524320 | tf_op jit(solution)/shard_map/ppermute | solution.py:516
  419.5 11.4 %collective-permute-done.31 = bf16[128,2048]{1,0:T(8,128)(2,1)S(1)} collective-permute-done((bf16[128,2048]{1,0:T(8,128)(2,1)S(1)}, bf16[128,2048]{1,0:T(8,128)(2,1)S(1)}, u32[]{:S(2)}, u32[]{:S(2)}) %collective-permute-start.31) | collective-permute-done | bytes 524320 | tf_op jit(solution)/shard_map/ppermute | solution.py:516
  439.8 7.6 %collective-permute-done.33 = bf16[128,2048]{1,0:T(8,128)(2,1)S(1)} collective-permute-done((bf16[128,2048]{1,0:T(8,128)(2,1)S(1)}, bf16[128,2048]{1,0:T(8,128)(2,1)S(1)}, u32[]{:S(2)}, u32[]{:S(2)}) %collective-permute-start.33) | collective-permute-done | bytes 524320 | tf_op jit(solution)/shard_map/ppermute | solution.py:516
  447.4 11.6 %collective-permute-done.34 = bf16[128,2048]{1,0:T(8,128)(2,1)S(1)} collective-permute-done((bf16[128,2048]{1,0:T(8,128)(2,1)S(1)}, bf16[128,2048]{1,0:T(8,128)(2,1)S(1)}, u32[]{:S(2)}, u32[]{:S(2)}) %collective-permute-start.34) | collective-permute-done | bytes 524320 | tf_op jit(solution)/shard_map/ppermute | solution.py:516
  465.7 28.3 %mix_backward.1 = (bf16[2,512,1664]{2,1,0:T(8,128)(2,1)}, f32[4,1024]{1,0:T(4,128)S(1)}, f32[1,256]{1,0:T(1,128)S(1)}, f32[8,128]{1,0:T(8,128)S(1)}) custom-call(bf16[2,512,1024]{2,1,0:T(8,128)(2,1)S(1)} %bitcast.186, bf16[2,512,1024]{2,1,0:T(8,128)(2,1)S(1)} %bitcast.187, f32[4,1024]{1,0:T(4,128)S(1)} %pad_maximum_fusion.14.taps_ref, ...), custom_call_target="tpu_custom_call" | custom-call | flops 1000000 | bytes 1000000 | tf_op jit(solution)/shard_map/mix_backward/pallas_call | solution.py:446
  494.0 7.1 convolution_convert_fusion.5
  505.0 7.4 %convolution_convert_fusion.1 = bf16[2048,1024]{0,1:T(8,128)(2,1)S(1)} fusion(bf16[1024,2048]{1,0:T(8,128)(2,1)} %constant_dynamic-update-slice_fusion.28, bf16[1024,1664]{1,0:T(8,128)(2,1)S(1)} %bitcast.240), kind=kOutput, calls=%fused_computation.11 | convolution fusion | flops 4297064448 | bytes 10485760 | tf_op jit(solution)/shard_map/dot_general | solution.py:497
  515.9 8.4 %convert_add_fusion.1 = f32[512,2048]{1,0:T(8,128)} fusion(bf16[512,2048]{1,0:T(8,128)(2,1)} %collective-permute-done.40, bf16[2,512,1664]{2,1,0:T(8,128)(2,1)} %get-tuple-element.95, bf16[2048,4]{1,0:T(8,128)(2,1)S(1)} %bitcast.214, bf16[2048,512]{1,0:T(8,128)(2,1)} %slice.360, bf16[2048,1024]{1,0:T(8,128)(2,1)} %bitcast.202), kind=kOutput, calls=%fused_computation.7 | convolution fusion | flops 3519021056 | bytes 14303232 | tf_op jit(solution)/shard_map/dot_general | solution.py:491
  524.2 6.0 reduce-scatter.4.cloned.1.call-done
  542.6 6.2 convolution_convert_fusion.3
  594.9 9.8 %collective-permute-done.46 = bf16[128,2048]{1,0:T(8,128)(2,1)S(1)} collective-permute-done((bf16[128,2048]{1,0:T(8,128)(2,1)S(1)}, bf16[128,2048]{1,0:T(8,128)(2,1)S(1)}, u32[]{:S(2)}, u32[]{:S(2)}) %collective-permute-start.46) | collective-permute-done | bytes 524320 | tf_op jit(solution)/shard_map/ppermute | solution.py:516
  616.3 11.7 %collective-permute-done.43 = bf16[128,2048]{1,0:T(8,128)(2,1)} collective-permute-done((bf16[128,2048]{1,0:T(8,128)(2,1)}, bf16[128,2048]{1,0:T(8,128)(2,1)}, u32[]{:S(2)}, u32[]{:S(2)}) %collective-permute-start.43) | collective-permute-done | bytes 524320 | tf_op jit(solution)/shard_map/ppermute | solution.py:516
  631.5 11.0 %collective-permute-start.52 = (f32[4352]{0:T(1024)S(1)}, f32[4352]{0:T(1024)S(1)}, u32[]{:S(2)}, u32[]{:S(2)}) collective-permute-start(f32[4352]{0:T(1024)S(1)} %pad_maximum_fusion.13), channel_id=1, source_target_pairs={{0,1},{1,0},{2,3},{3,2},{4,5},{5,4},{6,7},{7,6},{8,9},{9,8},{10,11... | collective-permute-start | bytes 52232 | tf_op jit(solution)/shard_map/ppermute | solution.py:516
  696.6 5.8 reduce-scatter.8.cloned.1.call-done
  709.6 5.8 all-to-all-done.2
  (473 shorter events, 344.8 us)
Async XLA Ops:
  7.2 96.4 %all-gather.12.cloned.1.call-start = ((), (), s32[]{:S(2)}) async-start(), calls=%async_computation.14 | async-start | bytes 5242880 | tf_op jit(solution)/shard_map/all_gather | solution.py:655
  14.8 23.3 %collective-permute-start = (bf16[128,2048]{1,0:T(8,128)(2,1)}, bf16[128,2048]{1,0:T(8,128)(2,1)}, u32[]{:S(2)}, u32[]{:S(2)}) collective-permute-start(bf16[128,2048]{1,0:T(8,128)(2,1)} %get-tuple-element.122), channel_id=1, source_target_pairs={{0,1},{1,0},{2,3},{3,2},{4,5},{5,4},{6,7},{7,6},{8,9},{9,8},{10,11... | collective-permute-start | bytes 1572872 | tf_op jit(solution)/shard_map/ppermute | solution.py:516
  17.7 24.9 %collective-permute-start.1 = (bf16[128,2048]{1,0:T(8,128)(2,1)}, bf16[128,2048]{1,0:T(8,128)(2,1)}, u32[]{:S(2)}, u32[]{:S(2)}) collective-permute-start(bf16[128,2048]{1,0:T(8,128)(2,1)} %get-tuple-element.122), channel_id=1, source_target_pairs={{0,2},{1,3},{2,0},{3,1},{4,6},{5,7},{6,4},{7,5},{8,10},{9,11},{10,... | collective-permute-start | bytes 1572872 | tf_op jit(solution)/shard_map/ppermute | solution.py:516
  19.2 23.5 %collective-permute-start.2 = (bf16[128,2048]{1,0:T(8,128)(2,1)}, bf16[128,2048]{1,0:T(8,128)(2,1)}, u32[]{:S(2)}, u32[]{:S(2)}) collective-permute-start(bf16[128,2048]{1,0:T(8,128)(2,1)} %get-tuple-element.122), channel_id=1, source_target_pairs={{0,3},{1,2},{2,1},{3,0},{4,7},{5,6},{6,5},{7,4},{8,11},{9,10},{10,... | collective-permute-start | bytes 1572872 | tf_op jit(solution)/shard_map/ppermute | solution.py:516
  19.2 29.7 %collective-permute-start.3 = (bf16[128,2048]{1,0:T(8,128)(2,1)}, bf16[128,2048]{1,0:T(8,128)(2,1)}, u32[]{:S(2)}, u32[]{:S(2)}) collective-permute-start(bf16[128,2048]{1,0:T(8,128)(2,1)} %get-tuple-element.122), channel_id=1, source_target_pairs={{0,4},{4,0},{1,5},{5,1},{2,6},{6,2},{3,7},{7,3},{8,12},{12,8},{9,1... | collective-permute-start | bytes 1572872 | tf_op jit(solution)/shard_map/ppermute | solution.py:512
  20.8 175.3 %all-gather.6.cloned.1.call-start = ((), (), s32[]{:S(2)}) async-start(), calls=%async_computation.8 | async-start | bytes 5242880 | tf_op jit(solution)/shard_map/all_gather | solution.py:582
  108.5 53.2 %all-to-all-start = ((bf16[8,4,64,1024]{3,2,1,0:T(8,128)(2,1)}), bf16[8,4,64,1024]{3,2,1,0:T(8,128)(2,1)}, u32[]{:S(2)}, u32[]{:S(2)}) async-start(bf16[8,4,64,1024]{3,2,1,0:T(8,128)(2,1)} %bitcast.191), calls=%async_computation | async-start | bytes 8388608 | tf_op jit(solution)/shard_map/all_to_all | solution.py:686
  113.1 212.1 %all-gather.8.cloned.1.call-start = ((), (), s32[]{:S(2)}) async-start(), calls=%async_computation.9 | async-start | bytes 7864320 | tf_op jit(solution)/shard_map/all_gather | solution.py:582
  199.5 168.0 %all-gather.10.cloned.1.call-start = ((), (), s32[]{:S(2)}) async-start(), calls=%async_computation.10 | async-start | bytes 3276800 | tf_op jit(solution)/shard_map/all_gather | solution.py:582
  200.9 25.0 %collective-permute-start.12 = (bf16[128,2048]{1,0:T(8,128)(2,1)}, bf16[128,2048]{1,0:T(8,128)(2,1)S(1)}, u32[]{:S(2)}, u32[]{:S(2)}) collective-permute-start(bf16[128,2048]{1,0:T(8,128)(2,1)} %bitcast.197), channel_id=1, source_target_pairs={{0,2},{1,3},{2,0},{3,1},{4,6},{5,7},{6,4},{7,5},{8,10},{9,11},{10,... | collective-permute-start | bytes 1572872 | tf_op jit(solution)/shard_map/ppermute | solution.py:516
  202.4 23.6 %collective-permute-start.13 = (bf16[128,2048]{1,0:T(8,128)(2,1)}, bf16[128,2048]{1,0:T(8,128)(2,1)S(1)}, u32[]{:S(2)}, u32[]{:S(2)}) collective-permute-start(bf16[128,2048]{1,0:T(8,128)(2,1)} %bitcast.198), channel_id=1, source_target_pairs={{0,3},{1,2},{2,1},{3,0},{4,7},{5,6},{6,5},{7,4},{8,11},{9,10},{10,... | collective-permute-start | bytes 1572872 | tf_op jit(solution)/shard_map/ppermute | solution.py:516
  203.3 23.9 %collective-permute-start.14 = (bf16[128,2048]{1,0:T(8,128)(2,1)}, bf16[128,2048]{1,0:T(8,128)(2,1)S(1)}, u32[]{:S(2)}, u32[]{:S(2)}) collective-permute-start(bf16[128,2048]{1,0:T(8,128)(2,1)} %bitcast.199), channel_id=1, source_target_pairs={{0,4},{4,0},{1,5},{5,1},{2,6},{6,2},{3,7},{7,3},{8,12},{12,8},{9,1... | collective-permute-start | bytes 1572872 | tf_op jit(solution)/shard_map/ppermute | solution.py:512
  232.2 298.0 %reduce-scatter.4.cloned.1.call-start = ((), (), s32[]{:S(2)}) async-start(), calls=%async_computation.11 | async-start | bytes 10567680 | tf_op jit(solution)/shard_map/reduce_scatter | solution.py:586
  244.1 26.1 %collective-permute-start.19 = (f32[128,2048]{1,0:T(8,128)S(1)}, f32[128,2048]{1,0:T(8,128)S(1)}, u32[]{:S(2)}, u32[]{:S(2)}) collective-permute-start(f32[128,2048]{1,0:T(8,128)S(1)} %get-tuple-element.137), channel_id=1, source_target_pairs={{0,1},{1,0},{2,3},{3,2},{4,5},{5,4},{6,7},{7,6},{8,9},{9,8},{10,11... | collective-permute-start | bytes 3145736 | tf_op jit(solution)/shard_map/ppermute | solution.py:516
  245.7 47.4 %collective-permute-start.20 = (f32[128,2048]{1,0:T(8,128)S(1)}, f32[128,2048]{1,0:T(8,128)S(1)}, u32[]{:S(2)}, u32[]{:S(2)}) collective-permute-start(f32[128,2048]{1,0:T(8,128)S(1)} %get-tuple-element.139), channel_id=1, source_target_pairs={{0,2},{1,3},{2,0},{3,1},{4,6},{5,7},{6,4},{7,5},{8,10},{9,11},{10,... | collective-permute-start | bytes 3145736 | tf_op jit(solution)/shard_map/ppermute | solution.py:516
  245.7 47.4 %collective-permute-start.21 = (f32[128,2048]{1,0:T(8,128)S(1)}, f32[128,2048]{1,0:T(8,128)S(1)}, u32[]{:S(2)}, u32[]{:S(2)}) collective-permute-start(f32[128,2048]{1,0:T(8,128)S(1)} %get-tuple-element.138), channel_id=1, source_target_pairs={{0,3},{1,2},{2,1},{3,0},{4,7},{5,6},{6,5},{7,4},{8,11},{9,10},{10,... | collective-permute-start | bytes 3145736 | tf_op jit(solution)/shard_map/ppermute | solution.py:516
  296.0 23.6 %collective-permute-start.23 = (bf16[128,2048]{1,0:T(8,128)(2,1)S(1)}, bf16[128,2048]{1,0:T(8,128)(2,1)S(1)}, u32[]{:S(2)}, u32[]{:S(2)}) collective-permute-start(bf16[128,2048]{1,0:T(8,128)(2,1)S(1)} %get-tuple-element.118), channel_id=1, source_target_pairs={{0,2},{1,3},{2,0},{3,1},{4,6},{5,7},{6,4},{7,5},{8,10},{9,11},{10,... | collective-permute-start | bytes 1572872 | tf_op jit(solution)/shard_map/ppermute | solution.py:516
  298.0 22.5 %collective-permute-start.24 = (bf16[128,2048]{1,0:T(8,128)(2,1)S(1)}, bf16[128,2048]{1,0:T(8,128)(2,1)S(1)}, u32[]{:S(2)}, u32[]{:S(2)}) collective-permute-start(bf16[128,2048]{1,0:T(8,128)(2,1)S(1)} %get-tuple-element.118), channel_id=1, source_target_pairs={{0,3},{1,2},{2,1},{3,0},{4,7},{5,6},{6,5},{7,4},{8,11},{9,10},{10,... | collective-permute-start | bytes 1572872 | tf_op jit(solution)/shard_map/ppermute | solution.py:516
  385.8 273.3 %reduce-scatter.6.cloned.1.call-start = ((), (), s32[]{:S(2)}) async-start(), calls=%async_computation.12 | async-start | bytes 7864320 | tf_op jit(solution)/shard_map/reduce_scatter | solution.py:586
  406.0 24.9 %collective-permute-start.31 = (bf16[128,2048]{1,0:T(8,128)(2,1)S(1)}, bf16[128,2048]{1,0:T(8,128)(2,1)S(1)}, u32[]{:S(2)}, u32[]{:S(2)}) collective-permute-start(bf16[128,2048]{1,0:T(8,128)(2,1)S(1)} %get-tuple-element.156), channel_id=1, source_target_pairs={{0,2},{1,3},{2,0},{3,1},{4,6},{5,7},{6,4},{7,5},{8,10},{9,11},{10,... | collective-permute-start | bytes 1572872 | tf_op jit(solution)/shard_map/ppermute | solution.py:516
  407.5 23.5 %collective-permute-start.32 = (bf16[128,2048]{1,0:T(8,128)(2,1)S(1)}, bf16[128,2048]{1,0:T(8,128)(2,1)S(1)}, u32[]{:S(2)}, u32[]{:S(2)}) collective-permute-start(bf16[128,2048]{1,0:T(8,128)(2,1)S(1)} %get-tuple-element.155), channel_id=1, source_target_pairs={{0,3},{1,2},{2,1},{3,0},{4,7},{5,6},{6,5},{7,4},{8,11},{9,10},{10,... | collective-permute-start | bytes 1572872 | tf_op jit(solution)/shard_map/ppermute | solution.py:516
  434.8 24.3 %collective-permute-start.34 = (bf16[128,2048]{1,0:T(8,128)(2,1)S(1)}, bf16[128,2048]{1,0:T(8,128)(2,1)S(1)}, u32[]{:S(2)}, u32[]{:S(2)}) collective-permute-start(bf16[128,2048]{1,0:T(8,128)(2,1)S(1)} %get-tuple-element.115), channel_id=1, source_target_pairs={{0,2},{1,3},{2,0},{3,1},{4,6},{5,7},{6,4},{7,5},{8,10},{9,11},{10,... | collective-permute-start | bytes 1572872 | tf_op jit(solution)/shard_map/ppermute | solution.py:516
  435.7 23.4 %collective-permute-start.35 = (bf16[128,2048]{1,0:T(8,128)(2,1)S(1)}, bf16[128,2048]{1,0:T(8,128)(2,1)S(1)}, u32[]{:S(2)}, u32[]{:S(2)}) collective-permute-start(bf16[128,2048]{1,0:T(8,128)(2,1)S(1)} %get-tuple-element.115), channel_id=1, source_target_pairs={{0,3},{1,2},{2,1},{3,0},{4,7},{5,6},{6,5},{7,4},{8,11},{9,10},{10,... | collective-permute-start | bytes 1572872 | tf_op jit(solution)/shard_map/ppermute | solution.py:516
  549.0 24.7 %collective-permute-start.44 = (bf16[512,2048]{1,0:T(8,128)(2,1)}, bf16[512,2048]{1,0:T(8,128)(2,1)}, u32[]{:S(2)}, u32[]{:S(2)}) collective-permute-start(bf16[512,2048]{1,0:T(8,128)(2,1)} %add_convert_fusion), channel_id=1, source_target_pairs={{0,4},{4,0},{1,5},{5,1},{2,6},{6,2},{3,7},{7,3},{8,12},{12,8},{9,1... | collective-permute-start | bytes 6291464 | tf_op jit(solution)/shard_map/ppermute | solution.py:512
  579.2 25.4 %collective-permute-start.46 = (bf16[128,2048]{1,0:T(8,128)(2,1)S(1)}, bf16[128,2048]{1,0:T(8,128)(2,1)S(1)}, u32[]{:S(2)}, u32[]{:S(2)}) collective-permute-start(bf16[128,2048]{1,0:T(8,128)(2,1)S(1)} %get-tuple-element.153), channel_id=1, source_target_pairs={{0,2},{1,3},{2,0},{3,1},{4,6},{5,7},{6,4},{7,5},{8,10},{9,11},{10,... | collective-permute-start | bytes 1572872 | tf_op jit(solution)/shard_map/ppermute | solution.py:516
  580.6 24.9 %collective-permute-start.47 = (bf16[128,2048]{1,0:T(8,128)(2,1)S(1)}, bf16[128,2048]{1,0:T(8,128)(2,1)S(1)}, u32[]{:S(2)}, u32[]{:S(2)}) collective-permute-start(bf16[128,2048]{1,0:T(8,128)(2,1)S(1)} %get-tuple-element.152), channel_id=1, source_target_pairs={{0,3},{1,2},{2,1},{3,0},{4,7},{5,6},{6,5},{7,4},{8,11},{9,10},{10,... | collective-permute-start | bytes 1572872 | tf_op jit(solution)/shard_map/ppermute | solution.py:516
  589.0 27.3 %collective-permute-start.41 = (bf16[128,2048]{1,0:T(8,128)(2,1)}, bf16[128,2048]{1,0:T(8,128)(2,1)}, u32[]{:S(2)}, u32[]{:S(2)}) collective-permute-start(bf16[128,2048]{1,0:T(8,128)(2,1)} %get-tuple-element.133), channel_id=1, source_target_pairs={{0,1},{1,0},{2,3},{3,2},{4,5},{5,4},{6,7},{7,6},{8,9},{9,8},{10,11... | collective-permute-start | bytes 1572872 | tf_op jit(solution)/shard_map/ppermute | solution.py:516
  589.3 27.0 %collective-permute-start.42 = (bf16[128,2048]{1,0:T(8,128)(2,1)}, bf16[128,2048]{1,0:T(8,128)(2,1)}, u32[]{:S(2)}, u32[]{:S(2)}) collective-permute-start(bf16[128,2048]{1,0:T(8,128)(2,1)} %get-tuple-element.135), channel_id=1, source_target_pairs={{0,2},{1,3},{2,0},{3,1},{4,6},{5,7},{6,4},{7,5},{8,10},{9,11},{10,... | collective-permute-start | bytes 1572872 | tf_op jit(solution)/shard_map/ppermute | solution.py:516
  593.7 34.4 %collective-permute-start.43 = (bf16[128,2048]{1,0:T(8,128)(2,1)}, bf16[128,2048]{1,0:T(8,128)(2,1)}, u32[]{:S(2)}, u32[]{:S(2)}) collective-permute-start(bf16[128,2048]{1,0:T(8,128)(2,1)} %get-tuple-element.134), channel_id=1, source_target_pairs={{0,3},{1,2},{2,1},{3,0},{4,7},{5,6},{6,5},{7,4},{8,11},{9,10},{10,... | collective-permute-start | bytes 1572872 | tf_op jit(solution)/shard_map/ppermute | solution.py:516
  610.6 53.9 %all-to-all-start.4 = ((bf16[8,64,2064]{2,1,0:T(8,128)(2,1)}), bf16[8,64,2064]{2,1,0:T(8,128)(2,1)}, u32[]{:S(2)}, u32[]{:S(2)}) async-start(bf16[8,64,2064]{2,1,0:T(8,128)(2,1)} %bitcast.192), calls=%async_computation.7 | async-start | bytes 4456448 | tf_op jit(solution)/shard_map/all_to_all | solution.py:590
  615.2 87.3 %reduce-scatter.8.cloned.1.call-start = ((), (), s32[]{:S(2)}) async-start(), calls=%async_computation.13 | async-start | bytes 2621440 | tf_op jit(solution)/shard_map/reduce_scatter | solution.py:586
  671.6 25.0 %all-to-all-start.3 = ((bf16[8,64,1536]{2,1,0:T(8,128)(2,1)}), bf16[8,64,1536]{2,1,0:T(8,128)(2,1)}, u32[]{:S(2)}, u32[]{:S(2)}) async-start(bf16[8,64,1536]{2,1,0:T(8,128)(2,1)} %bitcast.48), calls=%async_computation.6 | async-start | bytes 3145728 | tf_op jit(solution)/shard_map/all_to_all | solution.py:590
  (108 other events, 1535.0 us)
Sparse Core Ops, SparseCore 0:
  20.9 82.6 all-gather.11
  105.7 90.2 all-gather.5
  199.7 113.3 all-gather.7
  314.5 53.0 all-gather.9
  385.9 144.2 reduce-scatter.3
  532.4 115.0 reduce-scatter.5
  659.3 43.1 reduce-scatter.7
